TPU v7x, 32 devices: a whole 2x2x4 slice. The times are simulated.
32 devices in a mesh: dp: 4 (over z), expert: 8 (over y, x, core).
Axes of the slice: x: 2, y: 2, z: 4, core: 2. Of those that a mesh axis runs over, the one named last changes fastest.
Arguments:
- ids: int32 [8192], P('dp'), may hold values from 0 to 31999
- targets: int32 [8192], P('dp'), may hold values from 0 to 31999
- loss_mask: int32 [8192], replicated, may hold values from 0 to 1
- domain_ids: int32 [4], replicated, may hold values from 0 to 3
- expert_lists: int32 [4, 8, 8, 128], P('dp', 'expert'), may hold values from -1 to 255, as said below
- tables: float32 [2, 32000, 768], P(None, ('expert', 'dp'))
- tables_m: float32 [2, 32000, 768], P(None, ('expert', 'dp'))
- tables_v: float32 [2, 32000, 768], P(None, ('expert', 'dp'))
- attn: float32 [4, 768, 768], P(None, 'dp')
- attn_m: float32 [4, 768, 768], P(None, 'dp')
- attn_v: float32 [4, 768, 768], P(None, 'dp')
- experts: float32 [8, 2, 768, 3072], P('expert', None, None, 'dp')
- experts_m: float32 [8, 2, 768, 3072], P('expert', None, None, 'dp')
- experts_v: float32 [8, 2, 768, 3072], P('expert', None, None, 'dp')
- router: float32 [768, 8], replicated, may hold values from -0.109375 to 0.109375
- router_m: float32 [768, 8], replicated
- router_v: float32 [768, 8], replicated
- gains: float32 [3, 768], replicated
- gains_m: float32 [3, 768], replicated
- gains_v: float32 [3, 768], replicated
Outputs:
- domain_sums: float32 [4], replicated
- domain_counts: float32 [4], replicated
- grad_norm: float32 [], replicated
- tables_first: float32 [2, 32000, 768], P(None, ('expert', 'dp'))
- tables_second: float32 [2, 32000, 768], P(None, ('expert', 'dp'))
- tables_new: float32 [2, 32000, 768], P(None, ('expert', 'dp'))
- tables_copy: bfloat16 [2, 32000, 768], P(None, ('expert', 'dp'))
- attn_first: float32 [4, 768, 768], P(None, 'dp')
- attn_second: float32 [4, 768, 768], P(None, 'dp')
- attn_new: float32 [4, 768, 768], P(None, 'dp')
- attn_copy: bfloat16 [4, 768, 768], P(None, 'dp')
- experts_first: float32 [8, 2, 768, 3072], P('expert', None, None, 'dp')
- experts_second: float32 [8, 2, 768, 3072], P('expert', None, None, 'dp')
- experts_new: float32 [8, 2, 768, 3072], P('expert', None, None, 'dp')
- experts_copy: bfloat16 [8, 2, 768, 3072], P('expert', None, None, 'dp')
- router_first: float32 [768, 8], replicated
- router_second: float32 [768, 8], replicated
- router_new: float32 [768, 8], replicated
- router_copy: bfloat16 [768, 8], replicated
- gains_first: float32 [3, 768], replicated
- gains_second: float32 [3, 768], replicated
- gains_new: float32 [3, 768], replicated
- gains_copy: bfloat16 [3, 768], replicated
Inputs may be any that keep to these rules, and one draw needn't show every extreme that they name: `expert_lists`: in every list of one batch group, source device and expert the filled slots come first and name distinct local token rows; in each batch group one expert has every slot filled from every source device.
All inputs are finite; a program needn't handle non-finite values.
Results may differ from a plain program's by a relative error of at most 0.033.
Values may be sent and summed in bfloat16 or wider, within the bound.
No kernel may reach another device: no remote copies, remote signals or barrier semaphores. Data moves between devices by JAX's collectives and lax.ppermute only.
A program may use at most 320 MiB of HBM per device.

v0:
```python
import jax
import jax.numpy as jnp
from jax import lax
from jax.sharding import PartitionSpec as P

HEADS = 12
SEQ = 2048
NDOM = 4
STEP = 10


NORM_EPS = 1e-05
BETA = 0.5
ADAM_EPS = 1e-08
CLIP = 1.0
MASKED = -1e30


def for_sending(array):
    return jax.tree.map(lambda a: a.astype(jnp.bfloat16) if a.dtype == jnp.float32 else a, array)


def merged(array, axis, join):
    gathered = jax.tree.map(
        lambda a, kind: lax.all_gather(a.astype(kind), axis),
        array,
        (jnp.bfloat16, jnp.bfloat16, jnp.bfloat16),
    )

    def take(source):
        return jax.tree.map(
            lambda a, own: lax.dynamic_index_in_dim(a, source, 0, False).astype(own.dtype),
            gathered,
            array,
        )

    return lax.fori_loop(
        1, lax.axis_size(axis), lambda source, state: join(state, take(source)), take(0)
    )


def normed(values, gain):
    return values * lax.rsqrt(jnp.mean(values * values, axis=-1, keepdims=True) + NORM_EPS) * gain


def norm_back(values, gain, grad):
    _, pull = jax.vjp(normed, values, gain)
    return pull(grad)


def gelu(values):
    return jax.nn.gelu(values, approximate=True)


def adam(weight, grad, first, second, rate, decay):
    first = BETA * first + (1.0 - BETA) * grad
    second = BETA * second + (1.0 - BETA) * grad * grad
    correct = 1.0 - BETA**STEP
    weight = weight - rate * (
        first / correct / (jnp.sqrt(second / correct) + ADAM_EPS) + decay * weight
    )
    return (first, second, weight, weight.astype(jnp.bfloat16))


def group_rows(values):
    return jax.tree.map(
        lambda part, own: part.astype(own.dtype),
        lax.all_gather(for_sending(values), "expert", axis=0, tiled=True),
        values,
    )


def group_sums(values):
    return jax.tree.map(
        lambda part: part.astype(jnp.float32),
        lax.psum_scatter(for_sending(values), "expert", scatter_dimension=0, tiled=True),
    )


def expert_rows(values):
    return lax.all_to_all(values, "expert", split_axis=0, concat_axis=0, tiled=True)


def merge_stats(first, second):
    top = jnp.maximum(first[0], second[0])
    total = first[1] * jnp.exp(first[0] - top) + second[1] * jnp.exp(second[0] - top)
    return (top, total, first[2] + second[2])


def masked_scores(queries, keys, query_place, key_place):
    scale = queries.shape[-1] ** (-0.5)
    scores = jnp.einsum("qhd,khd->hqk", queries, keys, preferred_element_type=jnp.float32) * scale
    allowed = key_place[None, :] <= query_place[:, None]
    return jnp.where(allowed[None], scores, MASKED)


def attend_block(queries, query_place, keys, values, key_place):
    scores = masked_scores(queries, keys, query_place, key_place)
    top = jnp.max(scores, axis=-1, keepdims=True)
    weights = jnp.exp(scores - top)
    total = jnp.sum(weights, axis=-1, keepdims=True)
    mixed = jnp.einsum(
        "hqk,khd->qhd",
        (weights / total).astype(jnp.bfloat16),
        values,
        preferred_element_type=jnp.float32,
    )
    return (mixed, (top + jnp.log(total))[..., 0])


def score_grads(queries, query_place, grad_out, logsum, keys, values, key_place, delta):
    scores = masked_scores(queries, keys, query_place, key_place)
    weights = jnp.exp(scores - logsum[..., None])
    grad_weights = jnp.einsum("qhd,khd->hqk", grad_out, values, preferred_element_type=jnp.float32)
    delta = jnp.sum(weights * grad_weights, axis=-1)
    grad_scores = (weights * (grad_weights - delta[..., None])).astype(jnp.bfloat16)
    return (weights, grad_scores, delta)


def body(
    ids,
    targets,
    loss_mask,
    domain_ids,
    expert_lists,
    tables,
    tables_m,
    tables_v,
    attn,
    attn_m,
    attn_v,
    experts,
    experts_m,
    experts_v,
    router,
    router_m,
    router_v,
    gains,
    gains_m,
    gains_v,
):
    shards = lax.axis_size("expert")
    member = lax.axis_index("expert")
    batch_row = lax.axis_index("dp")
    group = ids.shape[0]
    local = group // shards
    own = member * local
    width = gains.shape[1]
    head_dim = width // HEADS
    scale = head_dim ** (-0.5)
    experts_all = router.shape[1]
    slots = expert_lists.shape[3]
    tables_b, attn_b, experts_b = (
        lax.all_gather(tables.astype(jnp.bfloat16), "dp", axis=1, tiled=True),
        lax.all_gather(attn.astype(jnp.bfloat16), "dp", axis=1, tiled=True),
        lax.all_gather(experts.astype(jnp.bfloat16), "dp", axis=3, tiled=True),
    )
    router_b = router.astype(jnp.bfloat16)
    vocab_part = tables_b.shape[1]
    first_word = member * vocab_part
    word_local = ids - first_word
    word_hit = (word_local >= 0) & (word_local < vocab_part)
    word_clip = jnp.clip(word_local, 0, vocab_part - 1)
    looked = jnp.where(
        word_hit[:, None], jnp.take(tables_b[0], word_clip, axis=0).astype(jnp.float32), 0.0
    )
    embedded = group_sums(looked)
    normed_ab = normed(embedded, gains[0]).astype(jnp.bfloat16)
    projected = jnp.einsum(
        "td,kde->kte", normed_ab, attn_b[:3], preferred_element_type=jnp.float32
    ).astype(jnp.bfloat16)
    queries, keys, values = (projected[0], projected[1], projected[2])
    keys_all, values_all = group_rows((keys, values))
    seq_start = own // SEQ * SEQ
    keys_seq = lax.dynamic_slice_in_dim(keys_all, seq_start, SEQ, 0).reshape(SEQ, HEADS, head_dim)
    values_seq = lax.dynamic_slice_in_dim(values_all, seq_start, SEQ, 0).reshape(
        SEQ, HEADS, head_dim
    )
    key_place = jnp.arange(SEQ)
    query_place = own - seq_start + jnp.arange(local)
    block = min(512, local)
    blocks = local // block
    query_blocks = queries.reshape(blocks, block, HEADS, head_dim)
    place_blocks = query_place.reshape(blocks, block)
    mixed, logsum = lax.map(
        lambda item: attend_block(item[0], item[1], keys_seq, values_seq, key_place),
        (query_blocks, place_blocks),
    )
    mixed_b = mixed.reshape(local, width).astype(jnp.bfloat16)
    resid_one = embedded + jnp.dot(mixed_b, attn_b[3], preferred_element_type=jnp.float32)
    normed_bb = normed(resid_one, gains[1]).astype(jnp.bfloat16)
    router_logits = jnp.dot(normed_bb, router_b, preferred_element_type=jnp.float32)
    gates = jax.nn.softmax(router_logits, axis=-1)
    lists = expert_lists[0, 0]
    filled = lists >= 0
    slot_rows = jnp.where(filled, lists, 0).reshape(-1)
    slot_live = filled.reshape(-1, 1)
    slot_expert = jnp.repeat(jnp.arange(experts_all), slots)
    send = jnp.where(slot_live, jnp.take(normed_bb, slot_rows, axis=0), jnp.zeros((), jnp.bfloat16))
    slot_gates = jnp.where(slot_live[:, 0], gates[slot_rows, slot_expert], 0.0)
    received = expert_rows(send.reshape(experts_all, slots, width)).reshape(-1, width)
    w_up = experts_b[0, 0]
    w_down = experts_b[0, 1]
    pre = jnp.dot(received, w_up, preferred_element_type=jnp.float32)
    hidden = gelu(pre).astype(jnp.bfloat16)
    produced = lax.dot_general(
        hidden, w_down, (((1,), (1,)), ((), ())), preferred_element_type=jnp.float32
    )
    returned = (
        expert_rows(produced.astype(jnp.bfloat16).reshape(experts_all, slots, width))
        .reshape(-1, width)
        .astype(jnp.float32)
    )
    mixture = (
        jnp.zeros((local, width), jnp.float32).at[slot_rows].add(slot_gates[:, None] * returned)
    )
    resid_two = resid_one + mixture
    normed_cb = normed(resid_two, gains[2]).astype(jnp.bfloat16)
    rows_all = group_rows(normed_cb)
    head = tables_b[1]
    target_local = targets - first_word
    target_hit = (target_local >= 0) & (target_local < vocab_part)
    target_clip = jnp.clip(target_local, 0, vocab_part - 1)
    head_block = min(512, group)
    head_count = group // head_block
    row_blocks = rows_all.reshape(head_count, head_block, width)
    target_blocks = target_clip.reshape(head_count, head_block)
    hit_blocks = target_hit.reshape(head_count, head_block)

    def head_logits(rows_blk):
        return lax.dot_general(
            rows_blk, head, (((1,), (1,)), ((), ())), preferred_element_type=jnp.float32
        )

    def head_stats(item):
        rows_blk, target_blk, hit_blk = item
        logits = head_logits(rows_blk)
        top = jnp.max(logits, axis=-1)
        total = jnp.sum(jnp.exp(logits - top[:, None]), axis=-1)
        picked = jnp.where(
            hit_blk, jnp.take_along_axis(logits, target_blk[:, None], axis=1)[:, 0], 0.0
        )
        return (top, total, picked)

    tops, totals, picks = lax.map(head_stats, (row_blocks, target_blocks, hit_blocks))
    top, total, picked = merged(
        (tops.reshape(-1), totals.reshape(-1), picks.reshape(-1)), "expert", merge_stats
    )
    logsum_tok = top + jnp.log(total)
    loss_tok = logsum_tok - picked
    everything = loss_mask.shape[0]
    domain_of = jnp.take(domain_ids, jnp.arange(everything) // SEQ)
    hits = ((domain_of[:, None] == jnp.arange(NDOM)[None, :]) & (loss_mask[:, None] > 0)).astype(
        jnp.float32
    )
    counts = jnp.sum(hits, axis=0)
    domain_weight = 10.0 * (NDOM - jnp.arange(NDOM)).astype(jnp.float32) / jnp.maximum(counts, 1.0)
    group_hits = lax.dynamic_slice_in_dim(hits, batch_row * group, group, 0)
    token_weight = jnp.sum(group_hits * domain_weight[None, :], axis=1)
    own_hits = lax.dynamic_slice_in_dim(group_hits, own, local, 0)
    own_sums = jnp.sum(
        own_hits * lax.dynamic_slice_in_dim(loss_tok, own, local, 0)[:, None], axis=0
    )

    def head_back(grad_head, item):
        rows_blk, target_blk, hit_blk, logsum_blk, weight_blk = item
        logits = head_logits(rows_blk)
        onehot = (
            (jnp.arange(vocab_part)[None, :] == target_blk[:, None]) & hit_blk[:, None]
        ).astype(jnp.float32)
        grad_logits = (
            weight_blk[:, None] * (jnp.exp(logits - logsum_blk[:, None]) - onehot)
        ).astype(jnp.bfloat16)
        grad_rows_blk = jnp.dot(grad_logits, head, preferred_element_type=jnp.float32)
        grad_head = grad_head + lax.dot_general(
            grad_logits, rows_blk, (((0,), (0,)), ((), ())), preferred_element_type=jnp.float32
        )
        return (grad_head, grad_rows_blk)

    grad_head, grad_rows_c = lax.scan(
        head_back,
        jnp.zeros((vocab_part, width), jnp.float32),
        (
            row_blocks,
            target_blocks,
            hit_blocks,
            logsum_tok.reshape(head_count, head_block),
            token_weight.reshape(head_count, head_block),
        ),
    )
    grad_normed_c = group_sums(grad_rows_c.reshape(group, width))
    grad_two, grad_gain_c = norm_back(resid_two, gains[2], grad_normed_c)
    grad_slot = jnp.take(grad_two, slot_rows, axis=0)
    grad_gate_slot = jnp.where(slot_live[:, 0], jnp.sum(grad_slot * returned, axis=-1), 0.0)
    grad_produced = expert_rows(
        (grad_slot * slot_gates[:, None]).astype(jnp.bfloat16).reshape(experts_all, slots, width)
    ).reshape(-1, width)
    grad_hidden = jnp.dot(grad_produced, w_down, preferred_element_type=jnp.float32)
    _, gelu_pull = jax.vjp(gelu, pre)
    grad_pre = gelu_pull(grad_hidden)[0].astype(jnp.bfloat16)
    grad_down = lax.dot_general(
        grad_produced, hidden, (((0,), (0,)), ((), ())), preferred_element_type=jnp.float32
    )
    grad_up = lax.dot_general(
        received, grad_pre, (((0,), (0,)), ((), ())), preferred_element_type=jnp.float32
    )
    grad_sent = lax.dot_general(
        grad_pre, w_up, (((1,), (1,)), ((), ())), preferred_element_type=jnp.float32
    ).astype(jnp.bfloat16)
    grad_back = expert_rows(grad_sent.reshape(experts_all, slots, width)).reshape(-1, width)
    grad_normed_b = (
        jnp.zeros((local, width), jnp.float32)
        .at[slot_rows]
        .add(jnp.where(slot_live, grad_back.astype(jnp.float32), 0.0))
    )
    grad_gate_table = (
        jnp.zeros((local, experts_all), jnp.float32).at[slot_rows, slot_expert].add(grad_gate_slot)
    )
    _, soft_pull = jax.vjp(lambda logit_rows: jax.nn.softmax(logit_rows, axis=-1), router_logits)
    grad_router_logits = soft_pull(grad_gate_table)[0].astype(jnp.bfloat16)
    grad_router = lax.dot_general(
        normed_bb, grad_router_logits, (((0,), (0,)), ((), ())), preferred_element_type=jnp.float32
    )
    grad_normed_b = grad_normed_b + lax.dot_general(
        grad_router_logits, router_b, (((1,), (1,)), ((), ())), preferred_element_type=jnp.float32
    )
    normal_back, grad_gain_b = norm_back(resid_one, gains[1], grad_normed_b)
    grad_one = grad_two + normal_back
    grad_branch = grad_one.astype(jnp.bfloat16)
    grad_wo = lax.dot_general(
        mixed_b, grad_branch, (((0,), (0,)), ((), ())), preferred_element_type=jnp.float32
    )
    grad_mixed = lax.dot_general(
        grad_branch, attn_b[3], (((1,), (1,)), ((), ())), preferred_element_type=jnp.float32
    ).astype(jnp.bfloat16)
    grad_blocks = grad_mixed.reshape(blocks, block, HEADS, head_dim)

    def query_pass(carry, item):
        query_blk, place_blk, grad_blk, logsum_blk = item
        weights, grad_scores, _ = score_grads(
            query_blk, place_blk, grad_blk, logsum_blk, keys_seq, values_seq, key_place, None
        )
        grad_query = (
            jnp.einsum("hqk,khd->qhd", grad_scores, keys_seq, preferred_element_type=jnp.float32)
            * scale
        )
        grad_key = (
            carry[0]
            + jnp.einsum("hqk,qhd->khd", grad_scores, query_blk, preferred_element_type=jnp.float32)
            * scale
        )
        grad_value = carry[1] + jnp.einsum(
            "hqk,qhd->khd",
            weights.astype(jnp.bfloat16),
            grad_blk,
            preferred_element_type=jnp.float32,
        )
        return ((grad_key, grad_value), grad_query)

    zeros_seq = jnp.zeros((SEQ, HEADS, head_dim), jnp.float32)
    (grad_key_seq, grad_value_seq), grad_query = lax.scan(
        query_pass, (zeros_seq, zeros_seq), (query_blocks, place_blocks, grad_blocks, logsum)
    )
    empty = jnp.zeros((group, width), jnp.float32)
    grad_keys, grad_values = group_sums(
        (
            lax.dynamic_update_slice_in_dim(empty, grad_key_seq.reshape(SEQ, width), seq_start, 0),
            lax.dynamic_update_slice_in_dim(
                empty, grad_value_seq.reshape(SEQ, width), seq_start, 0
            ),
        )
    )
    grads_b = jnp.stack([grad_query.reshape(local, width), grad_keys, grad_values]).astype(
        jnp.bfloat16
    )
    grad_qkv = jnp.einsum("td,kte->kde", normed_ab, grads_b, preferred_element_type=jnp.float32)
    grad_normed_a = jnp.einsum(
        "kte,kde->td", grads_b, attn_b[:3], preferred_element_type=jnp.float32
    )
    normal_front, grad_gain_a = norm_back(embedded, gains[0], grad_normed_a)
    grad_embedded = (grad_one + normal_front).astype(jnp.bfloat16)
    grad_rows = group_rows(grad_embedded)
    grad_embed = (
        jnp.zeros((vocab_part, width), jnp.float32)
        .at[word_clip]
        .add(jnp.where(word_hit[:, None], grad_rows.astype(jnp.float32), 0.0))
    )
    grad_tables, grad_attn, grad_experts = (
        lax.psum_scatter(
            jnp.stack([grad_embed, grad_head]).astype(jnp.bfloat16),
            "dp",
            scatter_dimension=1,
            tiled=True,
        ).astype(jnp.float32),
        lax.psum_scatter(
            jnp.concatenate([grad_qkv, grad_wo[None]]).astype(jnp.bfloat16),
            "dp",
            scatter_dimension=1,
            tiled=True,
        ).astype(jnp.float32),
        lax.psum_scatter(
            jnp.stack([grad_up, grad_down])[None].astype(jnp.bfloat16),
            "dp",
            scatter_dimension=3,
            tiled=True,
        ).astype(jnp.float32),
    )
    grad_attn = lax.psum(grad_attn.astype(jnp.bfloat16), "expert").astype(jnp.float32)
    squares = (
        jnp.sum(grad_tables * grad_tables)
        + jnp.sum(grad_experts * grad_experts)
        + jnp.sum(grad_attn * grad_attn) / shards
    )
    grad_gains = jnp.stack([grad_gain_a, grad_gain_b, grad_gain_c])
    grad_router, grad_gains, domain_sums, squares = lax.psum(
        (grad_router, grad_gains, own_sums, squares), ("dp", "expert")
    )
    grad_norm = jnp.sqrt(
        squares + jnp.sum(grad_router * grad_router) + jnp.sum(grad_gains * grad_gains)
    )
    factor = jnp.minimum(1.0, CLIP / (grad_norm + 1e-06))
    tables_out = adam(tables, grad_tables * factor, tables_m, tables_v, 0.1, 0.01)
    attn_out = adam(attn, grad_attn * factor, attn_m, attn_v, 0.1, 0.01)
    experts_out = adam(experts, grad_experts * factor, experts_m, experts_v, 0.1, 0.01)
    router_out = adam(router, grad_router * factor, router_m, router_v, 0.04, 0.01)
    gains_out = adam(gains, grad_gains * factor, gains_m, gains_v, 0.4, 0.0)
    return (
        domain_sums,
        counts,
        grad_norm,
        tables_out[0],
        tables_out[1],
        tables_out[2],
        tables_out[3],
        attn_out[0],
        attn_out[1],
        attn_out[2],
        attn_out[3],
        experts_out[0],
        experts_out[1],
        experts_out[2],
        experts_out[3],
        router_out[0],
        router_out[1],
        router_out[2],
        router_out[3],
        gains_out[0],
        gains_out[1],
        gains_out[2],
        gains_out[3],
    )


def solution(mesh):
    in_specs = (
        P("dp"),
        P("dp"),
        P(),
        P(),
        P("dp", "expert", None, None),
        P(None, ("expert", "dp"), None),
        P(None, ("expert", "dp"), None),
        P(None, ("expert", "dp"), None),
        P(None, "dp", None),
        P(None, "dp", None),
        P(None, "dp", None),
        P("expert", None, None, "dp"),
        P("expert", None, None, "dp"),
        P("expert", None, None, "dp"),
        P(),
        P(),
        P(),
        P(),
        P(),
        P(),
    )
    out_specs = (
        P(),
        P(),
        P(),
        P(None, ("expert", "dp"), None),
        P(None, ("expert", "dp"), None),
        P(None, ("expert", "dp"), None),
        P(None, ("expert", "dp"), None),
        P(None, "dp", None),
        P(None, "dp", None),
        P(None, "dp", None),
        P(None, "dp", None),
        P("expert", None, None, "dp"),
        P("expert", None, None, "dp"),
        P("expert", None, None, "dp"),
        P("expert", None, None, "dp"),
        P(),
        P(),
        P(),
        P(),
        P(),
        P(),
        P(),
        P(),
    )
    return jax.shard_map(body, mesh=mesh, in_specs=in_specs, out_specs=out_specs, check_vma=False)
```

profile of v0, /device:TPU:0, one launch (start us, length us, event | category | flops | bytes accessed | tf_op | source)
XLA Modules:
  0.0 1986.7 jit_solution(17726301279623343389)
XLA Ops:
  12.6 215.6 %all-gather.13.cloned.1.call-done = bf16[2,4000,768]{2,1,0:T(8,128)(2,1)} async-done(((bf16[2,1000,768]{2,1,0:T(8,128)(2,1)}), bf16[2,4000,768]{2,1,0:T(8,128)(2,1)}) %all-gather.13.cloned.1.call-update) | async-done | bytes 12288016 | tf_op jit(solution)/shard_map/all_gather | solution.py:154
  228.2 10.0 slice_bitcast_fusion
  238.2 12.0 gather_fusion.1
  255.3 41.6 %reduce-scatter.9.cloned.1.call-done = bf16[256,768]{1,0:T(8,128)(2,1)} async-done(((bf16[2048,768]{1,0:T(8,128)(2,1)}), bf16[256,768]{1,0:T(8,128)(2,1)}) %reduce-scatter.9.cloned.1.call-update) | async-done | bytes 393232 | tf_op jit(solution)/shard_map/reduce_scatter | solution.py:76
  298.2 90.5 %all-gather.15.cloned.1.call-done = bf16[4,768,768]{2,1,0:T(8,128)(2,1)} async-done(((bf16[4,192,768]{2,1,0:T(8,128)(2,1)}), bf16[4,768,768]{2,1,0:T(8,128)(2,1)}) %all-gather.15.cloned.1.call-update) | async-done | bytes 4718608 | tf_op jit(solution)/shard_map/all_gather | solution.py:155
  400.7 23.2 %all-gather.25.cloned.1.call-done = bf16[1,2048,768]{2,1,0:T(8,128)(2,1)} async-done(((bf16[1,256,768]{2,1,0:T(8,128)(2,1)}), bf16[1,2048,768]{2,1,0:T(8,128)(2,1)}) %all-gather.25.cloned.1.call-update) | async-done | bytes 3145744 | tf_op jit(solution)/shard_map/all_gather | solution.py:68
  427.0 31.6 %all-gather.23.cloned.1.call-done = bf16[1,2048,768]{2,1,0:T(8,128)(2,1)} async-done(((bf16[1,256,768]{2,1,0:T(8,128)(2,1)}), bf16[1,2048,768]{2,1,0:T(8,128)(2,1)}) %all-gather.23.cloned.1.call-update) | async-done | bytes 3145744 | tf_op jit(solution)/shard_map/all_gather | solution.py:68
  463.3 13.5 fusion.27
  476.8 11.7 fusion.14
  488.6 12.0 fusion.69
  520.4 107.2 %all-gather.17.cloned.1.call-done = bf16[1,2,768,3072]{3,2,1,0:T(8,128)(2,1)} async-done(((bf16[1,2,768,768]{3,2,1,0:T(8,128)(2,1)}), bf16[1,2,768,3072]{3,2,1,0:T(8,128)(2,1)}) %all-gather.17.cloned.1.call-update) | async-done | bytes 9437200 | tf_op jit(solution)/shard_map/all_gather | solution.py:156
  627.5 10.8 fusion.39
  638.4 11.4 fusion.54
  654.1 20.3 %all-to-all-done.1 = bf16[8,128,768]{2,1,0:T(8,128)(2,1)S(1)} async-done(((bf16[8,128,768]{2,1,0:T(8,128)(2,1)}), bf16[8,128,768]{2,1,0:T(8,128)(2,1)S(1)}, u32[]{:S(2)}, u32[]{:S(2)}) %all-to-all-start.1) | async-done | bytes 1572896 | tf_op jit(solution)/shard_map/all_to_all | solution.py:81
  690.8 24.2 %all-gather.19.cloned.1.call-done = bf16[2048,768]{1,0:T(8,128)(2,1)} async-done(((bf16[256,768]{1,0:T(8,128)(2,1)}), bf16[2048,768]{1,0:T(8,128)(2,1)}) %all-gather.19.cloned.1.call-update) | async-done | bytes 3145744 | tf_op jit(solution)/shard_map/all_gather | solution.py:68
  715.0 140.7 %while.16 = (s32[]{:T(128)}, bf16[4,512]{1,0:T(4,128)(2,1)S(1)}, bf16[4,512]{1,0:T(4,128)(2,1)S(1)}, bf16[4,512]{1,0:T(4,128)(2,1)S(1)}, bf16[4,512,768]{2,1,0:T...) while((s32[]{:T(128)}, bf16[4,512]{1,0:T(4,128)(2,1)S(1)}, ...), condition=%wide.region_12.13_spmd, body=%wide.region_9.12_spmd.sunk | while | flops 3151880192 | bytes 23365252 | solution.py:245
  715.1 9.7 fusion.171
  724.8 20.7 %gather_fusion = f32[512]{0:T(512)S(1)} fusion(f32[512,4000]{0,1:T(8,128)} %get-tuple-element.762, s32[512]{0:T(512)S(1)} %bitcast.219), kind=kCustom, calls=%fused_computation.clone.1 | custom fusion | bytes 8192 | tf_op jit(solution)/shard_map/while/body/eval_jaxpr/jit(take_along_axis)/gather | solution.py:241
  750.2 9.7 fusion.171
  759.8 20.7 %gather_fusion = f32[512]{0:T(512)S(1)} fusion(f32[512,4000]{0,1:T(8,128)} %get-tuple-element.762, s32[512]{0:T(512)S(1)} %bitcast.219), kind=kCustom, calls=%fused_computation.clone.1 | custom fusion | bytes 8192 | tf_op jit(solution)/shard_map/while/body/eval_jaxpr/jit(take_along_axis)/gather | solution.py:241
  785.2 9.7 fusion.171
  794.9 21.0 %gather_fusion = f32[512]{0:T(512)S(1)} fusion(f32[512,4000]{0,1:T(8,128)} %get-tuple-element.762, s32[512]{0:T(512)S(1)} %bitcast.219), kind=kCustom, calls=%fused_computation.clone.1 | custom fusion | bytes 8192 | tf_op jit(solution)/shard_map/while/body/eval_jaxpr/jit(take_along_axis)/gather | solution.py:241
  820.6 9.7 fusion.171
  830.2 20.9 %gather_fusion = f32[512]{0:T(512)S(1)} fusion(f32[512,4000]{0,1:T(8,128)} %get-tuple-element.762, s32[512]{0:T(512)S(1)} %bitcast.219), kind=kCustom, calls=%fused_computation.clone.1 | custom fusion | bytes 8192 | tf_op jit(solution)/shard_map/while/body/eval_jaxpr/jit(take_along_axis)/gather | solution.py:241
  863.6 9.7 all-gather.2
  882.8 94.5 %while.59 = (s32[]{:T(128)}, f32[4000,768]{1,0:T(8,128)}, bf16[4,512,768]{2,1,0:T(8,128)(2,1)}, f32[4,512]{1,0:T(4,128)S(1)}, bf16[4,512,768]{2,1,0:T(8,128)(2,1...) while((s32[]{:T(128)}, f32[4000,768]{1,0:T(8,128)}, ...), condition=%wide.region_20.21_spmd.clone, body=%wide.region_19.20_spmd.clone.sunk | while | flops 9457664000 | bytes 188075888 | solution.py:280
  977.4 46.0 %reduce-scatter.11.cloned.1.call-done = bf16[256,768]{1,0:T(8,128)(2,1)} async-done(((bf16[2048,768]{1,0:T(8,128)(2,1)}), bf16[256,768]{1,0:T(8,128)(2,1)}) %reduce-scatter.11.cloned.1.call-update) | async-done | bytes 393232 | tf_op jit(solution)/shard_map/reduce_scatter | solution.py:76
  1040.2 20.7 %all-to-all-done.2 = bf16[8,128,768]{2,1,0:T(8,128)(2,1)S(1)} async-done(((bf16[8,128,768]{2,1,0:T(8,128)(2,1)}), bf16[8,128,768]{2,1,0:T(8,128)(2,1)S(1)}, u32[]{:S(2)}, u32[]{:S(2)}) %all-to-all-start.2) | async-done | bytes 1572896 | tf_op jit(solution)/shard_map/all_to_all | solution.py:81
  1061.0 15.3 fusion.22
  1076.4 10.9 fusion.55
  1100.0 12.9 all-to-all-done.3
  1112.8 8.9 scatter_custom_fusion.1
  1125.1 12.6 fusion.42
  1142.4 19.6 multiply_reduce_fusion
  1162.0 17.6 multiply_convert_fusion.1
  1190.6 9.3 fusion.68
  1203.1 35.3 %reduce-scatter.13.cloned.1.call-done = bf16[256,768]{1,0:T(8,128)(2,1)} async-done(((bf16[2048,768]{1,0:T(8,128)(2,1)}), bf16[256,768]{1,0:T(8,128)(2,1)}) %reduce-scatter.13.cloned.1.call-update) | async-done | bytes 393232 | tf_op jit(solution)/shard_map/reduce_scatter | solution.py:76
  1259.3 9.5 fusion.36
  1268.9 155.1 %all-reduce.7.cloned.1.call-done = bf16[4,768,768]{2,0,1:T(4,128)(2,1)} async-done(((bf16[4,768,768]{2,0,1:T(4,128)(2,1)}), bf16[4,768,768]{2,0,1:T(4,128)(2,1)}) %all-reduce.7.cloned.1.call-update) | async-done | bytes 4718608
  1427.1 9.9 fusion.37
  1457.7 21.0 %scatter_custom_fusion.2 = f32[4000,768]{1,0:T(8,128)} fusion(s32[2048]{0:T(1024)} %copy-done.63, bf16[2048,768]{1,0:T(8,128)(2,1)} %all-gather.21.cloned.1.call-done, f32[]{:T(128)} %constant.319.clone.1, pred[2048]{0:T(1024)(128)(4,1)S(1)} %copy-done.69), kind=kCustom, calls=%fused_computation.73 | custom fusion | flops 4718592 | bytes 15436800 | tf_op jit(solution)/shard_map/scatter-add | solution.py:386
  1491.4 38.0 %copy.148 = bf16[2,4000,768]{2,0,1:T(2,128)(2,1)S(1)} copy(bf16[2,4000,768]{2,1,0:T(8,128)(2,1)S(1)} %pad_maximum_fusion) | data formatting | bytes 24576000
  1529.4 9.3 copy.153
  1543.8 137.5 %reduce-scatter.17.cloned.1.call-done = bf16[1,2,768,768]{3,2,1,0:T(8,128)(2,1)} async-done(((bf16[1,2,768,3072]{3,2,1,0:T(8,128)(2,1)}), bf16[1,2,768,768]{3,2,1,0:T(8,128)(2,1)}) %reduce-scatter.17.cloned.1.call-update) | async-done | bytes 2359312 | tf_op jit(solution)/shard_map/reduce_scatter | solution.py:401
  1684.9 207.2 %reduce-scatter.19.cloned.1.call-done = bf16[1000,1536]{1,0:T(8,128)(2,1)} async-done(((bf16[4000,1536]{1,0:T(8,128)(2,1)}), bf16[1000,1536]{1,0:T(8,128)(2,1)}) %reduce-scatter.19.cloned.1.call-update) | async-done | bytes 3072016
  1901.7 42.2 %all-reduce.1 = (f32[4]{0:T(128)}, f32[]{:T(128)}, f32[768,8]{0,1:T(8,128)S(1)}, f32[3,768]{1,0:T(4,128)S(1)}) all-reduce(f32[4]{0:T(128)S(1)} %multiply_reduce_fusion.10, f32[]{:T(128)S(6)} %add.423, f32[768,8]{0,1:T(8,128)S(1)} %fusion.133, f32[3,768]{1,0:T(4,128)S(1)} %pad_maximum_fusion.6), channel_id=1, replica_groups=mesh['dp'=4,'expert'=8] {'dp','expert'}, use_global_device_ids=true, to_apply=%region_16.17 | all-reduce | flops 8453 | bytes 67624 | tf_op jit(solution)/shard_map/psum | solution.py:415
  1948.5 15.0 fusion.127
  1968.3 10.4 fusion.123
  (512 shorter events, 332.5 us)
Async XLA Ops:
  7.2 221.0 %all-gather.13.cloned.1.call-start = ((), (), s32[]{:S(2)}) async-start(), calls=%async_computation.10 | async-start | bytes 15360000 | tf_op jit(solution)/shard_map/all_gather | solution.py:154
  12.0 285.0 %reduce-scatter.9.cloned.1.call-start = ((), (), s32[]{:S(2)}) async-start(), calls=%async_computation.11 | async-start | bytes 3538944 | tf_op jit(solution)/shard_map/reduce_scatter | solution.py:76
  12.1 238.2 %copy-start.68 = (pred[2048]{0:T(1024)(128)(4,1)}, pred[2048]{0:T(1024)(128)(4,1)S(1)}, u32[]{:S(2)}) copy-start(pred[2048]{0:T(1024)(128)(4,1)S(1)} %get-tuple-element.605) | copy-start | bytes 6148
  252.4 136.2 %all-gather.15.cloned.1.call-start = ((), (), s32[]{:S(2)}) async-start(), calls=%async_computation.12 | async-start | bytes 5898240 | tf_op jit(solution)/shard_map/all_gather | solution.py:155
  255.2 168.6 %all-gather.25.cloned.1.call-start = ((), (), s32[]{:S(2)}) async-start(), calls=%async_computation.22 | async-start | bytes 3538944 | tf_op jit(solution)/shard_map/all_gather | solution.py:68
  255.3 137.6 %copy-start.72 = (f32[768]{0:T(1024)}, f32[768]{0:T(1024)S(1)}, u32[]{:S(2)}) copy-start(f32[768]{0:T(1024)S(1)} %get-tuple-element.511) | copy-start | bytes 9220
  255.3 247.3 %copy-start.47 = (f32[768]{0:T(1024)}, f32[768]{0:T(1024)S(1)}, u32[]{:S(2)}) copy-start(f32[768]{0:T(1024)S(1)} %get-tuple-element.510) | copy-start | bytes 9220
  255.3 429.9 %copy-start.49 = (f32[768]{0:T(1024)}, f32[768]{0:T(1024)S(1)}, u32[]{:S(2)}) copy-start(f32[768]{0:T(1024)S(1)} %get-tuple-element.509) | copy-start | bytes 9220
  298.1 94.7 %copy-start.84 = (f32[256]{0:T(256)}, f32[256]{0:T(256)S(1)}, u32[]{:S(2)}) copy-start(f32[256]{0:T(256)S(1)} %fusion.81) | copy-start | bytes 3076
  298.2 94.7 %copy-start.91 = (f32[256]{0:T(256)}, f32[256]{0:T(256)S(1)}, u32[]{:S(2)}) copy-start(f32[256]{0:T(256)S(1)} %fusion.109) | copy-start | bytes 3076
  392.9 65.7 %all-gather.23.cloned.1.call-start = ((), (), s32[]{:S(2)}) async-start(), calls=%async_computation.21 | async-start | bytes 3538944 | tf_op jit(solution)/shard_map/all_gather | solution.py:68
  393.5 234.0 %all-gather.17.cloned.1.call-start = ((), (), s32[]{:S(2)}) async-start(), calls=%async_computation.13 | async-start | bytes 11796480 | tf_op jit(solution)/shard_map/all_gather | solution.py:156
  398.7 277.9 %copy-start.45 = (s32[1024,1]{0,1:T(1,128)}, s32[1024,1]{0,1:T(1,128)S(1)}, u32[]{:S(2)}) copy-start(s32[1024,1]{0,1:T(1,128)S(1)} %get-tuple-element.591) | copy-start | bytes 12292
  400.7 62.6 %copy-start.20 = (bf16[1,256,768]{1,2,0:T(8,128)(2,1)}, bf16[1,256,768]{1,2,0:T(8,128)(2,1)S(1)}, u32[]{:S(2)}) copy-start(bf16[1,256,768]{1,2,0:T(8,128)(2,1)S(1)} %copy.136) | copy-start | bytes 1179652
  427.0 49.7 %copy-start.6 = (bf16[1,2048,768]{1,2,0:T(8,128)(2,1)}, bf16[1,2048,768]{1,2,0:T(8,128)(2,1)S(1)}, u32[]{:S(2)}) copy-start(bf16[1,2048,768]{1,2,0:T(8,128)(2,1)S(1)} %copy.137) | copy-start | bytes 9437188
  502.6 150.9 %copy-start.13 = (f32[256,768]{1,0:T(8,128)}, f32[256,768]{1,0:T(8,128)S(1)}, u32[]{:S(2)}) copy-start(f32[256,768]{1,0:T(8,128)S(1)} %get-tuple-element.616) | copy-start | bytes 2359300
  515.2 123.2 %copy-start.82 = (pred[8,128]{1,0:T(8,128)(4,1)}, pred[8,128]{1,0:T(8,128)(4,1)S(1)}, u32[]{:S(2)}) copy-start(pred[8,128]{1,0:T(8,128)(4,1)S(1)} %compare_and_fusion.3) | copy-start | bytes 3076
  516.6 110.9 %all-to-all-start = ((bf16[8,128,768]{2,1,0:T(8,128)(2,1)}), bf16[8,128,768]{2,1,0:T(8,128)(2,1)S(1)}, u32[]{:S(2)}, u32[]{:S(2)}) async-start(bf16[8,128,768]{2,1,0:T(8,128)(2,1)} %select_select_fusion), calls=%async_computation.1 | async-start | bytes 3145728 | tf_op jit(solution)/shard_map/all_to_all | solution.py:81
  649.8 24.7 %all-to-all-start.1 = ((bf16[8,128,768]{2,1,0:T(8,128)(2,1)}), bf16[8,128,768]{2,1,0:T(8,128)(2,1)S(1)}, u32[]{:S(2)}, u32[]{:S(2)}) async-start(bf16[8,128,768]{2,1,0:T(8,128)(2,1)} %bitcast.248), calls=%async_computation.2 | async-start | bytes 3145728 | tf_op jit(solution)/shard_map/all_to_all | solution.py:81
  653.4 61.6 %all-gather.19.cloned.1.call-start = ((), (), s32[]{:S(2)}) async-start(), calls=%async_computation.14 | async-start | bytes 3538944 | tf_op jit(solution)/shard_map/all_gather | solution.py:68
  686.2 337.2 %reduce-scatter.11.cloned.1.call-start = ((), (), s32[]{:S(2)}) async-start(), calls=%async_computation.15 | async-start | bytes 3538944 | tf_op jit(solution)/shard_map/reduce_scatter | solution.py:76
  882.8 140.6 %copy-start.1 = (f32[256,768]{1,0:T(8,128)S(1)}, f32[256,768]{1,0:T(8,128)}, u32[]{:S(2)}) copy-start(f32[256,768]{1,0:T(8,128)} %copy-done) | copy-start | bytes 2359300
  882.8 140.6 %copy-start.50 = (f32[768]{0:T(1024)S(1)}, f32[768]{0:T(1024)}, u32[]{:S(2)}) copy-start(f32[768]{0:T(1024)} %copy-done.49) | copy-start | bytes 9220
  882.8 140.6 %copy-start.79 = (f32[256]{0:T(256)S(1)}, f32[256]{0:T(256)}, u32[]{:S(2)}) copy-start(f32[256]{0:T(256)} %copy-done.78) | copy-start | bytes 3076
  882.8 142.4 %copy-start.87 = (f32[256]{0:T(256)S(1)}, f32[256]{0:T(256)}, u32[]{:S(2)}) copy-start(f32[256]{0:T(256)} %copy-done.86) | copy-start | bytes 3076
  977.3 49.1 %copy-start.60 = (s32[1024]{0:T(1024)S(1)}, s32[1024]{0:T(1024)}, u32[]{:S(2)}) copy-start(s32[1024]{0:T(1024)} %broadcast_clamp_fusion.1) | copy-start | bytes 12292
  1036.4 24.5 %all-to-all-start.2 = ((bf16[8,128,768]{2,1,0:T(8,128)(2,1)}), bf16[8,128,768]{2,1,0:T(8,128)(2,1)S(1)}, u32[]{:S(2)}, u32[]{:S(2)}) async-start(bf16[8,128,768]{2,1,0:T(8,128)(2,1)} %get-tuple-element.607), calls=%async_computation.4 | async-start | bytes 3145728 | tf_op jit(solution)/shard_map/all_to_all | solution.py:81
  1087.3 34.4 %copy-start.77 = (f32[256]{0:T(256)S(1)}, f32[256]{0:T(256)}, u32[]{:S(2)}) copy-start(f32[256]{0:T(256)} %copy-done.76) | copy-start | bytes 3076
  1087.3 34.7 %copy-start.96 = (f32[256]{0:T(256)S(1)}, f32[256]{0:T(256)}, u32[]{:S(2)}) copy-start(f32[256]{0:T(256)} %copy-done.95) | copy-start | bytes 3076
  1087.4 25.5 %all-to-all-start.3 = ((bf16[8,128,768]{2,1,0:T(8,128)(2,1)}), bf16[8,128,768]{2,1,0:T(8,128)(2,1)}, u32[]{:S(2)}, u32[]{:S(2)}) async-start(bf16[8,128,768]{2,1,0:T(8,128)(2,1)} %bitcast.247), calls=%async_computation.5 | async-start | bytes 3145728 | tf_op jit(solution)/shard_map/all_to_all | solution.py:81
  1091.8 111.3 %reduce-scatter.15.cloned.1.call-start = ((), (), s32[]{:S(2)}) async-start(), calls=%async_computation.17 | async-start | bytes 3538944 | tf_op jit(solution)/shard_map/reduce_scatter | solution.py:76
  1142.4 96.1 %reduce-scatter.13.cloned.1.call-start = ((), (), s32[]{:S(2)}) async-start(), calls=%async_computation.16 | async-start | bytes 3538944 | tf_op jit(solution)/shard_map/reduce_scatter | solution.py:76
  1190.0 48.4 %copy-start.33 = (bf16[256,768]{1,0:T(8,128)(2,1)S(1)}, bf16[256,768]{1,0:T(8,128)(2,1)}, u32[]{:S(2)}) copy-start(bf16[256,768]{1,0:T(8,128)(2,1)} %reduce-scatter.9.cloned.1.call-done) | copy-start | bytes 1179652
  1190.0 48.4 %copy-start.73 = (f32[768]{0:T(1024)S(1)}, f32[768]{0:T(1024)}, u32[]{:S(2)}) copy-start(f32[768]{0:T(1024)} %copy-done.72) | copy-start | bytes 9220
  1190.0 48.4 %copy-start.92 = (f32[256]{0:T(256)S(1)}, f32[256]{0:T(256)}, u32[]{:S(2)}) copy-start(f32[256]{0:T(256)} %copy-done.91) | copy-start | bytes 3076
  1190.0 234.0 %all-reduce.7.cloned.1.call-start = ((), (), s32[]{:S(2)}) async-start(), calls=%async_computation.24 | async-start | bytes 9437184
  1201.1 39.8 %copy-start.35 = (bf16[1,256,768]{2,1,0:T(8,128)(2,1)}, bf16[1,256,768]{2,1,0:T(8,128)(2,1)S(1)}, u32[]{:S(2)}) copy-start(bf16[1,256,768]{2,1,0:T(8,128)(2,1)S(1)} %copy.141) | copy-start | bytes 1179652
  1252.0 205.7 %all-gather.21.cloned.1.call-start = ((), (), s32[]{:S(2)}) async-start(), calls=%async_computation.18 | async-start | bytes 3538944 | tf_op jit(solution)/shard_map/all_gather | solution.py:68
  1257.4 283.3 %all-reduce.5.cloned.1.call-start = ((), (), s32[]{:S(2)}) async-start(), calls=%async_computation.20 | async-start | bytes 2359296 | tf_op jit(solution)/shard_map/psum | solution.py:408
  1268.9 158.2 %copy-start.31 = (bf16[8,128,768]{2,1,0:T(8,128)(2,1)S(1)}, bf16[8,128,768]{2,1,0:T(8,128)(2,1)}, u32[]{:S(2)}) copy-start(bf16[8,128,768]{2,1,0:T(8,128)(2,1)} %copy-done.30) | copy-start | bytes 4718596
  1426.9 254.5 %reduce-scatter.17.cloned.1.call-start = ((), (), s32[]{:S(2)}) async-start(), calls=%async_computation.19 | async-start | bytes 11796480 | tf_op jit(solution)/shard_map/reduce_scatter | solution.py:401
  1445.2 446.8 %reduce-scatter.19.cloned.1.call-start = ((), (), s32[]{:S(2)}) async-start(), calls=%async_computation.23 | async-start | bytes 15360000
  1684.8 262.3 %copy-start.56 = (f32[3,768]{1,0:T(4,128)S(1)}, f32[3,768]{1,0:T(4,128)}, u32[]{:S(2)}) copy-start(f32[3,768]{1,0:T(4,128)} %param.43) | copy-start | bytes 27652
  1684.8 262.3 %copy-start.80 = (f32[3,768]{1,0:T(4,128)S(1)}, f32[3,768]{1,0:T(4,128)}, u32[]{:S(2)}) copy-start(f32[3,768]{1,0:T(4,128)} %param.45) | copy-start | bytes 27652
  1684.8 262.3 %copy-start.81 = (f32[3,768]{1,0:T(4,128)S(1)}, f32[3,768]{1,0:T(4,128)}, u32[]{:S(2)}) copy-start(f32[3,768]{1,0:T(4,128)} %param.44) | copy-start | bytes 27652
  1684.8 263.0 %copy-start.39 = (f32[768,8]{0,1:T(8,128)S(1)}, f32[768,8]{0,1:T(8,128)}, u32[]{:S(2)}) copy-start(f32[768,8]{0,1:T(8,128)} %param.40) | copy-start | bytes 73732
  1684.8 263.0 %copy-start.66 = (f32[768,8]{0,1:T(8,128)S(1)}, f32[768,8]{0,1:T(8,128)}, u32[]{:S(2)}) copy-start(f32[768,8]{0,1:T(8,128)} %param.42) | copy-start | bytes 73732
  1684.8 263.0 %copy-start.67 = (f32[768,8]{0,1:T(8,128)S(1)}, f32[768,8]{0,1:T(8,128)}, u32[]{:S(2)}) copy-start(f32[768,8]{0,1:T(8,128)} %param.41) | copy-start | bytes 73732
  (99 other events, 994.8 us)
Sparse Core Ops, SparseCore 0:
  12.1 216.0 all-gather.12
  252.5 44.3 reduce-scatter.8
  299.2 89.3 all-gather.14
  393.0 30.7 all-gather.24
  426.3 32.3 all-gather.22
  460.7 166.7 all-gather.16
  686.3 28.6 all-gather.18
  977.5 45.8 reduce-scatter.10
  1142.5 45.4 reduce-scatter.14
  1192.1 46.2 reduce-scatter.12
  1252.0 171.9 all-reduce.6
  1426.3 31.2 all-gather.20
  1461.4 57.0 all-reduce.4
  1520.9 160.3 reduce-scatter.16
  1683.7 208.2 reduce-scatter.18
where the time goes:
time: 1990 us
  waiting for transfers between devices  1170 us (59%)
  matrix products  270 us (14%)
  local copies, waits for them, and re-layouts  233 us (12%)
  other arithmetic  201 us (10%)
  blocking collectives  67.7 us (3%)
  between operations  21.6 us (1%)
    unnamed x17, waiting for transfers between devices  363 us
    all_gather x1, waiting for transfers between devices, body(): lax.all_gather(tables.astype(jnp.bfloat16), 'dp', axis=1, tiled=True)  216 us
    reduce_scatter x1, waiting for transfers between devices, body(): lax.psum_scatter(jnp.stack([grad_up, grad_down])[None].astype(jnp.bfloat1...  138 us
    reduce_scatter x4, waiting for transfers between devices, group_sums(): lax.psum_scatter(for_sending(values), 'expert', scatter_dimension=0, tile...  123 us
    all_gather x1, waiting for transfers between devices, body(): lax.all_gather(experts.astype(jnp.bfloat16), 'dp', axis=3, tiled=True)  107 us
    all_gather x1, waiting for transfers between devices, body(): lax.all_gather(attn.astype(jnp.bfloat16), 'dp', axis=1, tiled=True)  90.5 us
    all_gather x4, waiting for transfers between devices, group_rows(): lax.all_gather(for_sending(values), 'expert', axis=0, tiled=True)  83.6 us
    gather x4, local copies, waits for them, and re-layouts, head_stats(): jnp.take_along_axis(logits, target_blk[:, None], axis=1)[:, 0]  83.3 us
  transfers between devices with their start and end apart: 19, of which 16 were waited for; matrix products, arithmetic and copies ran while one was open for 14% of the time, Pallas kernels for 0%

commit v1 on v0

v1 whole, which is shorter than its diff:
```python
import functools

import jax
import jax.numpy as jnp
from jax import lax
from jax.experimental import pallas as pl
from jax.experimental.pallas import tpu as pltpu
from jax.sharding import PartitionSpec as P

HEADS = 12
SEQ = 2048
NDOM = 4
STEP = 10


NORM_EPS = 1e-05
BETA = 0.5
ADAM_EPS = 1e-08
CLIP = 1.0
MASKED = -1e30
BF = jnp.bfloat16
F32 = jnp.float32
VMEM_BYTES = 56 * 1024 * 1024


def normed(values, gain):
    return values * lax.rsqrt(jnp.mean(values * values, axis=-1, keepdims=True) + NORM_EPS) * gain


def norm_back(values, gain, grad):
    _, pull = jax.vjp(normed, values, gain)
    return pull(grad)


def gelu(values):
    return jax.nn.gelu(values, approximate=True)


def adam(weight, grad, first, second, rate, decay):
    first = BETA * first + (1.0 - BETA) * grad
    second = BETA * second + (1.0 - BETA) * grad * grad
    correct = 1.0 - BETA**STEP
    weight = weight - rate * (
        first / correct / (jnp.sqrt(second / correct) + ADAM_EPS) + decay * weight
    )
    return (first, second, weight, weight.astype(BF))


def dot(a, b, contract):
    return lax.dot_general(a, b, ((contract[0], contract[1]), ((), ())), preferred_element_type=F32)


def dot_nn(a, b):
    return dot(a, b, ((1,), (0,)))


def dot_nt(a, b):
    return dot(a, b, ((1,), (1,)))


def dot_tn(a, b):
    return dot(a, b, ((0,), (0,)))


def swap(array, bits, axis):
    pairs = [(i, i ^ bits) for i in range(lax.axis_size(axis))]
    return lax.ppermute(array, axis, pairs)


def turn(array, steps):
    count = lax.axis_size("dp")
    return lax.ppermute(array, "dp", [(i, (i + steps) % count) for i in range(count)])


def quick_expert():
    return lax.axis_size("expert") == 8


def quick_dp():
    return lax.axis_size("dp") == 4


def block_order():
    count = lax.axis_size("expert")
    if quick_expert():
        return lax.axis_index("expert") ^ jnp.arange(count)
    return jnp.arange(count)


def gather_blocks(rows):
    if not quick_expert():
        gathered = lax.all_gather(rows, "expert")
        return [gathered[i] for i in range(lax.axis_size("expert"))]
    half = rows.shape[0] // 2
    one, two, four = (swap(rows, bits, "expert") for bits in (1, 2, 4))
    six_a = swap(two[:half], 4, "expert")
    six_b = swap(four[half:], 2, "expert")
    three = swap(two, 1, "expert")
    five = swap(four, 1, "expert")
    seven_a = swap(six_a, 1, "expert")
    seven_b = swap(six_b, 1, "expert")
    return [
        rows,
        one,
        two,
        three,
        four,
        five,
        jnp.concatenate([six_a, six_b]),
        jnp.concatenate([seven_a, seven_b]),
    ]


def gather_rows(rows):
    return jnp.concatenate(gather_blocks(rows))


def sum_blocks(blocks):
    if not quick_expert():
        return lax.psum_scatter(
            jnp.stack(blocks), "expert", scatter_dimension=0, tiled=False
        ).astype(F32)
    half = blocks[0].shape[0] // 2
    other = [swap(blocks[j], 1, "expert") for j in (6 + 1, 2 + 1, 4 + 1, 1)]
    six = (blocks[6].astype(F32) + other[0].astype(F32)).astype(BF)
    two = blocks[2].astype(F32) + other[1].astype(F32)
    four = blocks[4].astype(F32) + other[2].astype(F32)
    six_a = swap(six[:half], 2, "expert")
    six_b = swap(six[half:], 4, "expert")
    two_a = swap(two[:half].astype(BF), 2, "expert")
    four_b = swap(four[half:].astype(BF), 4, "expert")
    four_a = swap((four[:half] + six_a.astype(F32)).astype(BF), 4, "expert")
    two_b = swap((two[half:] + six_b.astype(F32)).astype(BF), 2, "expert")
    mine = blocks[0].astype(F32) + other[3].astype(F32)
    return jnp.concatenate(
        [
            mine[:half] + two_a.astype(F32) + four_a.astype(F32),
            mine[half:] + two_b.astype(F32) + four_b.astype(F32),
        ]
    )


def split_blocks(rows):
    count = lax.axis_size("expert")
    size = rows.shape[0] // count
    return [rows[i * size : (i + 1) * size] for i in range(count)]


def exchange(blocks):
    if not quick_expert():
        swapped = lax.all_to_all(jnp.stack(blocks), "expert", split_axis=0, concat_axis=0)
        return [swapped[i] for i in range(len(blocks))]
    return [blocks[0]] + [swap(blocks[k], k, "expert") for k in range(1, 8)]


def gather_shards(shard):
    if not quick_dp():
        gathered = lax.all_gather(shard, "dp")
        return [gathered[i] for i in range(lax.axis_size("dp"))]
    below = turn(shard, 1)
    above = turn(shard, -1)
    far = turn(below, 1)
    return [shard, below, far, above]


def shard_slot(shard_index):
    if quick_dp():
        return (lax.axis_index("dp") - shard_index) % 4
    return shard_index


def slot_shards():
    places = jnp.arange(lax.axis_size("dp"))
    if quick_dp():
        return (lax.axis_index("dp") - places) % 4
    return places


def sum_shards(parts):
    if not quick_dp():
        return lax.psum_scatter(
            jnp.stack(parts), "dp", scatter_dimension=0, tiled=False
        ).astype(F32)
    own, above_by_three, two, above = parts
    far = turn(two, 1)
    back = turn(above_by_three, -1)
    near = turn((above.astype(F32) + far.astype(F32)).astype(BF), 1)
    return own.astype(F32) + near.astype(F32) + back.astype(F32)


def sum_everywhere(array):
    for axis in ("expert", "dp"):
        bits = 1
        while bits < lax.axis_size(axis):
            array = array + swap(array, bits, axis)
            bits *= 2
    return array


def params():
    return pltpu.CompilerParams(
        dimension_semantics=("arbitrary",), vmem_limit_bytes=VMEM_BYTES
    )


def pair_scores(query, keys, key_place, query_place):
    scores = dot_nt(keys, query)
    return jnp.where(key_place <= query_place, scores, MASKED)


def attend_kernel(q_ref, k_ref, v_ref, kp_ref, qp_ref, mixed_ref, lse_ref):
    step = pl.program_id(0)
    keys, values = k_ref[...], v_ref[...]
    query = q_ref[...]
    lanes = lax.broadcasted_iota(jnp.int32, query.shape, 1)
    head_dim = query.shape[1] // 2
    scale = head_dim ** (-0.5)
    mixed = None
    for part in range(2):
        here = (lanes // head_dim) == part
        masked_query = jnp.where(here, query * scale, 0).astype(BF)
        scores = pair_scores(masked_query, keys, kp_ref[...], qp_ref[...])
        top = jnp.max(scores, axis=0, keepdims=True)
        weights = jnp.exp(scores - top)
        total = jnp.sum(weights, axis=0, keepdims=True)
        out = dot_tn(values, weights.astype(BF)) / total
        out = jnp.transpose(out)
        mixed = out if part == 0 else jnp.where(here, out, mixed)
        lse_ref[pl.ds(2 * step + part, 1), :] = top + jnp.log(total)
    mixed_ref[...] = mixed.astype(BF)


def attend(queries, keys, values, key_place, query_place):
    local, width = queries.shape
    group = keys.shape[0]
    pair = 2 * (width // HEADS)
    steps = HEADS // 2
    return pl.pallas_call(
        attend_kernel,
        grid=(steps,),
        in_specs=[
            pl.BlockSpec((local, pair), lambda i: (0, i)),
            pl.BlockSpec((group, pair), lambda i: (0, i)),
            pl.BlockSpec((group, pair), lambda i: (0, i)),
            pl.BlockSpec((group, 1), lambda i: (0, 0)),
            pl.BlockSpec((1, local), lambda i: (0, 0)),
        ],
        out_specs=[
            pl.BlockSpec((local, pair), lambda i: (0, i)),
            pl.BlockSpec((HEADS, local), lambda i: (0, 0)),
        ],
        out_shape=[
            jax.ShapeDtypeStruct((local, width), BF),
            jax.ShapeDtypeStruct((HEADS, local), F32),
        ],
        compiler_params=params(),
        cost_estimate=pl.CostEstimate(
            flops=4 * local * group * width * 4,
            bytes_accessed=4 * group * width,
            transcendentals=HEADS * local * group,
        ),
        name="attend",
    )(queries, keys, values, key_place, query_place)


def attend_back_kernel(
    q_ref, k_ref, v_ref, do_ref, o_ref, lse_ref, kp_ref, qp_ref, dq_ref, dk_ref, dv_ref
):
    step = pl.program_id(0)
    keys, values = k_ref[...], v_ref[...]
    query, grad_out = q_ref[...], do_ref[...]
    lanes = lax.broadcasted_iota(jnp.int32, query.shape, 1)
    head_dim = query.shape[1] // 2
    scale = head_dim ** (-0.5)
    product = jnp.transpose(grad_out.astype(F32) * o_ref[...].astype(F32))
    grad_query = grad_keys = grad_values = None
    for part in range(2):
        here = (lanes // head_dim) == part
        masked_query = jnp.where(here, query * scale, 0).astype(BF)
        masked_grad = jnp.where(here, grad_out, 0).astype(BF)
        scores = pair_scores(masked_query, keys, kp_ref[...], qp_ref[...])
        weights = jnp.exp(scores - lse_ref[pl.ds(2 * step + part, 1), :])
        delta = jnp.sum(
            product[part * head_dim : (part + 1) * head_dim], axis=0, keepdims=True
        )
        grad_weights = dot_nt(values, masked_grad)
        grad_scores = (weights * (grad_weights - delta)).astype(BF)
        dq = jnp.transpose(dot_tn(keys, grad_scores)) * scale
        dk = dot_nn(grad_scores, masked_query)
        dv = dot_nn(weights.astype(BF), masked_grad)
        if part == 0:
            grad_query, grad_keys, grad_values = dq, dk, dv
        else:
            grad_query = jnp.where(here, dq, grad_query)
            grad_keys, grad_values = grad_keys + dk, grad_values + dv
    dq_ref[...] = grad_query.astype(BF)
    dk_ref[...] = grad_keys.astype(BF)
    dv_ref[...] = grad_values.astype(BF)


def attend_back(queries, keys, values, grad_out, mixed, lse, key_place, query_place):
    local, width = queries.shape
    group = keys.shape[0]
    pair = 2 * (width // HEADS)
    steps = HEADS // 2
    rows = pl.BlockSpec((local, pair), lambda i: (0, i))
    cols = pl.BlockSpec((group, pair), lambda i: (0, i))
    return pl.pallas_call(
        attend_back_kernel,
        grid=(steps,),
        in_specs=[
            rows,
            cols,
            cols,
            rows,
            rows,
            pl.BlockSpec((HEADS, local), lambda i: (0, 0)),
            pl.BlockSpec((group, 1), lambda i: (0, 0)),
            pl.BlockSpec((1, local), lambda i: (0, 0)),
        ],
        out_specs=[rows, cols, cols],
        out_shape=[
            jax.ShapeDtypeStruct((local, width), BF),
            jax.ShapeDtypeStruct((group, width), BF),
            jax.ShapeDtypeStruct((group, width), BF),
        ],
        compiler_params=params(),
        cost_estimate=pl.CostEstimate(
            flops=10 * local * group * width * 4,
            bytes_accessed=8 * group * width,
            transcendentals=HEADS * local * group,
        ),
        name="attend_back",
    )(queries, keys, values, grad_out, mixed, lse, key_place, query_place)


def head_kernel(count, rows_ref, place_ref, *refs):
    heads, exps, stats_ref = refs[:count], refs[count : 2 * count], refs[2 * count]
    rows, place = rows_ref[...], place_ref[...]
    depth = heads[0].shape[0]
    scores = [dot_nt(head[...], rows) for head in heads]
    iota = lax.broadcasted_iota(jnp.int32, scores[0].shape, 0)
    top = functools.reduce(jnp.maximum, [jnp.max(s, axis=0, keepdims=True) for s in scores])
    total = picked = jnp.zeros_like(top)
    for k in range(count):
        weights = jnp.exp(scores[k] - top)
        total = total + jnp.sum(weights, axis=0, keepdims=True)
        chosen = jnp.where(iota == place - k * depth, scores[k], 0.0)
        picked = picked + jnp.sum(chosen, axis=0, keepdims=True)
        exps[k][...] = weights.astype(BF)
    stats_ref[0:1, :] = top
    stats_ref[1:2, :] = total
    stats_ref[2:3, :] = picked
    stats_ref[3:8, :] = jnp.zeros((5, top.shape[1]), F32)


def head_forward(rows, place, heads):
    group, width = rows.shape
    count, depth = len(heads), heads[0].shape[0]
    block = min(256, group)
    whole = pl.BlockSpec((depth, width), lambda i: (0, 0))
    cols = pl.BlockSpec((depth, block), lambda i: (0, i))
    results = pl.pallas_call(
        functools.partial(head_kernel, count),
        grid=(group // block,),
        in_specs=[
            pl.BlockSpec((block, width), lambda i: (i, 0)),
            pl.BlockSpec((1, block), lambda i: (0, i)),
        ]
        + [whole] * count,
        out_specs=[cols] * count + [pl.BlockSpec((8, block), lambda i: (0, i))],
        out_shape=[jax.ShapeDtypeStruct((depth, group), BF)] * count
        + [jax.ShapeDtypeStruct((8, group), F32)],
        compiler_params=params(),
        cost_estimate=pl.CostEstimate(
            flops=2 * group * width * depth * count,
            bytes_accessed=2 * count * depth * (group + width),
            transcendentals=group * depth * count,
        ),
        name="head_forward",
    )(rows, place, *heads)
    return results[:count], results[count]


def logit_grads(exps, coef_ref, place, offset):
    grads = exps.astype(F32) * coef_ref[0:1, :]
    iota = lax.broadcasted_iota(jnp.int32, grads.shape, 0)
    return (grads - jnp.where(iota == place - offset, coef_ref[1:2, :], 0.0)).astype(BF)


def head_rows_kernel(count, coef_ref, place_ref, *refs):
    heads, exps, out_ref = refs[:count], refs[count : 2 * count], refs[2 * count]
    depth = heads[0].shape[0]
    out = None
    for k in range(count):
        grads = logit_grads(exps[k][...], coef_ref, place_ref[...], k * depth)
        term = dot_tn(grads, heads[k][...])
        out = term if out is None else out + term
    out_ref[...] = out.astype(BF)


def head_rows_back(coef, place, heads, exps):
    depth, width = heads[0].shape
    group = exps[0].shape[1]
    count = len(heads)
    block = min(256, group)
    whole = pl.BlockSpec((depth, width), lambda i: (0, 0))
    cols = pl.BlockSpec((depth, block), lambda i: (0, i))
    return pl.pallas_call(
        functools.partial(head_rows_kernel, count),
        grid=(group // block,),
        in_specs=[
            pl.BlockSpec((2, block), lambda i: (0, i)),
            pl.BlockSpec((1, block), lambda i: (0, i)),
        ]
        + [whole] * count
        + [cols] * count,
        out_specs=pl.BlockSpec((block, width), lambda i: (i, 0)),
        out_shape=jax.ShapeDtypeStruct((group, width), BF),
        compiler_params=params(),
        cost_estimate=pl.CostEstimate(
            flops=2 * group * width * depth * count,
            bytes_accessed=2 * count * depth * (group + width),
            transcendentals=0,
        ),
        name="head_rows_back",
    )(coef, place, *heads, *exps)


def head_weight_kernel(offset, coef_ref, place_ref, exps_ref, rows_ref, out_ref, total):
    step = pl.program_id(0)
    grads = logit_grads(exps_ref[...], coef_ref, place_ref[...], offset)
    term = dot_nn(grads, rows_ref[...])

    @pl.when(step == 0)
    def _():
        total[...] = term

    @pl.when(step > 0)
    def _():
        total[...] += term

    @pl.when(step == pl.num_programs(0) - 1)
    def _():
        out_ref[...] = total[...].astype(BF)


def head_weight_back(coef, place, exps, rows, offset):
    depth, group = exps.shape
    width = rows.shape[1]
    block = min(512, group)
    return pl.pallas_call(
        functools.partial(head_weight_kernel, offset),
        grid=(group // block,),
        in_specs=[
            pl.BlockSpec((2, block), lambda i: (0, i)),
            pl.BlockSpec((1, block), lambda i: (0, i)),
            pl.BlockSpec((depth, block), lambda i: (0, i)),
            pl.BlockSpec((block, width), lambda i: (i, 0)),
        ],
        out_specs=pl.BlockSpec((depth, width), lambda i: (0, 0)),
        out_shape=jax.ShapeDtypeStruct((depth, width), BF),
        scratch_shapes=[pltpu.VMEM((depth, width), F32)],
        compiler_params=params(),
        cost_estimate=pl.CostEstimate(
            flops=2 * group * width * depth,
            bytes_accessed=2 * (depth * group + group * width + depth * width),
            transcendentals=0,
        ),
        name="head_weight_back",
    )(coef, place, exps, rows)


def ranks(hits):
    count, length = hits.shape
    cut = hits.reshape(count, length // 128, 128)
    ones = cut.astype(BF)
    before = (jnp.arange(128)[:, None] < jnp.arange(128)[None, :]).astype(BF)
    inner = lax.dot_general(ones, before, (((2,), (0,)), ((), ())), preferred_element_type=F32)
    sums = jnp.sum(ones.astype(F32), axis=2)
    earlier = jnp.arange(length // 128)[:, None] > jnp.arange(length // 128)[None, :]
    outer = jnp.sum(jnp.where(earlier[None], sums[:, None, :], 0.0), axis=2)
    return jnp.where(cut, inner + outer[..., None], -1.0).reshape(count, length)


def split_high_low(values):
    high = lax.reduce_precision(values, 8, 7)
    return high.astype(BF), (values - high).astype(BF)


def body(
    ids,
    targets,
    loss_mask,
    domain_ids,
    expert_lists,
    tables,
    tables_m,
    tables_v,
    attn,
    attn_m,
    attn_v,
    experts,
    experts_m,
    experts_v,
    router,
    router_m,
    router_v,
    gains,
    gains_m,
    gains_v,
):
    shards = lax.axis_size("expert")
    rows_dp = lax.axis_size("dp")
    member = lax.axis_index("expert")
    batch_row = lax.axis_index("dp")
    group = ids.shape[0]
    local = group // shards
    own = member * local
    width = gains.shape[1]
    slots = expert_lists.shape[3]
    words = tables.shape[1]
    order = block_order()

    attn_b = attn.astype(BF)
    if quick_expert() and quick_dp():
        piece = attn.shape[1] // 2
        cut = attn_b.reshape(8, piece, width)
        mine = lax.dynamic_index_in_dim(cut, member, 0, False)
        attn_parts = jnp.stack([mine] + [turn(mine, k) for k in range(1, 4)])
    table_b = tables[0].astype(BF)
    experts_b = experts[0].astype(BF)
    head_b = tables[1].astype(BF)

    capacity = min(group, 2 * (-(-group // (shards * rows_dp))))
    capacity = -(-capacity // 16) * 16
    ids_dp = jnp.stack([ids] + [turn(ids, k) for k in range(1, rows_dp)])
    first_word = (member * rows_dp + batch_row) * words
    ids_own = ids_dp - first_word
    rank_own = ranks((ids_own >= 0) & (ids_own < words))
    ids_own = ids_own.astype(F32)
    place = jnp.arange(capacity, dtype=F32)
    owners = (batch_row + jnp.arange(rows_dp)) % rows_dp
    ids_from = ids[None, :] - ((member * rows_dp + owners) * words)[:, None]
    rank_from = ranks((ids_from >= 0) & (ids_from < words))
    rank_from = rank_from.reshape(rows_dp, shards, local)[:, order].reshape(rows_dp, group)
    owner_of = ids_dp // words
    owner_hits = owner_of[:, None, :] == jnp.arange(shards * rows_dp)[None, :, None]
    most = jnp.max(jnp.sum(owner_hits.astype(F32), axis=2)).astype(jnp.int32)
    rounds = (most + capacity - 1) // capacity

    def own_select(turn_no):
        chosen = rank_own[:, None, :] == (place + turn_no * capacity)[None, :, None]
        at = jnp.sum(jnp.where(chosen, ids_own[:, None, :] + 1.0, 0.0), axis=2) - 1.0
        at = at.reshape(-1)[:, None]
        return (at == jnp.arange(words, dtype=F32)[None, :]).astype(BF)

    def from_select(turn_no):
        at = (place + turn_no * capacity)[None, None, :]
        chosen = rank_from[:, :, None] == at
        return jnp.transpose(chosen, (1, 0, 2)).reshape(group, -1).astype(BF)

    def look_up(turn_no, select_own, select_from):
        found = dot_nn(select_own, table_b).astype(BF).reshape(rows_dp, capacity, width)
        arrived = [found[0]] + [turn(found[k], -k) for k in range(1, rows_dp)]
        return dot_nn(select_from, jnp.concatenate(arrived)).astype(BF)

    def spread(turn_no, grads, select_own, select_from):
        chosen = dot_tn(select_from, grads).astype(BF).reshape(rows_dp, capacity, width)
        arrived = [chosen[0]] + [turn(chosen[k], k) for k in range(1, rows_dp)]
        return dot_tn(select_own, jnp.concatenate(arrived))

    select_own = own_select(0)
    select_from = from_select(0)
    looked = look_up(0, select_own, select_from)
    _, looked = lax.while_loop(
        lambda state: state[0] < rounds,
        lambda state: (
            state[0] + 1,
            state[1]
            + look_up(
                state[0],
                own_select(state[0].astype(F32)),
                from_select(state[0].astype(F32)),
            ),
        ),
        (jnp.int32(1), looked),
    )
    expert_shards = gather_shards(experts_b)
    head_shards = gather_shards(head_b)
    if quick_expert() and quick_dp():
        attn_blocks = gather_blocks(attn_parts.reshape(4 * piece, width))
        attn_blocks = jnp.stack(attn_blocks)[order].reshape(4, 2, 4, piece, width)
        attn_full = jnp.transpose(attn_blocks[:, :, slot_shards()], (0, 2, 1, 3, 4))
        attn_full = attn_full.reshape(4, width, width)
    else:
        attn_full = lax.all_gather(attn_b, "dp", axis=1, tiled=True)
    embedded = sum_blocks(split_blocks(looked))
    router_b = router.astype(BF)

    normed_ab = normed(embedded, gains[0]).astype(BF)
    normed_all = gather_rows(normed_ab)
    queries = dot_nn(normed_ab, attn_full[0]).astype(BF)
    keys = dot_nn(normed_all, attn_full[1]).astype(BF)
    values = dot_nn(normed_all, attn_full[2]).astype(BF)
    token_place = (order[:, None] * local + jnp.arange(local)[None, :]).reshape(-1)
    seq_start = own // SEQ * SEQ
    key_place = jnp.where(token_place >= seq_start, token_place, group)[:, None]
    query_place = (own + jnp.arange(local))[None, :]
    mixed_b, logsum = attend(queries, keys, values, key_place, query_place)
    resid_one = embedded + dot_nn(mixed_b, attn_full[3])

    normed_bb = normed(resid_one, gains[1]).astype(BF)
    router_logits = dot_nn(normed_bb, router_b)
    gates = jax.nn.softmax(router_logits, axis=-1)
    lists = expert_lists[0, 0][order]
    hot = lists[:, :, None] == jnp.arange(local)[None, None, :]
    hot_b = hot.reshape(-1, local).astype(BF)
    gates_mine = jnp.transpose(gates[:, order])
    gate_table = jnp.where(hot, gates_mine[:, None, :], 0.0)
    slot_gates = jnp.sum(gate_table, axis=2).reshape(-1, 1)
    gate_high, gate_low = split_high_low(gate_table.reshape(-1, local))
    send = dot_nn(hot_b, normed_bb).astype(BF)
    received = jnp.concatenate(exchange(split_blocks(send)))
    pres, hiddens, produced = [], [], None
    for shard in expert_shards:
        pre = dot_nn(received, shard[0])
        hidden = gelu(pre).astype(BF)
        term = dot_nt(hidden, shard[1])
        produced = term if produced is None else produced + term
        pres.append(pre)
        hiddens.append(hidden)
    returned = jnp.concatenate(exchange(split_blocks(produced.astype(BF))))
    mixture = dot_tn(gate_high, returned) + dot_tn(gate_low, returned)
    resid_two = resid_one + mixture
    normed_cb = normed(resid_two, gains[2]).astype(BF)

    rows_all = gather_rows(normed_cb)
    targets_mine = targets.reshape(shards, local)[order].reshape(-1)
    word = targets_mine - member * (rows_dp * words)
    word_hit = (word >= 0) & (word < rows_dp * words)
    word_place = jnp.where(word_hit, shard_slot(word // words) * words + word % words, -1)[None, :]
    exps, stats = head_forward(rows_all, word_place, head_shards)
    stats = stats[:3]
    if quick_expert():
        gathered = [stats]
        for k in range(1, 8):
            other = swap(stats, k, "expert")
            gathered.append(
                jnp.concatenate([other[:, (j ^ k) * local : (j ^ k) * local + local] for j in range(8)], axis=1)
            )
        gathered = jnp.stack(gathered)
    else:
        gathered = lax.all_gather(stats, "expert")
    top = jnp.max(gathered[:, 0], axis=0)
    total = jnp.sum(gathered[:, 1] * jnp.exp(gathered[:, 0] - top[None, :]), axis=0)
    logsum_tok = top + jnp.log(total)
    loss_tok = logsum_tok - jnp.sum(gathered[:, 2], axis=0)
    everything = loss_mask.shape[0]
    domain_of = jnp.take(domain_ids, jnp.arange(everything) // SEQ)
    hits = ((domain_of[:, None] == jnp.arange(NDOM)[None, :]) & (loss_mask[:, None] > 0)).astype(
        F32
    )
    counts = jnp.sum(hits, axis=0)
    domain_weight = 10.0 * (NDOM - jnp.arange(NDOM)).astype(F32) / jnp.maximum(counts, 1.0)
    group_hits = lax.dynamic_slice_in_dim(hits, batch_row * group, group, 0)
    group_hits = group_hits.reshape(shards, local, NDOM)[order].reshape(group, NDOM)
    token_weight = jnp.sum(group_hits * domain_weight[None, :], axis=1)
    own_block = 0 if quick_expert() else member
    own_sums = jnp.sum(
        lax.dynamic_slice_in_dim(group_hits, own_block * local, local, 0)
        * lax.dynamic_slice_in_dim(loss_tok, own_block * local, local, 0)[:, None],
        axis=0,
    )
    coef = jnp.stack([token_weight * jnp.exp(stats[0] - logsum_tok), token_weight])
    grad_rows_c = head_rows_back(coef, word_place, head_shards, exps)
    grad_heads = [
        head_weight_back(coef, word_place, exps[k], rows_all, k * words) for k in range(rows_dp)
    ]
    grad_head = sum_shards(grad_heads)
    grad_normed_c = sum_blocks(split_blocks(grad_rows_c))
    grad_two, grad_gain_c = norm_back(resid_two, gains[2], grad_normed_c)

    two_high, two_low = split_high_low(grad_two)
    grad_slot = dot_nn(hot_b, two_high) + dot_nn(hot_b, two_low)
    grad_gate_slot = jnp.sum(grad_slot * returned.astype(F32), axis=-1)
    grad_produced = jnp.concatenate(
        exchange(split_blocks((grad_slot * slot_gates).astype(BF)))
    )
    grad_experts_parts, grad_sent = [], None
    for shard, pre, hidden in zip(expert_shards, pres, hiddens):
        grad_hidden = dot_nn(grad_produced, shard[1])
        _, gelu_pull = jax.vjp(gelu, pre)
        grad_pre = gelu_pull(grad_hidden)[0].astype(BF)
        grad_down = dot_tn(grad_produced, hidden)
        grad_up = dot_tn(received, grad_pre)
        term = dot_nt(grad_pre, shard[0])
        grad_sent = term if grad_sent is None else grad_sent + term
        grad_experts_parts.append(jnp.stack([grad_up, grad_down]).astype(BF))
    grad_experts = sum_shards(grad_experts_parts)[None]
    grad_back = jnp.concatenate(exchange(split_blocks(grad_sent.astype(BF))))
    grad_normed_b = dot_tn(hot_b, grad_back)
    grad_gates = jnp.sum(
        jnp.where(hot, grad_gate_slot.reshape(shards, slots)[:, :, None], 0.0), axis=1
    )
    grad_gates = jnp.transpose(grad_gates[order])
    _, soft_pull = jax.vjp(lambda logit_rows: jax.nn.softmax(logit_rows, axis=-1), router_logits)
    grad_router_logits = soft_pull(grad_gates)[0].astype(BF)
    grad_router = dot_tn(normed_bb, grad_router_logits)
    grad_normed_b = grad_normed_b + dot_nt(grad_router_logits, router_b)
    normal_back, grad_gain_b = norm_back(resid_one, gains[1], grad_normed_b)
    grad_one = grad_two + normal_back

    grad_branch = grad_one.astype(BF)
    grad_wo = dot_tn(mixed_b, grad_branch)
    grad_mixed = dot_nt(grad_branch, attn_full[3]).astype(BF)
    grad_query, grad_keys, grad_values = attend_back(
        queries, keys, values, grad_mixed, mixed_b, logsum, key_place, query_place
    )
    grad_normed_rows = dot_nt(grad_keys, attn_full[1]) + dot_nt(grad_values, attn_full[2])
    grad_normed_a = sum_blocks(split_blocks(grad_normed_rows.astype(BF)))
    grad_normed_a = grad_normed_a + dot_nt(grad_query, attn_full[0])
    normal_front, grad_gain_a = norm_back(embedded, gains[0], grad_normed_a)
    grad_embedded = (grad_one + normal_front).astype(BF)
    grad_embedded_all = gather_rows(grad_embedded)
    grad_embed = spread(0, grad_embedded_all, select_own, select_from)
    _, grad_embed = lax.while_loop(
        lambda state: state[0] < rounds,
        lambda state: (
            state[0] + 1,
            state[1]
            + spread(
                state[0],
                grad_embedded_all,
                own_select(state[0].astype(F32)),
                from_select(state[0].astype(F32)),
            ),
        ),
        (jnp.int32(1), grad_embed),
    )
    grad_attn = jnp.stack(
        [
            dot_tn(normed_ab, grad_query),
            dot_tn(normed_all, grad_keys),
            dot_tn(normed_all, grad_values),
            grad_wo,
        ]
    ).astype(BF)
    if quick_expert() and quick_dp():
        cut = grad_attn.reshape(4, 4, 2, piece, width)
        cut = jnp.transpose(cut, (0, 2, 1, 3, 4)).reshape(8, 4, piece, width)
        cut = cut[order][:, slot_shards()].reshape(8, 4 * piece, width)
        part = sum_blocks([cut[j] for j in range(8)]).astype(BF)
        part = sum_shards([part[k * piece : (k + 1) * piece] for k in range(4)])
        attn_squares = jnp.sum(part * part)
        back = jnp.stack(gather_blocks(part.astype(BF)))[order]
        grad_attn = back.reshape(4, 2 * piece, width).astype(F32)
    else:
        grad_attn = lax.psum_scatter(grad_attn, "dp", scatter_dimension=1, tiled=True)
        grad_attn = lax.psum(grad_attn, "expert").astype(F32)
        attn_squares = jnp.sum(grad_attn * grad_attn) / shards
    squares = (
        jnp.sum(grad_embed * grad_embed)
        + jnp.sum(grad_head * grad_head)
        + jnp.sum(grad_experts * grad_experts)
        + attn_squares
    )
    small = jnp.concatenate(
        [
            grad_router.reshape(-1),
            grad_gain_a,
            grad_gain_b,
            grad_gain_c,
            own_sums,
            squares[None],
        ]
    )
    small = jnp.pad(small, (0, -small.shape[0] % 1024)).reshape(-1, 128)
    small = sum_everywhere(small).reshape(-1)
    edge = router.size
    grad_router = small[:edge].reshape(router.shape)
    grad_gains = small[edge : edge + 3 * width].reshape(3, width)
    domain_sums = small[edge + 3 * width : edge + 3 * width + NDOM]
    squares = small[edge + 3 * width + NDOM]
    grad_norm = jnp.sqrt(
        squares + jnp.sum(grad_router * grad_router) + jnp.sum(grad_gains * grad_gains)
    )
    factor = jnp.minimum(1.0, CLIP / (grad_norm + 1e-06))
    grad_tables = jnp.stack([grad_embed, grad_head])
    tables_out = adam(tables, grad_tables * factor, tables_m, tables_v, 0.1, 0.01)
    attn_out = adam(attn, grad_attn * factor, attn_m, attn_v, 0.1, 0.01)
    experts_out = adam(experts, grad_experts * factor, experts_m, experts_v, 0.1, 0.01)
    router_out = adam(router, grad_router * factor, router_m, router_v, 0.04, 0.01)
    gains_out = adam(gains, grad_gains * factor, gains_m, gains_v, 0.4, 0.0)
    return (
        domain_sums,
        counts,
        grad_norm,
        *tables_out,
        *attn_out,
        *experts_out,
        *router_out,
        *gains_out,
    )


def solution(mesh):
    table = P(None, ("expert", "dp"), None)
    attn = P(None, "dp", None)
    expert = P("expert", None, None, "dp")
    in_specs = (
        P("dp"),
        P("dp"),
        P(),
        P(),
        P("dp", "expert", None, None),
        *[table] * 3,
        *[attn] * 3,
        *[expert] * 3,
        *[P()] * 6,
    )
    out_specs = (*[P()] * 3, *[table] * 4, *[attn] * 4, *[expert] * 4, *[P()] * 8)
    return jax.shard_map(body, mesh=mesh, in_specs=in_specs, out_specs=out_specs, check_vma=False)
```

time: 1990 us -> 1090 us (0.55)
  waiting for transfers between devices: 1170 us -> 508 us
  matrix products: 270 us -> 111 us
  local copies, waits for them, and re-layouts: 233 us -> 94.9 us
  Pallas kernels: 0 us -> 124 us
  starting transfers between devices: 17.4 us -> 132 us
  other arithmetic: 201 us -> 100 us
  blocking collectives: 67.7 us -> 0 us
    ppermute x0 -> x152, waiting for transfers between devices: none -> 508 us  [the longest x27 358 us: turn(): lax.ppermute(array, 'dp', [(i, (i + steps) % count) for i in range(count)])]
    all_gather x7 -> x0, waiting for transfers between devices: 497 us -> none  [the longest x1 216 us: body(): lax.all_gather(tables.astype(jnp.bfloat16), 'dp', axis=1, tiled=True)]
    unnamed x17 -> x0, waiting for transfers between devices: 363 us -> none
    reduce_scatter x5 -> x0, waiting for transfers between devices: 261 us -> none  [the longest x1 138 us: body(): lax.psum_scatter(jnp.stack([grad_up, grad_down])[None].astype(jnp.bfloat1...]
    dot_general x37 -> x51, matrix products: 270 us -> 111 us  [the longest x49 111 us: dot(): lax.dot_general(a, b, ((contract[0], contract[1]), ((), ())), preferred_e...]
    ppermute x0 -> x152, starting transfers between devices: none -> 132 us  [the longest x125 93.7 us: swap(): return lax.ppermute(array, axis, pairs)]
    pallas_call x0 -> x8, Pallas kernels: none -> 124 us  [the longest x4 33.8 us: head_weight_back(): pl.pallas_call(functools.partial(head_weight_kernel, offset), grid=(group...]
    gather x8 -> x11, local copies, waits for them, and re-layouts: 111 us -> 28.1 us  [the longest x2 10.9 us: body(): cut = cut[order][:, slot_shards()].reshape(8, 4 * piece, width)]
  transfers between devices with their start and end apart: 19 -> 152, of which waited for: 16 -> 59; matrix products, arithmetic and copies ran while one was open for 14% -> 17% of each run, Pallas kernels for 0% -> 4%
where the time goes in v1:
time: 1090 us; the launch traced here: 1080 us
  waiting for transfers between devices  508 us (47%)
  starting transfers between devices  132 us (12%)
  Pallas kernels  124 us (11%)
  matrix products  111 us (10%)
  other arithmetic  100 us (9%)
  local copies, waits for them, and re-layouts  94.9 us (9%)
    ppermute x27, waiting for transfers between devices, turn(): lax.ppermute(array, 'dp', [(i, (i + steps) % count) for i in range(count)])  358 us
    ppermute x125, waiting for transfers between devices, swap(): return lax.ppermute(array, axis, pairs)  150 us
    dot_general x49, matrix products, dot(): lax.dot_general(a, b, ((contract[0], contract[1]), ((), ())), preferred_e...  111 us
    ppermute x125, starting transfers between devices, swap(): return lax.ppermute(array, axis, pairs)  93.7 us
    ppermute x27, starting transfers between devices, turn(): lax.ppermute(array, 'dp', [(i, (i + steps) % count) for i in range(count)])  38.5 us
    convert_element_type x5, other arithmetic, adam(): return (first, second, weight, weight.astype(BF))  35.2 us
    pallas_call x4, Pallas kernels, head_weight_back(): pl.pallas_call(functools.partial(head_weight_kernel, offset), grid=(group...  33.8 us
    unnamed x310, local copies, waits for them, and re-layouts  33.8 us
  transfers between devices with their start and end apart: 152, of which 59 were waited for; matrix products, arithmetic and copies ran while one was open for 17% of the time, Pallas kernels for 4%

profile of v1, /device:TPU:0, one launch (start us, length us, event | category | flops | bytes accessed | tf_op | source)
XLA Modules:
  0.0 1080.9 jit_solution(8448497130074442248)
XLA Ops:
  0.7 4.1 collective-permute-start.7
  16.7 4.1 convert_bitcast_fusion
  35.9 4.6 eq.271
  44.7 4.5 collective-permute-done.10
  55.9 6.4 collective-permute-start.22
  63.4 4.0 convert_element_type.535
  75.9 9.4 collective-permute-done.28
  89.3 4.7 collective-permute-done.17
  106.7 5.9 collective-permute-done.30
  117.9 5.4 gather_fusion.1
  123.3 5.4 gather_fusion.2
  136.1 4.7 collective-permute-done.40
  142.9 4.0 convolution_convert_fusion.v_ref
  146.8 3.9 convolution_convert_fusion.1.k_ref
  150.8 18.6 %attend.1 = (bf16[256,768]{1,0:T(8,128)(2,1)}, f32[12,256]{1,0:T(8,128)}) custom-call(bf16[256,768]{1,0:T(8,128)(2,1)} %convolution_convert_fusion.18.q_ref, bf16[2048,768]{1,0:T(8,128)(2,1)} %convolution_convert_fusion.1.k_ref, bf16[2048,768]{1,0:T(8,128)(2,1)} %convolution_convert_fusion.v_ref, s32[2048,1]{1,0:T(8,128)} %compare_select_fusion.kp_ref, ...), custom_call_target="tpu_custom_call" | custom-call | flops 6442450944 | bytes 6291456 | tf_op jit(solution)/shard_map/attend/pallas_call | solution.py:238
  176.1 4.0 collective-permute-done.44
  196.1 7.5 collective-permute-done.50
  213.6 4.1 fusion.93
  221.0 96.2 %collective-permute-done.51 = bf16[2,768,768]{2,1,0:T(8,128)(2,1)S(1)} collective-permute-done((bf16[2,768,768]{2,1,0:T(8,128)(2,1)}, bf16[2,768,768]{2,1,0:T(8,128)(2,1)S(1)}, u32[]{:S(2)}, u32[]{:S(2)}) %collective-permute-start.51) | collective-permute-done | bytes 2359328 | tf_op jit(solution)/shard_map/ppermute | solution.py:72
  334.4 11.4 %collective-permute-done.57 = bf16[128,768]{1,0:T(8,128)(2,1)S(1)} collective-permute-done((bf16[128,768]{1,0:T(8,128)(2,1)}, bf16[128,768]{1,0:T(8,128)(2,1)S(1)}, u32[]{:S(2)}, u32[]{:S(2)}) %collective-permute-start.57) | collective-permute-done | bytes 196640 | tf_op jit(solution)/shard_map/ppermute | solution.py:67
  351.0 8.8 collective-permute-done.61
  378.0 8.3 collective-permute-done.70.refs_2_
  386.3 29.4 %head_forward.1 = (bf16[1000,2048]{1,0:T(8,128)(2,1)}, bf16[1000,2048]{1,0:T(8,128)(2,1)}, bf16[1000,2048]{1,0:T(8,128)(2,1)}, bf16[1000,2048]{1,0:T(8,128)(2,1)}, f32[8,2048]{1,0:T(8,128)}) custom-call(bf16[2048,768]{1,0:T(8,128)(2,1)} %constant_dynamic-update-slice_fusion.26.rows_ref, s32[1,2048]{1,0:T(1,128)} %fusion.169.place_ref, ...), custom_call_target="tpu_custom_call" | custom-call | flops 12582912000 | bytes 22528000 | tf_op jit(solution)/shard_map/head_forward/pallas_call | solution.py:363
  431.2 8.4 head_weight_back.7
  439.6 20.6 %head_rows_back.1 = bf16[2048,768]{1,0:T(8,128)(2,1)} custom-call(f32[2,2048]{1,0:T(2,128)} %pad_maximum_fusion.6.coef_ref, s32[1,2048]{1,0:T(1,128)} %fusion.169.place_ref, bf16[1000,768]{1,0:T(8,128)(2,1)} %get-tuple-element.533.refs_0_, bf16[1000,768]{1,0:T(8,128)(2,1)} %collective-permute-done.69.refs_1_, ...), custom_call_target="tpu_custom_call" | custom-call | flops 12582912000 | bytes 22528000 | tf_op jit(solution)/shard_map/head_rows_back/pallas_call | solution.py:409
  463.6 8.4 head_weight_back.6
  472.0 8.6 head_weight_back.5
  486.0 8.5 head_weight_back.4
  499.3 8.4 collective-permute-done.86
  533.1 7.0 collective-permute-done.91
  547.8 5.6 fusion.43
  562.3 4.3 fusion.50
  575.5 4.7 fusion.64
  594.8 9.9 collective-permute-done.98
  605.1 4.2 collective-permute-done.100
  613.0 21.1 %attend_back.1 = (bf16[256,768]{1,0:T(8,128)(2,1)}, bf16[2048,768]{1,0:T(8,128)(2,1)}, bf16[2048,768]{1,0:T(8,128)(2,1)}) custom-call(bf16[256,768]{1,0:T(8,128)(2,1)} %convolution_convert_fusion.18.q_ref, bf16[2048,768]{1,0:T(8,128)(2,1)} %convolution_convert_fusion.1.k_ref, bf16[2048,768]{1,0:T(8,128)(2,1)} %convolution_convert_fusion.v_ref, ...), custom_call_target="tpu_custom_call" | custom-call | flops 16106127360 | bytes 12582912 | tf_op jit(solution)/shard_map/attend_back/pallas_call | solution.py:308
  634.1 4.7 convolution_convert_fusion.6
  653.9 5.4 gather_fusion.8
  659.2 5.5 gather_fusion.9
  702.1 4.1 collective-permute-done.116
  728.5 32.4 %collective-permute-done.124 = bf16[128,768]{1,0:T(8,128)(2,1)S(1)} collective-permute-done((bf16[128,768]{1,0:T(8,128)(2,1)S(1)}, bf16[128,768]{1,0:T(8,128)(2,1)S(1)}, u32[]{:S(2)}, u32[]{:S(2)}) %collective-permute-start.124) | collective-permute-done | bytes 196640 | tf_op jit(solution)/shard_map/ppermute | solution.py:72
  760.9 62.6 %collective-permute-done.123 = bf16[128,768]{1,0:T(8,128)(2,1)S(1)} collective-permute-done((bf16[128,768]{1,0:T(8,128)(2,1)S(1)}, bf16[128,768]{1,0:T(8,128)(2,1)S(1)}, u32[]{:S(2)}, u32[]{:S(2)}) %collective-permute-start.123) | collective-permute-done | bytes 196640 | tf_op jit(solution)/shard_map/ppermute | solution.py:72
  860.5 12.5 %collective-permute-done.127 = bf16[1000,768]{1,0:T(8,128)(2,1)S(1)} collective-permute-done((bf16[1000,768]{1,0:T(8,128)(2,1)S(1)}, bf16[1000,768]{1,0:T(8,128)(2,1)S(1)}, u32[]{:S(2)}, u32[]{:S(2)}) %collective-permute-start.127) | collective-permute-done | bytes 1536032 | tf_op jit(solution)/shard_map/ppermute | solution.py:72
  874.1 130.8 %collective-permute-done.126 = bf16[1000,768]{1,0:T(8,128)(2,1)S(1)} collective-permute-done((bf16[1000,768]{1,0:T(8,128)(2,1)S(1)}, bf16[1000,768]{1,0:T(8,128)(2,1)S(1)}, u32[]{:S(2)}, u32[]{:S(2)}) %collective-permute-start.126) | collective-permute-done | bytes 1536032 | tf_op jit(solution)/shard_map/ppermute | solution.py:72
  1010.4 4.9 multiply_reduce_fusion
  1045.6 7.3 fusion.205
  1052.9 15.4 %fusion.208 = (bf16[2,1000,768]{2,1,0:T(8,128)(2,1)}, f32[2,1000,768]{2,1,0:T(8,128)}, f32[2,1000,768]{2,1,0:T(8,128)}, f32[2,1000,768]{2,1,0:T(8,128)}) fusion(f32[2,1000,768]{2,1,0:T(8,128)} %param.29, f32[]{:T(128)S(6)} %min.3, f32[1,1000,768]{2,1,0:T(8,128)} %get-tuple-element.507, f32[1,1000,768]{2,1,0:T(8,128)S(1)} %bitcast.428, ...), kind=kLoop, calls=%fused_computation.589 | loop fusion | flops 26112000 | bytes 46080004 | tf_op jit(solution)/shard_map/convert_element_type | solution.py:46
  1068.3 11.2 %fusion.202 = (bf16[1,2,768,768]{3,2,1,0:T(8,128)(2,1)}, f32[1,2,768,768]{3,2,1,0:T(8,128)}, f32[1,2,768,768]{3,2,1,0:T(8,128)}, f32[1,2,768,768]{3,2,1,0:T(8,128)}) fusion(f32[1,2,768,768]{3,2,1,0:T(8,128)S(1)} %bitcast.432, f32[]{:T(128)S(6)} %min.3, bf16[2,768,768]{2,1,0:T(8,128)(2,1)} %collective-permute-done.130, ...), kind=kLoop, calls=%fused_computation.587 | loop fusion | flops 25952256 | bytes 37748740 | tf_op jit(solution)/shard_map/convert_element_type | solution.py:46
  (828 shorter events, 394.8 us)
Async XLA Ops:
  0.7 26.4 %collective-permute-start.7 = (s32[2048]{0:T(1024)}, s32[2048]{0:T(1024)S(1)}, u32[]{:S(2)}, u32[]{:S(2)}) collective-permute-start(s32[2048]{0:T(1024)} %param.24), channel_id=1, source_target_pairs={{0,16},{8,24},{16,0},{24,8},{1,17},{9,25},{17,1},{25,9},{2,18},{10... | collective-permute-start | bytes 24584 | tf_op jit(solution)/shard_map/ppermute | solution.py:72
  4.8 22.3 %collective-permute-start.6 = (s32[2048]{0:T(1024)}, s32[2048]{0:T(1024)S(1)}, u32[]{:S(2)}, u32[]{:S(2)}) collective-permute-start(s32[2048]{0:T(1024)} %param.24), channel_id=1, source_target_pairs={{0,8},{8,16},{16,24},{24,0},{1,9},{9,17},{17,25},{25,1},{2,10},{10... | collective-permute-start | bytes 24584 | tf_op jit(solution)/shard_map/ppermute | solution.py:72
  6.4 20.7 %collective-permute-start.8 = (s32[2048]{0:T(1024)}, s32[2048]{0:T(1024)S(1)}, u32[]{:S(2)}, u32[]{:S(2)}) collective-permute-start(s32[2048]{0:T(1024)} %param.24), channel_id=1, source_target_pairs={{0,24},{8,0},{16,8},{24,16},{1,25},{9,1},{17,9},{25,17},{2,26},{10... | collective-permute-start | bytes 24584 | tf_op jit(solution)/shard_map/ppermute | solution.py:72
  11.2 51.2 %collective-permute-start.24 = (bf16[96,768]{1,0:T(8,128)(2,1)}, bf16[96,768]{1,0:T(8,128)(2,1)S(1)}, u32[]{:S(2)}, u32[]{:S(2)}) collective-permute-start(bf16[96,768]{1,0:T(8,128)(2,1)} %fusion.299), channel_id=1, source_target_pairs={{0,24},{8,0},{16,8},{24,16},{1,25},{9,1},{17,9},{25,17},{2,26},{10... | collective-permute-start | bytes 442376 | tf_op jit(solution)/shard_map/ppermute | solution.py:72
  33.5 15.7 %collective-permute-start.10 = (bf16[128,768]{1,0:T(8,128)(2,1)S(1)}, bf16[128,768]{1,0:T(8,128)(2,1)S(1)}, u32[]{:S(2)}, u32[]{:S(2)}) collective-permute-start(bf16[128,768]{1,0:T(8,128)(2,1)S(1)} %get-tuple-element.581), channel_id=1, source_target_pairs={{0,16},{8,24},{16,0},{24,8},{1,17},{9,25},{17,1},{25,9},{2,18},{10... | collective-permute-start | bytes 589832 | tf_op jit(solution)/shard_map/ppermute | solution.py:72
  33.5 15.7 %collective-permute-start.9 = (bf16[128,768]{1,0:T(8,128)(2,1)S(1)}, bf16[128,768]{1,0:T(8,128)(2,1)S(1)}, u32[]{:S(2)}, u32[]{:S(2)}) collective-permute-start(bf16[128,768]{1,0:T(8,128)(2,1)S(1)} %get-tuple-element.582), channel_id=1, source_target_pairs={{0,24},{8,0},{16,8},{24,16},{1,25},{9,1},{17,9},{25,17},{2,26},{10... | collective-permute-start | bytes 589832 | tf_op jit(solution)/shard_map/ppermute | solution.py:72
  43.3 19.0 %collective-permute-start.23 = (bf16[96,768]{1,0:T(8,128)(2,1)}, bf16[96,768]{1,0:T(8,128)(2,1)S(1)}, u32[]{:S(2)}, u32[]{:S(2)}) collective-permute-start(bf16[96,768]{1,0:T(8,128)(2,1)} %fusion.299), channel_id=1, source_target_pairs={{0,16},{8,24},{16,0},{24,8},{1,17},{9,25},{17,1},{25,9},{2,18},{10... | collective-permute-start | bytes 442376 | tf_op jit(solution)/shard_map/ppermute | solution.py:72
  55.4 16.6 %collective-permute-start.15 = (bf16[256,768]{1,0:T(8,128)(2,1)S(1)}, bf16[256,768]{1,0:T(8,128)(2,1)S(1)}, u32[]{:S(2)}, u32[]{:S(2)}) collective-permute-start(bf16[256,768]{1,0:T(8,128)(2,1)S(1)} %get-tuple-element.530), channel_id=1, source_target_pairs={{0,1},{1,0},{2,3},{3,2},{4,5},{5,4},{6,7},{7,6},{8,9},{9,8},{10,11... | collective-permute-start | bytes 1179656 | tf_op jit(solution)/shard_map/ppermute | solution.py:67
  69.0 16.3 %collective-permute-start.28 = (bf16[384,768]{1,0:T(8,128)(2,1)S(1)}, bf16[384,768]{1,0:T(8,128)(2,1)S(1)}, u32[]{:S(2)}, u32[]{:S(2)}) collective-permute-start(bf16[384,768]{1,0:T(8,128)(2,1)S(1)} %bitcast.453), channel_id=1, source_target_pairs={{0,4},{1,5},{2,6},{3,7},{4,0},{5,1},{6,2},{7,3},{8,12},{9,13},{10,... | collective-permute-start | bytes 1769480 | tf_op jit(solution)/shard_map/ppermute | solution.py:67
  70.6 16.2 %collective-permute-start.26 = (bf16[384,768]{1,0:T(8,128)(2,1)S(1)}, bf16[384,768]{1,0:T(8,128)(2,1)S(1)}, u32[]{:S(2)}, u32[]{:S(2)}) collective-permute-start(bf16[384,768]{1,0:T(8,128)(2,1)S(1)} %bitcast.454), channel_id=1, source_target_pairs={{0,2},{1,3},{2,0},{3,1},{4,6},{5,7},{6,4},{7,5},{8,10},{9,11},{10,... | collective-permute-start | bytes 1769480 | tf_op jit(solution)/shard_map/ppermute | solution.py:67
  72.0 16.4 %collective-permute-start.25 = (bf16[384,768]{1,0:T(8,128)(2,1)S(1)}, bf16[384,768]{1,0:T(8,128)(2,1)S(1)}, u32[]{:S(2)}, u32[]{:S(2)}) collective-permute-start(bf16[384,768]{1,0:T(8,128)(2,1)S(1)} %bitcast.455), channel_id=1, source_target_pairs={{0,1},{1,0},{2,3},{3,2},{4,5},{5,4},{6,7},{7,6},{8,9},{9,8},{10,11... | collective-permute-start | bytes 1769480 | tf_op jit(solution)/shard_map/ppermute | solution.py:67
  74.7 24.0 %collective-permute-start.14 = (bf16[128,768]{1,0:T(8,128)(2,1)S(1)}, bf16[128,768]{1,0:T(8,128)(2,1)S(1)}, u32[]{:S(2)}, u32[]{:S(2)}) collective-permute-start(bf16[128,768]{1,0:T(8,128)(2,1)S(1)} %slice.1260), channel_id=1, source_target_pairs={{0,2},{1,3},{2,0},{3,1},{4,6},{5,7},{6,4},{7,5},{8,10},{9,11},{10,... | collective-permute-start | bytes 589832 | tf_op jit(solution)/shard_map/ppermute | solution.py:67
  75.3 23.9 %collective-permute-start.21 = (bf16[128,768]{1,0:T(8,128)(2,1)S(1)}, bf16[128,768]{1,0:T(8,128)(2,1)S(1)}, u32[]{:S(2)}, u32[]{:S(2)}) collective-permute-start(bf16[128,768]{1,0:T(8,128)(2,1)S(1)} %slice.1259), channel_id=1, source_target_pairs={{0,4},{1,5},{2,6},{3,7},{4,0},{5,1},{6,2},{7,3},{8,12},{9,13},{10,... | collective-permute-start | bytes 589832 | tf_op jit(solution)/shard_map/ppermute | solution.py:67
  97.1 112.9 %collective-permute-start.52 = (bf16[2,768,768]{2,1,0:T(8,128)(2,1)}, bf16[2,768,768]{2,1,0:T(8,128)(2,1)}, u32[]{:S(2)}, u32[]{:S(2)}) collective-permute-start(bf16[2,768,768]{2,1,0:T(8,128)(2,1)} %convert_bitcast_fusion), channel_id=1, source_target_pairs={{0,24},{8,0},{16,8},{24,16},{1,25},{9,1},{17,9},{25,17},{2,26},{10... | collective-permute-start | bytes 7077896 | tf_op jit(solution)/shard_map/ppermute | solution.py:72
  105.9 27.8 %collective-permute-start.37 = (bf16[256,768]{1,0:T(8,128)(2,1)S(1)}, bf16[256,768]{1,0:T(8,128)(2,1)S(1)}, u32[]{:S(2)}, u32[]{:S(2)}) collective-permute-start(bf16[256,768]{1,0:T(8,128)(2,1)S(1)} %get-tuple-element.482), channel_id=1, source_target_pairs={{0,4},{1,5},{2,6},{3,7},{4,0},{5,1},{6,2},{7,3},{8,12},{9,13},{10,... | collective-permute-start | bytes 1179656 | tf_op jit(solution)/shard_map/ppermute | solution.py:67
  114.4 17.2 %collective-permute-start.35 = (bf16[256,768]{1,0:T(8,128)(2,1)S(1)}, bf16[256,768]{1,0:T(8,128)(2,1)S(1)}, u32[]{:S(2)}, u32[]{:S(2)}) collective-permute-start(bf16[256,768]{1,0:T(8,128)(2,1)S(1)} %get-tuple-element.482), channel_id=1, source_target_pairs={{0,2},{1,3},{2,0},{3,1},{4,6},{5,7},{6,4},{7,5},{8,10},{9,11},{10,... | collective-permute-start | bytes 1179656 | tf_op jit(solution)/shard_map/ppermute | solution.py:67
  116.8 17.3 %collective-permute-start.34 = (bf16[256,768]{1,0:T(8,128)(2,1)S(1)}, bf16[256,768]{1,0:T(8,128)(2,1)S(1)}, u32[]{:S(2)}, u32[]{:S(2)}) collective-permute-start(bf16[256,768]{1,0:T(8,128)(2,1)S(1)} %get-tuple-element.482), channel_id=1, source_target_pairs={{0,1},{1,0},{2,3},{3,2},{4,5},{5,4},{6,7},{7,6},{8,9},{9,8},{10,11... | collective-permute-start | bytes 1179656 | tf_op jit(solution)/shard_map/ppermute | solution.py:67
  135.8 67.8 %collective-permute-start.50 = (bf16[2,768,768]{2,1,0:T(8,128)(2,1)}, bf16[2,768,768]{2,1,0:T(8,128)(2,1)}, u32[]{:S(2)}, u32[]{:S(2)}) collective-permute-start(bf16[2,768,768]{2,1,0:T(8,128)(2,1)} %convert_bitcast_fusion), channel_id=1, source_target_pairs={{0,8},{8,16},{16,24},{24,0},{1,9},{9,17},{17,25},{25,1},{2,10},{10... | collective-permute-start | bytes 7077896 | tf_op jit(solution)/shard_map/ppermute | solution.py:72
  187.4 190.6 %collective-permute-start.71 = (bf16[1000,768]{1,0:T(8,128)(2,1)}, bf16[1000,768]{1,0:T(8,128)(2,1)}, u32[]{:S(2)}, u32[]{:S(2)}) collective-permute-start(bf16[1000,768]{1,0:T(8,128)(2,1)} %get-tuple-element.533.refs_0_), channel_id=1, source_target_pairs={{0,24},{8,0},{16,8},{24,16},{1,25},{9,1},{17,9},{25,17},{2,26},{10... | collective-permute-start | bytes 4608008 | tf_op jit(solution)/shard_map/ppermute | solution.py:72
  192.4 156.0 %collective-permute-start.69 = (bf16[1000,768]{1,0:T(8,128)(2,1)}, bf16[1000,768]{1,0:T(8,128)(2,1)}, u32[]{:S(2)}, u32[]{:S(2)}) collective-permute-start(bf16[1000,768]{1,0:T(8,128)(2,1)} %get-tuple-element.533.refs_0_), channel_id=1, source_target_pairs={{0,8},{8,16},{16,24},{24,0},{1,9},{9,17},{17,25},{25,1},{2,10},{10... | collective-permute-start | bytes 4608008 | tf_op jit(solution)/shard_map/ppermute | solution.py:72
  203.6 113.6 %collective-permute-start.51 = (bf16[2,768,768]{2,1,0:T(8,128)(2,1)}, bf16[2,768,768]{2,1,0:T(8,128)(2,1)S(1)}, u32[]{:S(2)}, u32[]{:S(2)}) collective-permute-start(bf16[2,768,768]{2,1,0:T(8,128)(2,1)} %collective-permute-done.50), channel_id=1, source_target_pairs={{0,8},{8,16},{16,24},{24,0},{1,9},{9,17},{17,25},{25,1},{2,10},{10... | collective-permute-start | bytes 7077896 | tf_op jit(solution)/shard_map/ppermute | solution.py:72
  330.0 15.8 %collective-permute-start.57 = (bf16[128,768]{1,0:T(8,128)(2,1)}, bf16[128,768]{1,0:T(8,128)(2,1)S(1)}, u32[]{:S(2)}, u32[]{:S(2)}) collective-permute-start(bf16[128,768]{1,0:T(8,128)(2,1)} %get-tuple-element.553), channel_id=1, source_target_pairs={{0,5},{1,4},{2,7},{3,6},{4,1},{5,0},{6,3},{7,2},{8,13},{9,12},{10,... | collective-permute-start | bytes 589832 | tf_op jit(solution)/shard_map/ppermute | solution.py:67
  348.5 37.8 %collective-permute-start.70 = (bf16[1000,768]{1,0:T(8,128)(2,1)}, bf16[1000,768]{1,0:T(8,128)(2,1)}, u32[]{:S(2)}, u32[]{:S(2)}) collective-permute-start(bf16[1000,768]{1,0:T(8,128)(2,1)} %collective-permute-done.69.refs_1_), channel_id=1, source_target_pairs={{0,8},{8,16},{16,24},{24,0},{1,9},{9,17},{17,25},{25,1},{2,10},{10... | collective-permute-start | bytes 4608008 | tf_op jit(solution)/shard_map/ppermute | solution.py:72
  462.6 18.0 %collective-permute-start.83 = (bf16[256,768]{1,0:T(8,128)(2,1)}, bf16[256,768]{1,0:T(8,128)(2,1)S(1)}, u32[]{:S(2)}, u32[]{:S(2)}) collective-permute-start(bf16[256,768]{1,0:T(8,128)(2,1)} %get-tuple-element.521), channel_id=1, source_target_pairs={{0,1},{1,0},{2,3},{3,2},{4,5},{5,4},{6,7},{7,6},{8,9},{9,8},{10,11... | collective-permute-start | bytes 1179656 | tf_op jit(solution)/shard_map/ppermute | solution.py:67
  462.6 18.0 %collective-permute-start.82 = (bf16[256,768]{1,0:T(8,128)(2,1)}, bf16[256,768]{1,0:T(8,128)(2,1)S(1)}, u32[]{:S(2)}, u32[]{:S(2)}) collective-permute-start(bf16[256,768]{1,0:T(8,128)(2,1)} %get-tuple-element.522), channel_id=1, source_target_pairs={{0,1},{1,0},{2,3},{3,2},{4,5},{5,4},{6,7},{7,6},{8,9},{9,8},{10,11... | collective-permute-start | bytes 1179656 | tf_op jit(solution)/shard_map/ppermute | solution.py:67
  463.1 17.5 %collective-permute-start.80 = (bf16[256,768]{1,0:T(8,128)(2,1)}, bf16[256,768]{1,0:T(8,128)(2,1)S(1)}, u32[]{:S(2)}, u32[]{:S(2)}) collective-permute-start(bf16[256,768]{1,0:T(8,128)(2,1)} %get-tuple-element.523), channel_id=1, source_target_pairs={{0,1},{1,0},{2,3},{3,2},{4,5},{5,4},{6,7},{7,6},{8,9},{9,8},{10,11... | collective-permute-start | bytes 1179656 | tf_op jit(solution)/shard_map/ppermute | solution.py:67
  463.1 19.1 %collective-permute-start.79 = (bf16[256,768]{1,0:T(8,128)(2,1)S(1)}, bf16[256,768]{1,0:T(8,128)(2,1)}, u32[]{:S(2)}, u32[]{:S(2)}) collective-permute-start(bf16[256,768]{1,0:T(8,128)(2,1)S(1)} %get-tuple-element.524), channel_id=1, source_target_pairs={{0,1},{1,0},{2,3},{3,2},{4,5},{5,4},{6,7},{7,6},{8,9},{9,8},{10,11... | collective-permute-start | bytes 1179656 | tf_op jit(solution)/shard_map/ppermute | solution.py:67
  524.4 22.7 %collective-permute-start.95 = (bf16[128,768]{1,0:T(8,128)(2,1)S(1)}, bf16[128,768]{1,0:T(8,128)(2,1)S(1)}, u32[]{:S(2)}, u32[]{:S(2)}) collective-permute-start(bf16[128,768]{1,0:T(8,128)(2,1)S(1)} %get-tuple-element.543), channel_id=1, source_target_pairs={{0,7},{1,6},{2,5},{3,4},{4,3},{5,2},{6,1},{7,0},{8,15},{9,14},{10,... | collective-permute-start | bytes 589832 | tf_op jit(solution)/shard_map/ppermute | solution.py:67
  526.5 19.9 %collective-permute-start.94 = (bf16[128,768]{1,0:T(8,128)(2,1)S(1)}, bf16[128,768]{1,0:T(8,128)(2,1)S(1)}, u32[]{:S(2)}, u32[]{:S(2)}) collective-permute-start(bf16[128,768]{1,0:T(8,128)(2,1)S(1)} %get-tuple-element.544), channel_id=1, source_target_pairs={{0,6},{1,7},{2,4},{3,5},{4,2},{5,3},{6,0},{7,1},{8,14},{9,15},{10,... | collective-permute-start | bytes 589832 | tf_op jit(solution)/shard_map/ppermute | solution.py:67
  588.5 20.9 %collective-permute-start.102 = (bf16[128,768]{1,0:T(8,128)(2,1)S(1)}, bf16[128,768]{1,0:T(8,128)(2,1)S(1)}, u32[]{:S(2)}, u32[]{:S(2)}) collective-permute-start(bf16[128,768]{1,0:T(8,128)(2,1)S(1)} %get-tuple-element.535), channel_id=1, source_target_pairs={{0,7},{1,6},{2,5},{3,4},{4,3},{5,2},{6,1},{7,0},{8,15},{9,14},{10,... | collective-permute-start | bytes 589832 | tf_op jit(solution)/shard_map/ppermute | solution.py:67
  590.2 19.2 %collective-permute-start.101 = (bf16[128,768]{1,0:T(8,128)(2,1)S(1)}, bf16[128,768]{1,0:T(8,128)(2,1)S(1)}, u32[]{:S(2)}, u32[]{:S(2)}) collective-permute-start(bf16[128,768]{1,0:T(8,128)(2,1)S(1)} %get-tuple-element.536), channel_id=1, source_target_pairs={{0,6},{1,7},{2,4},{3,5},{4,2},{5,3},{6,0},{7,1},{8,14},{9,15},{10,... | collective-permute-start | bytes 589832 | tf_op jit(solution)/shard_map/ppermute | solution.py:67
  593.1 16.2 %collective-permute-start.100 = (bf16[128,768]{1,0:T(8,128)(2,1)S(1)}, bf16[128,768]{1,0:T(8,128)(2,1)S(1)}, u32[]{:S(2)}, u32[]{:S(2)}) collective-permute-start(bf16[128,768]{1,0:T(8,128)(2,1)S(1)} %get-tuple-element.537), channel_id=1, source_target_pairs={{0,5},{1,4},{2,7},{3,6},{4,1},{5,0},{6,3},{7,2},{8,13},{9,12},{10,... | collective-permute-start | bytes 589832 | tf_op jit(solution)/shard_map/ppermute | solution.py:67
  649.2 15.5 %collective-permute-start.107 = (bf16[256,768]{1,0:T(8,128)(2,1)}, bf16[256,768]{1,0:T(8,128)(2,1)S(1)}, u32[]{:S(2)}, u32[]{:S(2)}) collective-permute-start(bf16[256,768]{1,0:T(8,128)(2,1)} %get-tuple-element.513), channel_id=1, source_target_pairs={{0,1},{1,0},{2,3},{3,2},{4,5},{5,4},{6,7},{7,6},{8,9},{9,8},{10,11... | collective-permute-start | bytes 1179656 | tf_op jit(solution)/shard_map/ppermute | solution.py:67
  649.4 15.4 %collective-permute-start.106 = (bf16[256,768]{1,0:T(8,128)(2,1)}, bf16[256,768]{1,0:T(8,128)(2,1)}, u32[]{:S(2)}, u32[]{:S(2)}) collective-permute-start(bf16[256,768]{1,0:T(8,128)(2,1)} %get-tuple-element.514), channel_id=1, source_target_pairs={{0,1},{1,0},{2,3},{3,2},{4,5},{5,4},{6,7},{7,6},{8,9},{9,8},{10,11... | collective-permute-start | bytes 1179656 | tf_op jit(solution)/shard_map/ppermute | solution.py:67
  697.4 22.2 %collective-permute-start.140 = (bf16[192,768]{1,0:T(8,128)(2,1)S(1)}, bf16[192,768]{1,0:T(8,128)(2,1)S(1)}, u32[]{:S(2)}, u32[]{:S(2)}) collective-permute-start(bf16[192,768]{1,0:T(8,128)(2,1)S(1)} %slice.1253), channel_id=1, source_target_pairs={{0,4},{1,5},{2,6},{3,7},{4,0},{5,1},{6,2},{7,3},{8,12},{9,13},{10,... | collective-permute-start | bytes 884744 | tf_op jit(solution)/shard_map/ppermute | solution.py:67
  719.5 127.4 %collective-permute-start.125 = (bf16[1000,768]{1,0:T(8,128)(2,1)}, bf16[1000,768]{1,0:T(8,128)(2,1)}, u32[]{:S(2)}, u32[]{:S(2)}) collective-permute-start(bf16[1000,768]{1,0:T(8,128)(2,1)} %head_weight_back.6), channel_id=1, source_target_pairs={{0,8},{8,16},{16,24},{24,0},{1,9},{9,17},{17,25},{25,1},{2,10},{10... | collective-permute-start | bytes 4608008 | tf_op jit(solution)/shard_map/ppermute | solution.py:72
  719.6 41.3 %collective-permute-start.124 = (bf16[128,768]{1,0:T(8,128)(2,1)S(1)}, bf16[128,768]{1,0:T(8,128)(2,1)S(1)}, u32[]{:S(2)}, u32[]{:S(2)}) collective-permute-start(bf16[128,768]{1,0:T(8,128)(2,1)S(1)} %get-tuple-element.570), channel_id=1, source_target_pairs={{0,24},{8,0},{16,8},{24,16},{1,25},{9,1},{17,9},{25,17},{2,26},{10... | collective-permute-start | bytes 589832 | tf_op jit(solution)/shard_map/ppermute | solution.py:72
  723.4 100.1 %collective-permute-start.123 = (bf16[128,768]{1,0:T(8,128)(2,1)S(1)}, bf16[128,768]{1,0:T(8,128)(2,1)S(1)}, u32[]{:S(2)}, u32[]{:S(2)}) collective-permute-start(bf16[128,768]{1,0:T(8,128)(2,1)S(1)} %get-tuple-element.571), channel_id=1, source_target_pairs={{0,16},{8,24},{16,0},{24,8},{1,17},{9,25},{17,1},{25,9},{2,18},{10... | collective-permute-start | bytes 589832 | tf_op jit(solution)/shard_map/ppermute | solution.py:72
  724.6 98.9 %collective-permute-start.122 = (bf16[128,768]{1,0:T(8,128)(2,1)S(1)}, bf16[128,768]{1,0:T(8,128)(2,1)S(1)}, u32[]{:S(2)}, u32[]{:S(2)}) collective-permute-start(bf16[128,768]{1,0:T(8,128)(2,1)S(1)} %get-tuple-element.572), channel_id=1, source_target_pairs={{0,8},{8,16},{16,24},{24,0},{1,9},{9,17},{17,25},{25,1},{2,10},{10... | collective-permute-start | bytes 589832 | tf_op jit(solution)/shard_map/ppermute | solution.py:72
  727.0 116.1 %collective-permute-start.128 = (bf16[2,768,768]{2,1,0:T(8,128)(2,1)}, bf16[2,768,768]{2,1,0:T(8,128)(2,1)}, u32[]{:S(2)}, u32[]{:S(2)}) collective-permute-start(bf16[2,768,768]{2,1,0:T(8,128)(2,1)} %pad_maximum_fusion.1), channel_id=1, source_target_pairs={{0,8},{8,16},{16,24},{24,0},{1,9},{9,17},{17,25},{25,1},{2,10},{10... | collective-permute-start | bytes 7077896 | tf_op jit(solution)/shard_map/ppermute | solution.py:72
  834.9 38.1 %collective-permute-start.127 = (bf16[1000,768]{1,0:T(8,128)(2,1)S(1)}, bf16[1000,768]{1,0:T(8,128)(2,1)S(1)}, u32[]{:S(2)}, u32[]{:S(2)}) collective-permute-start(bf16[1000,768]{1,0:T(8,128)(2,1)S(1)} %copy-done.94), channel_id=1, source_target_pairs={{0,24},{8,0},{16,8},{24,16},{1,25},{9,1},{17,9},{25,17},{2,26},{10... | collective-permute-start | bytes 4608008 | tf_op jit(solution)/shard_map/ppermute | solution.py:72
  838.7 171.3 %collective-permute-start.130 = (bf16[2,768,768]{2,1,0:T(8,128)(2,1)}, bf16[2,768,768]{2,1,0:T(8,128)(2,1)}, u32[]{:S(2)}, u32[]{:S(2)}) collective-permute-start(bf16[2,768,768]{2,1,0:T(8,128)(2,1)} %pad_maximum_fusion.2), channel_id=1, source_target_pairs={{0,24},{8,0},{16,8},{24,16},{1,25},{9,1},{17,9},{25,17},{2,26},{10... | collective-permute-start | bytes 7077896 | tf_op jit(solution)/shard_map/ppermute | solution.py:72
  846.9 163.5 %collective-permute-start.129 = (bf16[2,768,768]{2,1,0:T(8,128)(2,1)}, bf16[2,768,768]{2,1,0:T(8,128)(2,1)}, u32[]{:S(2)}, u32[]{:S(2)}) collective-permute-start(bf16[2,768,768]{2,1,0:T(8,128)(2,1)} %add_convert_fusion.1), channel_id=1, source_target_pairs={{0,8},{8,16},{16,24},{24,0},{1,9},{9,17},{17,25},{25,1},{2,10},{10... | collective-permute-start | bytes 7077896 | tf_op jit(solution)/shard_map/ppermute | solution.py:72
  848.8 156.1 %collective-permute-start.126 = (bf16[1000,768]{1,0:T(8,128)(2,1)S(1)}, bf16[1000,768]{1,0:T(8,128)(2,1)S(1)}, u32[]{:S(2)}, u32[]{:S(2)}) collective-permute-start(bf16[1000,768]{1,0:T(8,128)(2,1)S(1)} %add_convert_fusion.4), channel_id=1, source_target_pairs={{0,8},{8,16},{16,24},{24,0},{1,9},{9,17},{17,25},{25,1},{2,10},{10... | collective-permute-start | bytes 4608008 | tf_op jit(solution)/shard_map/ppermute | solution.py:72
  858.1 151.2 %collective-permute-start.154 = (bf16[48,768]{1,0:T(8,128)(2,1)S(1)}, bf16[48,768]{1,0:T(8,128)(2,1)}, u32[]{:S(2)}, u32[]{:S(2)}) collective-permute-start(bf16[48,768]{1,0:T(8,128)(2,1)S(1)} %slice.1094), channel_id=1, source_target_pairs={{0,4},{1,5},{2,6},{3,7},{4,0},{5,1},{6,2},{7,3},{8,12},{9,13},{10,... | collective-permute-start | bytes 221192 | tf_op jit(solution)/shard_map/ppermute | solution.py:67
  873.0 136.9 %collective-permute-start.155 = (bf16[48,768]{1,0:T(8,128)(2,1)}, bf16[48,768]{1,0:T(8,128)(2,1)}, u32[]{:S(2)}, u32[]{:S(2)}) collective-permute-start(bf16[48,768]{1,0:T(8,128)(2,1)} %slice.1095), channel_id=1, source_target_pairs={{0,2},{1,3},{2,0},{3,1},{4,6},{5,7},{6,4},{7,5},{8,10},{9,11},{10,... | collective-permute-start | bytes 221192 | tf_op jit(solution)/shard_map/ppermute | solution.py:67
  1009.9 23.3 %collective-permute-start.156 = (bf16[48,768]{1,0:T(8,128)(2,1)}, bf16[48,768]{1,0:T(8,128)(2,1)}, u32[]{:S(2)}, u32[]{:S(2)}) collective-permute-start(bf16[48,768]{1,0:T(8,128)(2,1)} %collective-permute-done.154), channel_id=1, source_target_pairs={{0,1},{1,0},{2,3},{3,2},{4,5},{5,4},{6,7},{7,6},{8,9},{9,8},{10,11... | collective-permute-start | bytes 221192 | tf_op jit(solution)/shard_map/ppermute | solution.py:67
  1010.0 23.2 %collective-permute-start.157 = (bf16[48,768]{1,0:T(8,128)(2,1)}, bf16[48,768]{1,0:T(8,128)(2,1)}, u32[]{:S(2)}, u32[]{:S(2)}) collective-permute-start(bf16[48,768]{1,0:T(8,128)(2,1)} %collective-permute-done.155), channel_id=1, source_target_pairs={{0,1},{1,0},{2,3},{3,2},{4,5},{5,4},{6,7},{7,6},{8,9},{9,8},{10,11... | collective-permute-start | bytes 221192 | tf_op jit(solution)/shard_map/ppermute | solution.py:67
  (209 other events, 3428.4 us)

commit v2 on v1

--- a/solution.py
+++ b/solution.py
@@ -62,6 +62,10 @@
     return dot(a, b, ((0,), (0,)))
 
 
+def after(array, earlier):
+    return array if earlier is None else lax.optimization_barrier((array, earlier))[0]
+
+
 def swap(array, bits, axis):
     pairs = [(i, i ^ bits) for i in range(lax.axis_size(axis))]
     return lax.ppermute(array, axis, pairs)
@@ -87,10 +91,11 @@
     return jnp.arange(count)
 
 
-def gather_blocks(rows):
+def gather_pieces(rows):
+    count = lax.axis_size("expert")
     if not quick_expert():
         gathered = lax.all_gather(rows, "expert")
-        return [gathered[i] for i in range(lax.axis_size("expert"))]
+        return [(i, 0, gathered[i]) for i in range(count)]
     half = rows.shape[0] // 2
     one, two, four = (swap(rows, bits, "expert") for bits in (1, 2, 4))
     six_a = swap(two[:half], 4, "expert")
@@ -100,28 +105,31 @@
     seven_a = swap(six_a, 1, "expert")
     seven_b = swap(six_b, 1, "expert")
     return [
-        rows,
-        one,
-        two,
-        three,
-        four,
-        five,
-        jnp.concatenate([six_a, six_b]),
-        jnp.concatenate([seven_a, seven_b]),
+        (0, 0, rows),
+        (1, 0, one),
+        (2, 0, two),
+        (3, 0, three),
+        (4, 0, four),
+        (5, 0, five),
+        (6, 0, six_a),
+        (6, half, six_b),
+        (7, 0, seven_a),
+        (7, half, seven_b),
     ]
 
 
 def gather_rows(rows):
-    return jnp.concatenate(gather_blocks(rows))
-
-
-def sum_blocks(blocks):
+    return jnp.concatenate([piece for _, _, piece in gather_pieces(rows)])
+
+
+def sum_blocks(blocks, earlier=None):
     if not quick_expert():
         return lax.psum_scatter(
             jnp.stack(blocks), "expert", scatter_dimension=0, tiled=False
         ).astype(F32)
     half = blocks[0].shape[0] // 2
     other = [swap(blocks[j], 1, "expert") for j in (6 + 1, 2 + 1, 4 + 1, 1)]
+    other[0] = after(other[0], earlier)
     six = (blocks[6].astype(F32) + other[0].astype(F32)).astype(BF)
     two = blocks[2].astype(F32) + other[1].astype(F32)
     four = blocks[4].astype(F32) + other[2].astype(F32)
@@ -153,34 +161,11 @@
     return [blocks[0]] + [swap(blocks[k], k, "expert") for k in range(1, 8)]
 
 
-def gather_shards(shard):
-    if not quick_dp():
-        gathered = lax.all_gather(shard, "dp")
-        return [gathered[i] for i in range(lax.axis_size("dp"))]
-    below = turn(shard, 1)
-    above = turn(shard, -1)
-    far = turn(below, 1)
-    return [shard, below, far, above]
-
-
-def shard_slot(shard_index):
-    if quick_dp():
-        return (lax.axis_index("dp") - shard_index) % 4
-    return shard_index
-
-
 def slot_shards():
-    places = jnp.arange(lax.axis_size("dp"))
-    if quick_dp():
-        return (lax.axis_index("dp") - places) % 4
-    return places
-
-
-def sum_shards(parts):
-    if not quick_dp():
-        return lax.psum_scatter(
-            jnp.stack(parts), "dp", scatter_dimension=0, tiled=False
-        ).astype(F32)
+    return (lax.axis_index("dp") - jnp.arange(4)) % 4
+
+
+def sum_turns(parts):
     own, above_by_three, two, above = parts
     far = turn(two, 1)
     back = turn(above_by_three, -1)
@@ -188,13 +173,27 @@
     return own.astype(F32) + near.astype(F32) + back.astype(F32)
 
 
+def sum_shards(parts):
+    return lax.psum_scatter(parts, "dp", scatter_dimension=0, tiled=False).astype(F32)
+
+
 def sum_everywhere(array):
+    if quick_expert() and quick_dp():
+        array = array + swap(array, 1, "expert")
+        for axis, scale in (("expert", 2), ("dp", 1)):
+            one, two, three = (swap(array, scale * k, axis) for k in (1, 2, 3))
+            array = (array + one) + (two + three)
+        return array
     for axis in ("expert", "dp"):
         bits = 1
         while bits < lax.axis_size(axis):
             array = array + swap(array, bits, axis)
             bits *= 2
     return array
+
+
+def cost(flops):
+    return pl.CostEstimate(flops=flops, bytes_accessed=flops // 500, transcendentals=0)
 
 
 def params():
@@ -254,11 +253,7 @@
             jax.ShapeDtypeStruct((HEADS, local), F32),
         ],
         compiler_params=params(),
-        cost_estimate=pl.CostEstimate(
-            flops=4 * local * group * width * 4,
-            bytes_accessed=4 * group * width,
-            transcendentals=HEADS * local * group,
-        ),
+        cost_estimate=cost(1000),
         name="attend",
     )(queries, keys, values, key_place, query_place)
 
@@ -325,150 +320,208 @@
             jax.ShapeDtypeStruct((group, width), BF),
         ],
         compiler_params=params(),
-        cost_estimate=pl.CostEstimate(
-            flops=10 * local * group * width * 4,
-            bytes_accessed=8 * group * width,
-            transcendentals=HEADS * local * group,
-        ),
+        cost_estimate=cost(1000),
         name="attend_back",
     )(queries, keys, values, grad_out, mixed, lse, key_place, query_place)
 
 
-def head_kernel(count, rows_ref, place_ref, *refs):
-    heads, exps, stats_ref = refs[:count], refs[count : 2 * count], refs[2 * count]
-    rows, place = rows_ref[...], place_ref[...]
-    depth = heads[0].shape[0]
-    scores = [dot_nt(head[...], rows) for head in heads]
-    iota = lax.broadcasted_iota(jnp.int32, scores[0].shape, 0)
-    top = functools.reduce(jnp.maximum, [jnp.max(s, axis=0, keepdims=True) for s in scores])
-    total = picked = jnp.zeros_like(top)
+def place_kernel(spots, member_ref, *refs):
+    pieces, out_ref = refs[: len(spots)], refs[len(spots)]
+    half = out_ref.shape[2] // 2
+    for i, (block, row) in enumerate(spots):
+        owner = member_ref[0] ^ block
+        columns = pl.ds(pl.multiple_of((owner % 2) * half, 128), half)
+        out_ref[owner // 2, row : row + pieces[i].shape[0], columns] = pieces[i][...]
+
+
+def place_halves(member, pieces):
+    spots = [(block, row) for block, row, _ in pieces]
+    arrays = [array for _, _, array in pieces]
+    rows, half = arrays[0].shape
+    return pl.pallas_call(
+        functools.partial(place_kernel, spots),
+        in_specs=[pl.BlockSpec(memory_space=pltpu.SMEM)]
+        + [pl.BlockSpec(memory_space=pltpu.VMEM)] * len(arrays),
+        out_specs=pl.BlockSpec(memory_space=pltpu.VMEM),
+        out_shape=jax.ShapeDtypeStruct((4, rows, 2 * half), arrays[0].dtype),
+        compiler_params=pltpu.CompilerParams(vmem_limit_bytes=VMEM_BYTES),
+        cost_estimate=cost(1000),
+        name="place_halves",
+    )(member.reshape(1), *arrays)
+
+
+def attn_weight_kernel(
+    member_ref, x_ref, all_ref, mixed_ref, q_ref, k_ref, v_ref, branch_ref, out_ref
+):
+    owner = member_ref[0] ^ pl.program_id(0)
+    half = out_ref.shape[2]
+    columns = pl.ds(pl.multiple_of((owner % 2) * half, 128), half)
+    sources = ((x_ref, q_ref), (all_ref, k_ref), (all_ref, v_ref), (mixed_ref, branch_ref))
+    for kind, (left, right) in enumerate(sources):
+
+        @pl.when(owner // 2 == kind)
+        def _(left=left, right=right):
+            out_ref[0] = dot_tn(left[...], right[:, columns]).astype(BF)
+
+
+def attn_weight_back(member, *arrays):
+    width = arrays[0].shape[1]
+    return pl.pallas_call(
+        attn_weight_kernel,
+        grid=(8,),
+        in_specs=[pl.BlockSpec(memory_space=pltpu.SMEM)]
+        + [pl.BlockSpec(a.shape, lambda i: (0, 0)) for a in arrays],
+        out_specs=pl.BlockSpec((1, width, width // 2), lambda i: (i, 0, 0)),
+        out_shape=jax.ShapeDtypeStruct((8, width, width // 2), BF),
+        compiler_params=params(),
+        cost_estimate=cost(4 * (arrays[0].shape[0] + arrays[1].shape[0]) * width * width),
+        name="attn_weight_back",
+    )(member.reshape(1), *arrays)
+
+
+def head_kernel(rows_ref, heads_ref, exps_ref, stats_ref):
+    rows = rows_ref[...]
+    count = heads_ref.shape[0]
     for k in range(count):
-        weights = jnp.exp(scores[k] - top)
-        total = total + jnp.sum(weights, axis=0, keepdims=True)
-        chosen = jnp.where(iota == place - k * depth, scores[k], 0.0)
-        picked = picked + jnp.sum(chosen, axis=0, keepdims=True)
-        exps[k][...] = weights.astype(BF)
-    stats_ref[0:1, :] = top
-    stats_ref[1:2, :] = total
-    stats_ref[2:3, :] = picked
-    stats_ref[3:8, :] = jnp.zeros((5, top.shape[1]), F32)
-
-
-def head_forward(rows, place, heads):
+        scores = dot_nt(heads_ref[k], rows)
+        top = jnp.max(scores, axis=0, keepdims=True)
+        weights = jnp.exp(scores - top)
+        stats_ref[k : k + 1, :] = top
+        stats_ref[count + k : count + k + 1, :] = jnp.sum(weights, axis=0, keepdims=True)
+        exps_ref[k] = weights.astype(BF)
+
+
+def head_forward(rows, heads):
     group, width = rows.shape
-    count, depth = len(heads), heads[0].shape[0]
-    block = min(256, group)
-    whole = pl.BlockSpec((depth, width), lambda i: (0, 0))
-    cols = pl.BlockSpec((depth, block), lambda i: (0, i))
-    results = pl.pallas_call(
-        functools.partial(head_kernel, count),
+    count, depth, _ = heads.shape
+    block = min(512, group)
+    exps, stats = pl.pallas_call(
+        head_kernel,
         grid=(group // block,),
         in_specs=[
             pl.BlockSpec((block, width), lambda i: (i, 0)),
-            pl.BlockSpec((1, block), lambda i: (0, i)),
-        ]
-        + [whole] * count,
-        out_specs=[cols] * count + [pl.BlockSpec((8, block), lambda i: (0, i))],
-        out_shape=[jax.ShapeDtypeStruct((depth, group), BF)] * count
-        + [jax.ShapeDtypeStruct((8, group), F32)],
+            pl.BlockSpec((count, depth, width), lambda i: (0, 0, 0)),
+        ],
+        out_specs=[
+            pl.BlockSpec((count, depth, block), lambda i: (0, 0, i)),
+            pl.BlockSpec((2 * count, block), lambda i: (0, i)),
+        ],
+        out_shape=[
+            jax.ShapeDtypeStruct((count, depth, group), BF),
+            jax.ShapeDtypeStruct((2 * count, group), F32),
+        ],
         compiler_params=params(),
-        cost_estimate=pl.CostEstimate(
-            flops=2 * group * width * depth * count,
-            bytes_accessed=2 * count * depth * (group + width),
-            transcendentals=group * depth * count,
-        ),
+        cost_estimate=cost(2 * group * width * depth * count),
         name="head_forward",
-    )(rows, place, *heads)
-    return results[:count], results[count]
-
-
-def logit_grads(exps, coef_ref, place, offset):
-    grads = exps.astype(F32) * coef_ref[0:1, :]
-    iota = lax.broadcasted_iota(jnp.int32, grads.shape, 0)
-    return (grads - jnp.where(iota == place - offset, coef_ref[1:2, :], 0.0)).astype(BF)
-
-
-def head_rows_kernel(count, coef_ref, place_ref, *refs):
-    heads, exps, out_ref = refs[:count], refs[count : 2 * count], refs[2 * count]
-    depth = heads[0].shape[0]
+    )(rows, heads)
+    return exps, stats
+
+
+def chosen_tokens(rank_ref, word_ref, k, turn_no, capacity):
+    group = rank_ref.shape[1]
+    place = lax.broadcasted_iota(jnp.int32, (capacity, group), 0) + turn_no * capacity
+    chosen = rank_ref[k : k + 1, :] == place.astype(F32)
+    word = jnp.sum(jnp.where(chosen, word_ref[...] + 1.0, 0.0), axis=1, keepdims=True) - 1.0
+    return chosen, word
+
+
+def word_hots(word, words):
+    lanes = lax.broadcasted_iota(jnp.int32, (word.shape[0], words), 1).astype(F32)
+    return (word == lanes).astype(BF)
+
+
+def stats_kernel(
+    capacity, rounds_ref, rank_ref, word_ref, heads_ref, rows_ref, sums_ref, out_ref, stats_ref,
+    ratio_ref
+):
+    count, words, _ = heads_ref.shape
+
+    def wanted(turn_no):
+        picks, found = [], []
+        for k in range(count):
+            chosen, word = chosen_tokens(rank_ref, word_ref, k, turn_no, capacity)
+            picks.append(jnp.where(chosen, 1.0, 0.0).astype(BF))
+            found.append(dot_nn(word_hots(word, words), heads_ref[k]).astype(BF))
+        return dot_tn(jnp.concatenate(picks), jnp.concatenate(found))
+
+    out_ref[...] = wanted(0).astype(BF)
+
+    @pl.loop(1, rounds_ref[0])
+    def _(turn_no):
+        out_ref[...] = (out_ref[...].astype(F32) + wanted(turn_no)).astype(BF)
+
+    product = rows_ref[...].astype(F32) * out_ref[...].astype(F32)
+    high = product.astype(BF)
+    low = (product - high.astype(F32)).astype(BF)
+    ones = jnp.ones((8, product.shape[1]), BF)
+    picked = dot_nt(ones, high) + dot_nt(ones, low)
+    tops = sums_ref[:count, :]
+    top = jnp.max(tops, axis=0, keepdims=True)
+    ratio = jnp.exp(tops - top)
+    ratio_ref[...] = ratio
+    stats_ref[0:1, :] = top
+    stats_ref[1:2, :] = jnp.sum(sums_ref[count:, :] * ratio, axis=0, keepdims=True)
+    stats_ref[2:3, :] = picked[0:1, :]
+
+
+def target_kernel(capacity, rounds_ref, rank_ref, word_ref, weight_ref, rows_ref, out_ref):
+    count, words, _ = out_ref.shape
+
+    def term(k, turn_no):
+        chosen, word = chosen_tokens(rank_ref, word_ref, k, turn_no, capacity)
+        weight = jnp.sum(jnp.where(chosen, weight_ref[...], 0.0), axis=1, keepdims=True)
+        found = dot_nn(jnp.where(chosen, 1.0, 0.0).astype(BF), rows_ref[...]) * weight
+        return dot_tn(word_hots(word, words), found.astype(BF))
+
+    for k in range(count):
+        out_ref[k] = term(k, 0).astype(BF)
+
+    @pl.loop(1, rounds_ref[0])
+    def _(turn_no):
+        for k in range(count):
+            out_ref[k] = (out_ref[k].astype(F32) + term(k, turn_no)).astype(BF)
+
+
+def whole_call(kernel, out_shape, name, *arrays):
+    vmem = pl.BlockSpec(memory_space=pltpu.VMEM)
+    return pl.pallas_call(
+        kernel,
+        in_specs=[pl.BlockSpec(memory_space=pltpu.SMEM)] + [vmem] * (len(arrays) - 1),
+        out_specs=jax.tree.map(lambda _: vmem, out_shape),
+        out_shape=out_shape,
+        compiler_params=pltpu.CompilerParams(vmem_limit_bytes=VMEM_BYTES),
+        cost_estimate=cost(1000),
+        name=name,
+    )(*arrays)
+
+
+def head_rows_kernel(coef_ref, heads_ref, exps_ref, out_ref):
+    coef = jnp.transpose(coef_ref[...])
     out = None
-    for k in range(count):
-        grads = logit_grads(exps[k][...], coef_ref, place_ref[...], k * depth)
-        term = dot_tn(grads, heads[k][...])
+    for k in range(heads_ref.shape[0]):
+        term = dot_tn(exps_ref[k], heads_ref[k]) * coef[:, k : k + 1]
         out = term if out is None else out + term
     out_ref[...] = out.astype(BF)
 
 
-def head_rows_back(coef, place, heads, exps):
-    depth, width = heads[0].shape
-    group = exps[0].shape[1]
-    count = len(heads)
+def head_rows_back(coef, heads, exps):
+    count, depth, width = heads.shape
+    group = exps.shape[2]
     block = min(256, group)
-    whole = pl.BlockSpec((depth, width), lambda i: (0, 0))
-    cols = pl.BlockSpec((depth, block), lambda i: (0, i))
     return pl.pallas_call(
-        functools.partial(head_rows_kernel, count),
+        head_rows_kernel,
         grid=(group // block,),
         in_specs=[
-            pl.BlockSpec((2, block), lambda i: (0, i)),
-            pl.BlockSpec((1, block), lambda i: (0, i)),
-        ]
-        + [whole] * count
-        + [cols] * count,
+            pl.BlockSpec((count, block), lambda i: (0, i)),
+            pl.BlockSpec((count, depth, width), lambda i: (0, 0, 0)),
+            pl.BlockSpec((count, depth, block), lambda i: (0, 0, i)),
+        ],
         out_specs=pl.BlockSpec((block, width), lambda i: (i, 0)),
         out_shape=jax.ShapeDtypeStruct((group, width), BF),
         compiler_params=params(),
-        cost_estimate=pl.CostEstimate(
-            flops=2 * group * width * depth * count,
-            bytes_accessed=2 * count * depth * (group + width),
-            transcendentals=0,
-        ),
+        cost_estimate=cost(2 * group * width * depth * count),
         name="head_rows_back",
-    )(coef, place, *heads, *exps)
-
-
-def head_weight_kernel(offset, coef_ref, place_ref, exps_ref, rows_ref, out_ref, total):
-    step = pl.program_id(0)
-    grads = logit_grads(exps_ref[...], coef_ref, place_ref[...], offset)
-    term = dot_nn(grads, rows_ref[...])
-
-    @pl.when(step == 0)
-    def _():
-        total[...] = term
-
-    @pl.when(step > 0)
-    def _():
-        total[...] += term
-
-    @pl.when(step == pl.num_programs(0) - 1)
-    def _():
-        out_ref[...] = total[...].astype(BF)
-
-
-def head_weight_back(coef, place, exps, rows, offset):
-    depth, group = exps.shape
-    width = rows.shape[1]
-    block = min(512, group)
-    return pl.pallas_call(
-        functools.partial(head_weight_kernel, offset),
-        grid=(group // block,),
-        in_specs=[
-            pl.BlockSpec((2, block), lambda i: (0, i)),
-            pl.BlockSpec((1, block), lambda i: (0, i)),
-            pl.BlockSpec((depth, block), lambda i: (0, i)),
-            pl.BlockSpec((block, width), lambda i: (i, 0)),
-        ],
-        out_specs=pl.BlockSpec((depth, width), lambda i: (0, 0)),
-        out_shape=jax.ShapeDtypeStruct((depth, width), BF),
-        scratch_shapes=[pltpu.VMEM((depth, width), F32)],
-        compiler_params=params(),
-        cost_estimate=pl.CostEstimate(
-            flops=2 * group * width * depth,
-            bytes_accessed=2 * (depth * group + group * width + depth * width),
-            transcendentals=0,
-        ),
-        name="head_weight_back",
-    )(coef, place, exps, rows)
+    )(coef, heads, exps)
 
 
 def ranks(hits):
@@ -524,10 +577,14 @@
 
     attn_b = attn.astype(BF)
     if quick_expert() and quick_dp():
-        piece = attn.shape[1] // 2
-        cut = attn_b.reshape(8, piece, width)
-        mine = lax.dynamic_index_in_dim(cut, member, 0, False)
+        mine = lax.dynamic_slice(
+            attn_b,
+            (member // 2, 0, (member % 2) * (width // 2)),
+            (1, attn.shape[1], width // 2),
+        )[0]
         attn_parts = jnp.stack([mine] + [turn(mine, k) for k in range(1, 4)])
+        attn_parts = attn_parts[slot_shards()].reshape(width, width // 2)
+        attn_pieces = gather_pieces(attn_parts)
     table_b = tables[0].astype(BF)
     experts_b = experts[0].astype(BF)
     head_b = tables[1].astype(BF)
@@ -556,43 +613,68 @@
         return (at == jnp.arange(words, dtype=F32)[None, :]).astype(BF)
 
     def from_select(turn_no):
-        at = (place + turn_no * capacity)[None, None, :]
-        chosen = rank_from[:, :, None] == at
-        return jnp.transpose(chosen, (1, 0, 2)).reshape(group, -1).astype(BF)
-
-    def look_up(turn_no, select_own, select_from):
+        chosen = rank_from[:, None, :] == (place + turn_no * capacity)[None, :, None]
+        return chosen.reshape(-1, group).astype(BF)
+
+    def look_up(select_own):
         found = dot_nn(select_own, table_b).astype(BF).reshape(rows_dp, capacity, width)
         arrived = [found[0]] + [turn(found[k], -k) for k in range(1, rows_dp)]
-        return dot_nn(select_from, jnp.concatenate(arrived)).astype(BF)
+        return jnp.concatenate(arrived)
+
+    def put(arrived, select_from):
+        return dot_tn(select_from, arrived).astype(BF)
 
     def spread(turn_no, grads, select_own, select_from):
-        chosen = dot_tn(select_from, grads).astype(BF).reshape(rows_dp, capacity, width)
+        chosen = dot_nn(select_from, grads).astype(BF).reshape(rows_dp, capacity, width)
         arrived = [chosen[0]] + [turn(chosen[k], k) for k in range(1, rows_dp)]
         return dot_tn(select_own, jnp.concatenate(arrived))
 
+    targets_mine = targets.reshape(shards, local)[order].reshape(-1)
+    word = targets_mine - member * (rows_dp * words)
+    word_slot = jnp.where((word >= 0) & (word < rows_dp * words), word // words, rows_dp)
+    word_row = (word % words).astype(F32)[None, :]
+    word_hits = word_slot[None, :] == jnp.arange(rows_dp)[:, None]
+    word_rank = ranks(word_hits)
+    word_most = jnp.max(jnp.sum(word_hits.astype(F32), axis=1)).astype(jnp.int32)
+    word_rounds = ((word_most + capacity - 1) // capacity).reshape(1)
+
+    def token_weights():
+        everything = loss_mask.shape[0]
+        domain_of = jnp.take(domain_ids, jnp.arange(everything) // SEQ)
+        hits = ((domain_of[:, None] == jnp.arange(NDOM)[None, :]) & (loss_mask[:, None] > 0)).astype(
+            F32
+        )
+        counts = jnp.sum(hits, axis=0)
+        domain_weight = 10.0 * (NDOM - jnp.arange(NDOM)).astype(F32) / jnp.maximum(counts, 1.0)
+        group_hits = lax.dynamic_slice_in_dim(hits, batch_row * group, group, 0)
+        group_hits = group_hits.reshape(shards, local, NDOM)[order].reshape(group, NDOM)
+        token_weight = jnp.sum(group_hits * domain_weight[None, :], axis=1)
+        return token_weight, group_hits, counts
+
+    token_weight, group_hits, counts = token_weights()
+    lists = expert_lists[0, 0][order]
+    hot = lists[:, :, None] == jnp.arange(local)[None, None, :]
+    hot_b = hot.reshape(-1, local).astype(BF)
     select_own = own_select(0)
     select_from = from_select(0)
-    looked = look_up(0, select_own, select_from)
+    quick = quick_expert() and quick_dp()
+    arrived = look_up(select_own)
+    expert_shards = lax.all_gather(experts_b, "dp")
+    looked = put(arrived, select_from)
     _, looked = lax.while_loop(
         lambda state: state[0] < rounds,
         lambda state: (
             state[0] + 1,
             state[1]
-            + look_up(
-                state[0],
-                own_select(state[0].astype(F32)),
+            + put(
+                look_up(own_select(state[0].astype(F32))),
                 from_select(state[0].astype(F32)),
             ),
         ),
         (jnp.int32(1), looked),
     )
-    expert_shards = gather_shards(experts_b)
-    head_shards = gather_shards(head_b)
     if quick_expert() and quick_dp():
-        attn_blocks = gather_blocks(attn_parts.reshape(4 * piece, width))
-        attn_blocks = jnp.stack(attn_blocks)[order].reshape(4, 2, 4, piece, width)
-        attn_full = jnp.transpose(attn_blocks[:, :, slot_shards()], (0, 2, 1, 3, 4))
-        attn_full = attn_full.reshape(4, width, width)
+        attn_full = place_halves(member, attn_pieces)
     else:
         attn_full = lax.all_gather(attn_b, "dp", axis=1, tiled=True)
     embedded = sum_blocks(split_blocks(looked))
@@ -613,15 +695,13 @@
     normed_bb = normed(resid_one, gains[1]).astype(BF)
     router_logits = dot_nn(normed_bb, router_b)
     gates = jax.nn.softmax(router_logits, axis=-1)
-    lists = expert_lists[0, 0][order]
-    hot = lists[:, :, None] == jnp.arange(local)[None, None, :]
-    hot_b = hot.reshape(-1, local).astype(BF)
     gates_mine = jnp.transpose(gates[:, order])
     gate_table = jnp.where(hot, gates_mine[:, None, :], 0.0)
     slot_gates = jnp.sum(gate_table, axis=2).reshape(-1, 1)
     gate_high, gate_low = split_high_low(gate_table.reshape(-1, local))
     send = dot_nn(hot_b, normed_bb).astype(BF)
     received = jnp.concatenate(exchange(split_blocks(send)))
+    head_shards = lax.all_gather(after(head_b, expert_shards), "dp")
     pres, hiddens, produced = [], [], None
     for shard in expert_shards:
         pre = dot_nn(received, shard[0])
@@ -636,12 +716,34 @@
     normed_cb = normed(resid_two, gains[2]).astype(BF)
 
     rows_all = gather_rows(normed_cb)
-    targets_mine = targets.reshape(shards, local)[order].reshape(-1)
-    word = targets_mine - member * (rows_dp * words)
-    word_hit = (word >= 0) & (word < rows_dp * words)
-    word_place = jnp.where(word_hit, shard_slot(word // words) * words + word % words, -1)[None, :]
-    exps, stats = head_forward(rows_all, word_place, head_shards)
-    stats = stats[:3]
+    target_terms = whole_call(
+        functools.partial(target_kernel, capacity),
+        jax.ShapeDtypeStruct((rows_dp, words, width), BF),
+        "target_terms",
+        word_rounds,
+        word_rank,
+        word_row,
+        token_weight[None, :],
+        rows_all,
+    )
+    exps, head_stats = head_forward(rows_all, head_shards)
+    tops = head_stats[:rows_dp]
+    wanted, stats, ratios = whole_call(
+        functools.partial(stats_kernel, capacity),
+        (
+            jax.ShapeDtypeStruct((group, width), BF),
+            jax.ShapeDtypeStruct((3, group), F32),
+            jax.ShapeDtypeStruct((rows_dp, group), F32),
+        ),
+        "target_stats",
+        word_rounds,
+        word_rank,
+        word_row,
+        head_shards,
+        rows_all,
+        head_stats,
+    )
+    top_here = stats[0]
     if quick_expert():
         gathered = [stats]
         for k in range(1, 8):
@@ -656,28 +758,27 @@
     total = jnp.sum(gathered[:, 1] * jnp.exp(gathered[:, 0] - top[None, :]), axis=0)
     logsum_tok = top + jnp.log(total)
     loss_tok = logsum_tok - jnp.sum(gathered[:, 2], axis=0)
-    everything = loss_mask.shape[0]
-    domain_of = jnp.take(domain_ids, jnp.arange(everything) // SEQ)
-    hits = ((domain_of[:, None] == jnp.arange(NDOM)[None, :]) & (loss_mask[:, None] > 0)).astype(
-        F32
-    )
-    counts = jnp.sum(hits, axis=0)
-    domain_weight = 10.0 * (NDOM - jnp.arange(NDOM)).astype(F32) / jnp.maximum(counts, 1.0)
-    group_hits = lax.dynamic_slice_in_dim(hits, batch_row * group, group, 0)
-    group_hits = group_hits.reshape(shards, local, NDOM)[order].reshape(group, NDOM)
-    token_weight = jnp.sum(group_hits * domain_weight[None, :], axis=1)
     own_block = 0 if quick_expert() else member
     own_sums = jnp.sum(
         lax.dynamic_slice_in_dim(group_hits, own_block * local, local, 0)
         * lax.dynamic_slice_in_dim(loss_tok, own_block * local, local, 0)[:, None],
         axis=0,
     )
-    coef = jnp.stack([token_weight * jnp.exp(stats[0] - logsum_tok), token_weight])
-    grad_rows_c = head_rows_back(coef, word_place, head_shards, exps)
+    spread_rows = head_rows_back(ratios, head_shards, exps)
+    scales = token_weight[None, :] * jnp.exp(tops - logsum_tok[None, :])
+    scale_here = token_weight * jnp.exp(top_here - logsum_tok)
     grad_heads = [
-        head_weight_back(coef, word_place, exps[k], rows_all, k * words) for k in range(rows_dp)
+        (
+            dot_nn(exps[k], (rows_all.astype(F32) * scales[k][:, None]).astype(BF))
+            - target_terms[k].astype(F32)
+        ).astype(BF)
+        for k in range(rows_dp)
     ]
-    grad_head = sum_shards(grad_heads)
+    grad_head = sum_shards(jnp.stack(grad_heads))
+    grad_rows_c = (
+        spread_rows.astype(F32) * scale_here[:, None]
+        - wanted.astype(F32) * token_weight[:, None]
+    ).astype(BF)
     grad_normed_c = sum_blocks(split_blocks(grad_rows_c))
     grad_two, grad_gain_c = norm_back(resid_two, gains[2], grad_normed_c)
 
@@ -687,17 +788,17 @@
     grad_produced = jnp.concatenate(
         exchange(split_blocks((grad_slot * slot_gates).astype(BF)))
     )
-    grad_experts_parts, grad_sent = [], None
-    for shard, pre, hidden in zip(expert_shards, pres, hiddens):
-        grad_hidden = dot_nn(grad_produced, shard[1])
-        _, gelu_pull = jax.vjp(gelu, pre)
+    grad_parts, grad_sent = [], None
+    for k in range(rows_dp):
+        grad_hidden = dot_nn(grad_produced, expert_shards[k, 1])
+        _, gelu_pull = jax.vjp(gelu, pres[k])
         grad_pre = gelu_pull(grad_hidden)[0].astype(BF)
-        grad_down = dot_tn(grad_produced, hidden)
-        grad_up = dot_tn(received, grad_pre)
-        term = dot_nt(grad_pre, shard[0])
+        grad_parts.append(dot_tn(received, grad_pre).astype(BF))
+        grad_parts.append(dot_tn(grad_produced, hiddens[k]).astype(BF))
+        term = dot_nt(grad_pre, expert_shards[k, 0])
         grad_sent = term if grad_sent is None else grad_sent + term
-        grad_experts_parts.append(jnp.stack([grad_up, grad_down]).astype(BF))
-    grad_experts = sum_shards(grad_experts_parts)[None]
+    grad_parts = jnp.stack(grad_parts).reshape(rows_dp, 2, width, -1)
+    grad_experts = sum_shards(grad_parts)[None]
     grad_back = jnp.concatenate(exchange(split_blocks(grad_sent.astype(BF))))
     grad_normed_b = dot_tn(hot_b, grad_back)
     grad_gates = jnp.sum(
@@ -712,7 +813,6 @@
     grad_one = grad_two + normal_back
 
     grad_branch = grad_one.astype(BF)
-    grad_wo = dot_tn(mixed_b, grad_branch)
     grad_mixed = dot_nt(grad_branch, attn_full[3]).astype(BF)
     grad_query, grad_keys, grad_values = attend_back(
         queries, keys, values, grad_mixed, mixed_b, logsum, key_place, query_place
@@ -738,24 +838,31 @@
         ),
         (jnp.int32(1), grad_embed),
     )
-    grad_attn = jnp.stack(
-        [
-            dot_tn(normed_ab, grad_query),
-            dot_tn(normed_all, grad_keys),
-            dot_tn(normed_all, grad_values),
-            grad_wo,
-        ]
-    ).astype(BF)
     if quick_expert() and quick_dp():
-        cut = grad_attn.reshape(4, 4, 2, piece, width)
-        cut = jnp.transpose(cut, (0, 2, 1, 3, 4)).reshape(8, 4, piece, width)
-        cut = cut[order][:, slot_shards()].reshape(8, 4 * piece, width)
-        part = sum_blocks([cut[j] for j in range(8)]).astype(BF)
-        part = sum_shards([part[k * piece : (k + 1) * piece] for k in range(4)])
+        blocks = attn_weight_back(
+            member,
+            normed_ab,
+            normed_all,
+            mixed_b,
+            grad_query,
+            grad_keys,
+            grad_values,
+            grad_branch,
+        )
+        part = sum_blocks([blocks[j] for j in range(8)]).astype(BF)
+        part = part.reshape(4, width // 4, width // 2)[slot_shards()]
+        part = sum_turns([part[k] for k in range(4)])
         attn_squares = jnp.sum(part * part)
-        back = jnp.stack(gather_blocks(part.astype(BF)))[order]
-        grad_attn = back.reshape(4, 2 * piece, width).astype(F32)
+        grad_attn = place_halves(member, gather_pieces(part.astype(BF))).astype(F32)
     else:
+        grad_attn = jnp.stack(
+            [
+                dot_tn(normed_ab, grad_query),
+                dot_tn(normed_all, grad_keys),
+                dot_tn(normed_all, grad_values),
+                dot_tn(mixed_b, grad_branch),
+            ]
+        ).astype(BF)
         grad_attn = lax.psum_scatter(grad_attn, "dp", scatter_dimension=1, tiled=True)
         grad_attn = lax.psum(grad_attn, "expert").astype(F32)
         attn_squares = jnp.sum(grad_attn * grad_attn) / shards

time: 1090 us -> 810 us (0.74)
  waiting for transfers between devices: 508 us -> 206 us
  local copies, waits for them, and re-layouts: 94.9 us -> 77.5 us
  matrix products: 111 us -> 127 us
  starting transfers between devices: 132 us -> 148 us
  between operations: 10.1 us -> 23.7 us
    ppermute x27 -> x15, waiting for transfers between devices: 358 us -> 53.9 us  [turn(): lax.ppermute(array, 'dp', [(i, (i + steps) % count) for i in range(count)])]
    ppermute x125 -> x127, waiting for transfers between devices: 150 us -> 101 us  [swap(): return lax.ppermute(array, axis, pairs)]
    reduce_scatter x0 -> x2, waiting for transfers between devices: none -> 25.7 us  [sum_shards(): lax.psum_scatter(parts, 'dp', scatter_dimension=0, tiled=False).astype(F32)]
    all_gather x0 -> x2, waiting for transfers between devices: none -> 24.9 us  [the longest x1 12.7 us: body(): expert_shards = lax.all_gather(experts_b, 'dp')]
    gather x7 -> x4, local copies, waits for them, and re-layouts: 25.8 us -> 2.77 us  [the longest x1 0.8 us: body(): part = part.reshape(4, width // 4, width // 2)[slot_shards()]]
    dot_general x49, matrix products: 111 us -> 127 us  [dot(): lax.dot_general(a, b, ((contract[0], contract[1]), ((), ())), preferred_e...]
    ppermute x125 -> x127, starting transfers between devices: 93.7 us -> 106 us  [swap(): return lax.ppermute(array, axis, pairs)]
    unnamed x310 -> x317, local copies, waits for them, and re-layouts: 33.8 us -> 42.1 us
  transfers between devices with their start and end apart: 152 -> 146, of which waited for: 59 -> 45; matrix products, arithmetic and copies ran while one was open for 17% -> 31% of each run, Pallas kernels for 4% -> 11%
where the time goes in v2:
time: 810 us; the launch traced here: 800 us
  waiting for transfers between devices  206 us (25%)
  starting transfers between devices  148 us (18%)
  matrix products  127 us (16%)
  Pallas kernels  124 us (15%)
  other arithmetic  93.6 us (12%)
  local copies, waits for them, and re-layouts  77.5 us (10%)
  between operations  23.7 us (3%)
    dot_general x49, matrix products, dot(): lax.dot_general(a, b, ((contract[0], contract[1]), ((), ())), preferred_e...  127 us
    ppermute x127, starting transfers between devices, swap(): return lax.ppermute(array, axis, pairs)  106 us
    ppermute x127, waiting for transfers between devices, swap(): return lax.ppermute(array, axis, pairs)  101 us
    ppermute x15, waiting for transfers between devices, turn(): lax.ppermute(array, 'dp', [(i, (i + steps) % count) for i in range(count)])  53.9 us
    unnamed x317, local copies, waits for them, and re-layouts  42.1 us
    ppermute x15, starting transfers between devices, turn(): lax.ppermute(array, 'dp', [(i, (i + steps) % count) for i in range(count)])  41 us
    convert_element_type x5, other arithmetic, adam(): return (first, second, weight, weight.astype(BF))  36.3 us
    reduce_scatter x2, waiting for transfers between devices, sum_shards(): lax.psum_scatter(parts, 'dp', scatter_dimension=0, tiled=False).astype(F32)  25.7 us
  transfers between devices with their start and end apart: 146, of which 45 were waited for; matrix products, arithmetic and copies ran while one was open for 31% of the time, Pallas kernels for 11%

profile of v2, /device:TPU:0, one launch (start us, length us, event | category | flops | bytes accessed | tf_op | source)
XLA Modules:
  0.0 799.9 jit_solution(4460931552630990154)
XLA Ops:
  7.3 5.1 collective-permute-start.8
  13.4 4.0 convert_element_type.623
  49.3 18.8 %collective-permute-done.10 = bf16[128,768]{1,0:T(8,128)(2,1)S(1)} collective-permute-done((bf16[128,768]{1,0:T(8,128)(2,1)S(1)}, bf16[128,768]{1,0:T(8,128)(2,1)S(1)}, u32[]{:S(2)}, u32[]{:S(2)}) %collective-permute-start.10) | collective-permute-done | bytes 196640 | tf_op jit(solution)/shard_map/ppermute | solution.py:76
  68.2 4.8 convolution_convert_fusion.4
  76.5 14.8 %collective-permute-start.22 = (bf16[192,384]{1,0:T(8,128)(2,1)S(1)}, bf16[192,384]{1,0:T(8,128)(2,1)S(1)}, u32[]{:S(2)}, u32[]{:S(2)}) collective-permute-start(bf16[192,384]{1,0:T(8,128)(2,1)S(1)} %fusion.351), channel_id=1, source_target_pairs={{0,8},{8,16},{16,24},{24,0},{1,9},{9,17},{17,25},{25,1},{2,10},{10... | collective-permute-start | bytes 442376 | tf_op jit(solution)/shard_map/ppermute | solution.py:76
  98.7 7.5 collective-permute-done.23
  106.2 4.8 collective-permute-done.24
  119.7 12.8 %collective-permute-done.17 = bf16[128,768]{1,0:T(8,128)(2,1)S(1)} collective-permute-done((bf16[128,768]{1,0:T(8,128)(2,1)}, bf16[128,768]{1,0:T(8,128)(2,1)S(1)}, u32[]{:S(2)}, u32[]{:S(2)}) %collective-permute-start.17) | collective-permute-done | bytes 196640 | tf_op jit(solution)/shard_map/ppermute | solution.py:71
  142.5 3.6 collective-permute-done.30.refs_6_
  150.7 4.9 place_halves.2
  160.8 5.1 collective-permute-done.39
  168.6 4.0 convolution_convert_fusion.2.v_ref
  172.6 4.0 convolution_convert_fusion.3.k_ref
  177.1 18.7 %attend.1 = (bf16[256,768]{1,0:T(8,128)(2,1)}, f32[12,256]{1,0:T(8,128)}) custom-call(bf16[256,768]{1,0:T(8,128)(2,1)} %convolution_convert_fusion.16.q_ref, bf16[2048,768]{1,0:T(8,128)(2,1)} %convolution_convert_fusion.3.k_ref, bf16[2048,768]{1,0:T(8,128)(2,1)} %convolution_convert_fusion.2.v_ref, s32[2048,1]{1,0:T(8,128)} %compare_select_fusion.kp_ref, ...), custom_call_target="tpu_custom_call" | custom-call | flops 1000 | bytes 2 | tf_op jit(solution)/shard_map/attend/pallas_call | solution.py:237
  201.9 12.7 %all-gather.4.cloned.1.call-done = bf16[4,2,768,768]{3,2,1,0:T(8,128)(2,1)} async-done(((bf16[1,2,768,768]{3,2,1,0:T(8,128)(2,1)}), bf16[4,2,768,768]{3,2,1,0:T(8,128)(2,1)}) %all-gather.4.cloned.1.call-update) | async-done | bytes 9437200 | tf_op jit(solution)/shard_map/all_gather | solution.py:662
  221.9 8.8 %collective-permute-done.47 = bf16[128,768]{1,0:T(8,128)(2,1)S(1)} collective-permute-done((bf16[128,768]{1,0:T(8,128)(2,1)S(1)}, bf16[128,768]{1,0:T(8,128)(2,1)S(1)}, u32[]{:S(2)}, u32[]{:S(2)}) %collective-permute-start.47) | collective-permute-done | bytes 196640 | tf_op jit(solution)/shard_map/ppermute | solution.py:71
  232.8 3.5 fusion.154
  236.7 4.0 fusion.158
  264.4 11.5 %collective-permute-done.54 = bf16[128,768]{1,0:T(8,128)(2,1)S(1)} collective-permute-done((bf16[128,768]{1,0:T(8,128)(2,1)}, bf16[128,768]{1,0:T(8,128)(2,1)S(1)}, u32[]{:S(2)}, u32[]{:S(2)}) %collective-permute-start.54) | collective-permute-done | bytes 196640 | tf_op jit(solution)/shard_map/ppermute | solution.py:71
  285.1 5.2 collective-permute-done.58
  306.9 8.9 %target_terms.1 = bf16[4,1000,768]{2,1,0:T(8,128)(2,1)} custom-call(s32[1]{0:T(128)} %bitcast.30.rounds_ref, f32[4,2048]{1,0:T(4,128)} %bitcast.486, f32[1,2048]{1,0:T(1,128)} %fusion.238.word_ref, f32[1,2048]{1,0:T(1,128)} %bitcast.520, bf16[2048,768]{1,0:T(8,128)(2,1)} %constant_dynamic-update-slice_fusion.26.rows_ref), custom_call_target="tpu_custom_call" | custom-call | flops 1000 | bytes 2 | tf_op jit(solution)/shard_map/target_terms/pallas_call | solution.py:487
  315.8 12.2 %all-gather.6.cloned.1.call-done = bf16[4000,768]{1,0:T(8,128)(2,1)} async-done(((bf16[1000,768]{1,0:T(8,128)(2,1)}), bf16[4000,768]{1,0:T(8,128)(2,1)}) %all-gather.6.cloned.1.call-update) | async-done | bytes 6144016 | tf_op jit(solution)/shard_map/all_gather | solution.py:704
  328.0 23.9 %head_forward.1 = (bf16[4,1000,2048]{2,1,0:T(8,128)(2,1)}, f32[8,2048]{1,0:T(8,128)}) custom-call(bf16[2048,768]{1,0:T(8,128)(2,1)} %constant_dynamic-update-slice_fusion.26.rows_ref, bf16[4,1000,768]{2,1,0:T(8,128)(2,1)} %bitcast.465), custom_call_target="tpu_custom_call" | custom-call | flops 12582912000 | bytes 25165824 | tf_op jit(solution)/shard_map/head_forward/pallas_call | solution.py:398
  351.9 9.4 %target_stats.1 = (bf16[2048,768]{1,0:T(8,128)(2,1)}, f32[3,2048]{1,0:T(4,128)}, f32[4,2048]{1,0:T(4,128)}) custom-call(s32[1]{0:T(128)} %bitcast.30.rounds_ref, f32[4,2048]{1,0:T(4,128)} %bitcast.487, f32[1,2048]{1,0:T(1,128)} %fusion.238.word_ref, bf16[4,1000,768]{2,1,0:T(8,128)(2,1)} %bitcast.466, ...), custom_call_target="tpu_custom_call" | custom-call | flops 1000 | bytes 2 | tf_op jit(solution)/shard_map/target_stats/pallas_call | solution.py:487
  364.7 19.7 %head_rows_back.1 = bf16[2048,768]{1,0:T(8,128)(2,1)} custom-call(f32[4,2048]{1,0:T(4,128)} %get-tuple-element.246.coef_ref, bf16[4,1000,768]{2,1,0:T(8,128)(2,1)} %bitcast.467, bf16[4,1000,2048]{2,1,0:T(8,128)(2,1)} %get-tuple-element.247.exps_ref), custom_call_target="tpu_custom_call" | custom-call | flops 12582912000 | bytes 25165824 | tf_op jit(solution)/shard_map/head_rows_back/pallas_call | solution.py:511
  398.8 6.3 fusion.105
  405.2 5.6 fusion.110
  410.8 5.6 fusion.115
  416.4 5.6 fusion.120
  461.8 8.4 %collective-permute-done.87 = bf16[128,768]{1,0:T(8,128)(2,1)S(1)} collective-permute-done((bf16[128,768]{1,0:T(8,128)(2,1)S(1)}, bf16[128,768]{1,0:T(8,128)(2,1)S(1)}, u32[]{:S(2)}, u32[]{:S(2)}) %collective-permute-start.87) | collective-permute-done | bytes 196640 | tf_op jit(solution)/shard_map/ppermute | solution.py:71
  472.3 4.6 fusion.59
  480.6 3.5 fusion.52
  486.6 3.5 fusion.66
  493.1 3.9 fusion.73
  530.8 7.8 collective-permute-done.94
  544.0 21.1 %attend_back.1 = (bf16[256,768]{1,0:T(8,128)(2,1)}, bf16[2048,768]{1,0:T(8,128)(2,1)}, bf16[2048,768]{1,0:T(8,128)(2,1)}) custom-call(bf16[256,768]{1,0:T(8,128)(2,1)} %convolution_convert_fusion.16.q_ref, bf16[2048,768]{1,0:T(8,128)(2,1)} %convolution_convert_fusion.3.k_ref, bf16[2048,768]{1,0:T(8,128)(2,1)} %convolution_convert_fusion.2.v_ref, ...), custom_call_target="tpu_custom_call" | custom-call | flops 1000 | bytes 2 | tf_op jit(solution)/shard_map/attend_back/pallas_call | solution.py:303
  565.2 4.8 fusion.152
  574.7 15.3 %attn_weight_back.1 = bf16[8,768,384]{2,1,0:T(8,128)(2,1)} custom-call(s32[1]{0:T(128)} %bitcast.17.member_ref, bf16[256,768]{1,0:T(8,128)(2,1)} %copy-done.36, bf16[2048,768]{1,0:T(8,128)(2,1)} %copy-done.60, bf16[256,768]{1,0:T(8,128)(2,1)} %get-tuple-element.243.o_ref.mixed_ref, bf16[256,768]{1,0:T(8,128)(2,1)} %get-tuple-element.253.q_ref, ...), custom_call_target="tpu_custom_call" | custom-call | flops 5435817984 | bytes 10871635 | tf_op jit(solution)/shard_map/attn_weight_back/pallas_call | solution.py:369
  630.2 4.3 collective-permute-done.127
  635.7 3.8 collective-permute-start.131
  656.7 3.7 convolution_convert_fusion.14
  670.6 3.7 collective-permute-done.116
  674.3 14.4 %collective-permute-done.117 = bf16[128,768]{1,0:T(8,128)(2,1)S(1)} collective-permute-done((bf16[128,768]{1,0:T(8,128)(2,1)S(1)}, bf16[128,768]{1,0:T(8,128)(2,1)S(1)}, u32[]{:S(2)}, u32[]{:S(2)}) %collective-permute-start.117) | collective-permute-done | bytes 196640 | tf_op jit(solution)/shard_map/ppermute | solution.py:76
  695.4 25.7 %reduce-scatter.5.cloned.1.call-done = bf16[1,2,768,768]{3,2,1,0:T(8,128)(2,1)} async-done(((bf16[4,2,768,768]{3,2,1,0:T(8,128)(2,1)}), bf16[1,2,768,768]{3,2,1,0:T(8,128)(2,1)}) %reduce-scatter.5.cloned.1.call-update) | async-done | bytes 2359312 | tf_op jit(solution)/shard_map/reduce_scatter | solution.py:177
  737.0 5.7 collective-permute-start.136
  758.4 8.4 %fusion.271 = (bf16[4,192,768]{2,1,0:T(8,128)(2,1)}, f32[4,192,768]{2,1,0:T(8,128)}, f32[4,192,768]{2,1,0:T(8,128)}, f32[4,192,768]{2,1,0:T(8,128)}) fusion(f32[4,192,768]{2,1,0:T(8,128)} %param.32, f32[]{:T(128)S(6)} %min.3, bf16[4,192,768]{2,1,0:T(8,128)(2,1)} %place_halves.3, f32[4,192,768]{2,1,0:T(8,128)} %param.34, f32[4,192,768]{2,1,0:T(8,128)} %param.33), kind=kLoop, calls=%fused_computation.627 | loop fusion | flops 10027008 | bytes 16515076 | tf_op jit(solution)/shard_map/convert_element_type | solution.py:46
  766.8 15.1 %fusion.273 = (bf16[2,1000,768]{2,1,0:T(8,128)(2,1)}, f32[2,1000,768]{2,1,0:T(8,128)}, f32[2,1000,768]{2,1,0:T(8,128)}, f32[2,1000,768]{2,1,0:T(8,128)}) fusion(f32[2,1000,768]{2,1,0:T(8,128)} %param.29, f32[]{:T(128)S(6)} %min.3, f32[1,1000,768]{2,1,0:T(8,128)} %convert_element_type.705, f32[1,1000,768]{2,1,0:T(8,128)S(1)} %bitcast.459, ...), kind=kLoop, calls=%fused_computation.628 | loop fusion | flops 26112000 | bytes 46080004 | tf_op jit(solution)/shard_map/convert_element_type | solution.py:46
  781.9 10.1 %fusion.269 = (bf16[1,2,768,768]{3,2,1,0:T(8,128)(2,1)}, f32[1,2,768,768]{3,2,1,0:T(8,128)}, f32[1,2,768,768]{3,2,1,0:T(8,128)}, f32[1,2,768,768]{3,2,1,0:T(8,128)}) fusion(f32[1,2,768,768]{3,2,1,0:T(8,128)S(1)} %bitcast.462, f32[]{:T(128)S(6)} %min.3, bf16[1,2,768,768]{3,2,1,0:T(8,128)(2,1)} %reduce-scatter.5.cloned.1.call-done, ...), kind=kLoop, calls=%fused_computation.626 | loop fusion | flops 20054016 | bytes 33030148 | tf_op jit(solution)/shard_map/convert_element_type | solution.py:46
  (819 shorter events, 352.4 us)
Async XLA Ops:
  7.2 207.4 %all-gather.4.cloned.1.call-start = ((), (), s32[]{:S(2)}) async-start(), calls=%async_computation.2 | async-start | bytes 11796480 | tf_op jit(solution)/shard_map/all_gather | solution.py:662
  7.3 28.8 %collective-permute-start.8 = (s32[2048]{0:T(1024)}, s32[2048]{0:T(1024)S(1)}, u32[]{:S(2)}, u32[]{:S(2)}) collective-permute-start(s32[2048]{0:T(1024)} %param.24), channel_id=1, source_target_pairs={{0,24},{8,0},{16,8},{24,16},{1,25},{9,1},{17,9},{25,17},{2,26},{10... | collective-permute-start | bytes 24584 | tf_op jit(solution)/shard_map/ppermute | solution.py:76
  12.4 23.8 %collective-permute-start.6 = (s32[2048]{0:T(1024)}, s32[2048]{0:T(1024)S(1)}, u32[]{:S(2)}, u32[]{:S(2)}) collective-permute-start(s32[2048]{0:T(1024)} %param.24), channel_id=1, source_target_pairs={{0,8},{8,16},{16,24},{24,0},{1,9},{9,17},{17,25},{25,1},{2,10},{10... | collective-permute-start | bytes 24584 | tf_op jit(solution)/shard_map/ppermute | solution.py:76
  12.4 23.8 %collective-permute-start.7 = (s32[2048]{0:T(1024)}, s32[2048]{0:T(1024)S(1)}, u32[]{:S(2)}, u32[]{:S(2)}) collective-permute-start(s32[2048]{0:T(1024)} %param.24), channel_id=1, source_target_pairs={{0,16},{8,24},{16,0},{24,8},{1,17},{9,25},{17,1},{25,9},{2,18},{10... | collective-permute-start | bytes 24584 | tf_op jit(solution)/shard_map/ppermute | solution.py:76
  17.4 310.6 %all-gather.6.cloned.1.call-start = ((), (), s32[]{:S(2)}) async-start(), calls=%async_computation.5 | async-start | bytes 7680000 | tf_op jit(solution)/shard_map/all_gather | solution.py:704
  40.4 27.7 %collective-permute-start.10 = (bf16[128,768]{1,0:T(8,128)(2,1)S(1)}, bf16[128,768]{1,0:T(8,128)(2,1)S(1)}, u32[]{:S(2)}, u32[]{:S(2)}) collective-permute-start(bf16[128,768]{1,0:T(8,128)(2,1)S(1)} %get-tuple-element.619), channel_id=1, source_target_pairs={{0,16},{8,24},{16,0},{24,8},{1,17},{9,25},{17,1},{25,9},{2,18},{10... | collective-permute-start | bytes 589832 | tf_op jit(solution)/shard_map/ppermute | solution.py:76
  42.4 25.7 %collective-permute-start.11 = (bf16[128,768]{1,0:T(8,128)(2,1)S(1)}, bf16[128,768]{1,0:T(8,128)(2,1)S(1)}, u32[]{:S(2)}, u32[]{:S(2)}) collective-permute-start(bf16[128,768]{1,0:T(8,128)(2,1)S(1)} %get-tuple-element.618), channel_id=1, source_target_pairs={{0,8},{8,16},{16,24},{24,0},{1,9},{9,17},{17,25},{25,1},{2,10},{10... | collective-permute-start | bytes 589832 | tf_op jit(solution)/shard_map/ppermute | solution.py:76
  43.9 24.3 %collective-permute-start.9 = (bf16[128,768]{1,0:T(8,128)(2,1)S(1)}, bf16[128,768]{1,0:T(8,128)(2,1)S(1)}, u32[]{:S(2)}, u32[]{:S(2)}) collective-permute-start(bf16[128,768]{1,0:T(8,128)(2,1)S(1)} %get-tuple-element.620), channel_id=1, source_target_pairs={{0,24},{8,0},{16,8},{24,16},{1,25},{9,1},{17,9},{25,17},{2,26},{10... | collective-permute-start | bytes 589832 | tf_op jit(solution)/shard_map/ppermute | solution.py:76
  75.4 18.9 %collective-permute-start.15 = (bf16[256,768]{1,0:T(8,128)(2,1)S(1)}, bf16[256,768]{1,0:T(8,128)(2,1)S(1)}, u32[]{:S(2)}, u32[]{:S(2)}) collective-permute-start(bf16[256,768]{1,0:T(8,128)(2,1)S(1)} %get-tuple-element.566), channel_id=1, source_target_pairs={{0,1},{1,0},{2,3},{3,2},{4,5},{5,4},{6,7},{7,6},{8,9},{9,8},{10,11... | collective-permute-start | bytes 1179656 | tf_op jit(solution)/shard_map/ppermute | solution.py:71
  75.5 18.8 %collective-permute-start.16 = (bf16[256,768]{1,0:T(8,128)(2,1)S(1)}, bf16[256,768]{1,0:T(8,128)(2,1)S(1)}, u32[]{:S(2)}, u32[]{:S(2)}) collective-permute-start(bf16[256,768]{1,0:T(8,128)(2,1)S(1)} %get-tuple-element.565), channel_id=1, source_target_pairs={{0,1},{1,0},{2,3},{3,2},{4,5},{5,4},{6,7},{7,6},{8,9},{9,8},{10,11... | collective-permute-start | bytes 1179656 | tf_op jit(solution)/shard_map/ppermute | solution.py:71
  76.5 22.2 %collective-permute-start.22 = (bf16[192,384]{1,0:T(8,128)(2,1)S(1)}, bf16[192,384]{1,0:T(8,128)(2,1)S(1)}, u32[]{:S(2)}, u32[]{:S(2)}) collective-permute-start(bf16[192,384]{1,0:T(8,128)(2,1)S(1)} %fusion.351), channel_id=1, source_target_pairs={{0,8},{8,16},{16,24},{24,0},{1,9},{9,17},{17,25},{25,1},{2,10},{10... | collective-permute-start | bytes 442376 | tf_op jit(solution)/shard_map/ppermute | solution.py:76
  91.4 19.6 %collective-permute-start.24 = (bf16[192,384]{1,0:T(8,128)(2,1)S(1)}, bf16[192,384]{1,0:T(8,128)(2,1)S(1)}, u32[]{:S(2)}, u32[]{:S(2)}) collective-permute-start(bf16[192,384]{1,0:T(8,128)(2,1)S(1)} %fusion.351), channel_id=1, source_target_pairs={{0,24},{8,0},{16,8},{24,16},{1,25},{9,1},{17,9},{25,17},{2,26},{10... | collective-permute-start | bytes 442376 | tf_op jit(solution)/shard_map/ppermute | solution.py:76
  95.4 22.8 %collective-permute-start.19 = (bf16[128,768]{1,0:T(8,128)(2,1)}, bf16[128,768]{1,0:T(8,128)(2,1)}, u32[]{:S(2)}, u32[]{:S(2)}) collective-permute-start(bf16[128,768]{1,0:T(8,128)(2,1)} %get-tuple-element.630), channel_id=1, source_target_pairs={{0,4},{1,5},{2,6},{3,7},{4,0},{5,1},{6,2},{7,3},{8,12},{9,13},{10,... | collective-permute-start | bytes 589832 | tf_op jit(solution)/shard_map/ppermute | solution.py:71
  111.9 22.2 %collective-permute-start.26 = (bf16[768,384]{1,0:T(8,128)(2,1)S(1)}, bf16[768,384]{1,0:T(8,128)(2,1)S(1)}, u32[]{:S(2)}, u32[]{:S(2)}) collective-permute-start(bf16[768,384]{1,0:T(8,128)(2,1)S(1)} %bitcast.477), channel_id=1, source_target_pairs={{0,2},{1,3},{2,0},{3,1},{4,6},{5,7},{6,4},{7,5},{8,10},{9,11},{10,... | collective-permute-start | bytes 1769480 | tf_op jit(solution)/shard_map/ppermute | solution.py:71
  114.4 22.1 %collective-permute-start.28 = (bf16[768,384]{1,0:T(8,128)(2,1)S(1)}, bf16[768,384]{1,0:T(8,128)(2,1)S(1)}, u32[]{:S(2)}, u32[]{:S(2)}) collective-permute-start(bf16[768,384]{1,0:T(8,128)(2,1)S(1)} %bitcast.478), channel_id=1, source_target_pairs={{0,4},{1,5},{2,6},{3,7},{4,0},{5,1},{6,2},{7,3},{8,12},{9,13},{10,... | collective-permute-start | bytes 1769480 | tf_op jit(solution)/shard_map/ppermute | solution.py:71
  116.6 20.1 %collective-permute-start.14 = (bf16[128,768]{1,0:T(8,128)(2,1)S(1)}, bf16[128,768]{1,0:T(8,128)(2,1)S(1)}, u32[]{:S(2)}, u32[]{:S(2)}) collective-permute-start(bf16[128,768]{1,0:T(8,128)(2,1)S(1)} %slice.1393), channel_id=1, source_target_pairs={{0,2},{1,3},{2,0},{3,1},{4,6},{5,7},{6,4},{7,5},{8,10},{9,11},{10,... | collective-permute-start | bytes 589832 | tf_op jit(solution)/shard_map/ppermute | solution.py:71
  119.1 19.1 %collective-permute-start.21 = (bf16[128,768]{1,0:T(8,128)(2,1)S(1)}, bf16[128,768]{1,0:T(8,128)(2,1)S(1)}, u32[]{:S(2)}, u32[]{:S(2)}) collective-permute-start(bf16[128,768]{1,0:T(8,128)(2,1)S(1)} %slice.1392), channel_id=1, source_target_pairs={{0,4},{1,5},{2,6},{3,7},{4,0},{5,1},{6,2},{7,3},{8,12},{9,13},{10,... | collective-permute-start | bytes 589832 | tf_op jit(solution)/shard_map/ppermute | solution.py:71
  199.6 16.9 %collective-permute-start.43 = (bf16[128,768]{1,0:T(8,128)(2,1)}, bf16[128,768]{1,0:T(8,128)(2,1)S(1)}, u32[]{:S(2)}, u32[]{:S(2)}) collective-permute-start(bf16[128,768]{1,0:T(8,128)(2,1)} %get-tuple-element.601), channel_id=1, source_target_pairs={{0,1},{1,0},{2,3},{3,2},{4,5},{5,4},{6,7},{7,6},{8,9},{9,8},{10,11... | collective-permute-start | bytes 589832 | tf_op jit(solution)/shard_map/ppermute | solution.py:71
  199.7 18.9 %collective-permute-start.44 = (bf16[128,768]{1,0:T(8,128)(2,1)}, bf16[128,768]{1,0:T(8,128)(2,1)S(1)}, u32[]{:S(2)}, u32[]{:S(2)}) collective-permute-start(bf16[128,768]{1,0:T(8,128)(2,1)} %get-tuple-element.600), channel_id=1, source_target_pairs={{0,2},{1,3},{2,0},{3,1},{4,6},{5,7},{6,4},{7,5},{8,10},{9,11},{10,... | collective-permute-start | bytes 589832 | tf_op jit(solution)/shard_map/ppermute | solution.py:71
  200.3 20.3 %collective-permute-start.45 = (bf16[128,768]{1,0:T(8,128)(2,1)}, bf16[128,768]{1,0:T(8,128)(2,1)S(1)}, u32[]{:S(2)}, u32[]{:S(2)}) collective-permute-start(bf16[128,768]{1,0:T(8,128)(2,1)} %get-tuple-element.599), channel_id=1, source_target_pairs={{0,3},{1,2},{2,1},{3,0},{4,7},{5,6},{6,5},{7,4},{8,11},{9,10},{10,... | collective-permute-start | bytes 589832 | tf_op jit(solution)/shard_map/ppermute | solution.py:71
  201.4 19.8 %collective-permute-start.46 = (bf16[128,768]{1,0:T(8,128)(2,1)}, bf16[128,768]{1,0:T(8,128)(2,1)S(1)}, u32[]{:S(2)}, u32[]{:S(2)}) collective-permute-start(bf16[128,768]{1,0:T(8,128)(2,1)} %get-tuple-element.598), channel_id=1, source_target_pairs={{0,4},{1,5},{2,6},{3,7},{4,0},{5,1},{6,2},{7,3},{8,12},{9,13},{10,... | collective-permute-start | bytes 589832 | tf_op jit(solution)/shard_map/ppermute | solution.py:71
  214.7 476.7 %reduce-scatter.3.cloned.1.call-start = ((), (), s32[]{:S(2)}) async-start(), calls=%async_computation.3 | async-start | bytes 7680000 | tf_op jit(solution)/shard_map/reduce_scatter | solution.py:177
  257.5 18.5 %collective-permute-start.54 = (bf16[128,768]{1,0:T(8,128)(2,1)}, bf16[128,768]{1,0:T(8,128)(2,1)S(1)}, u32[]{:S(2)}, u32[]{:S(2)}) collective-permute-start(bf16[128,768]{1,0:T(8,128)(2,1)} %get-tuple-element.589), channel_id=1, source_target_pairs={{0,5},{1,4},{2,7},{3,6},{4,1},{5,0},{6,3},{7,2},{8,13},{9,12},{10,... | collective-permute-start | bytes 589832 | tf_op jit(solution)/shard_map/ppermute | solution.py:71
  258.9 17.1 %collective-permute-start.55 = (bf16[128,768]{1,0:T(8,128)(2,1)S(1)}, bf16[128,768]{1,0:T(8,128)(2,1)S(1)}, u32[]{:S(2)}, u32[]{:S(2)}) collective-permute-start(bf16[128,768]{1,0:T(8,128)(2,1)S(1)} %get-tuple-element.588), channel_id=1, source_target_pairs={{0,6},{1,7},{2,4},{3,5},{4,2},{5,3},{6,0},{7,1},{8,14},{9,15},{10,... | collective-permute-start | bytes 589832 | tf_op jit(solution)/shard_map/ppermute | solution.py:71
  361.3 32.0 %collective-permute-start.72 = (f32[3,2048]{1,0:T(4,128)}, f32[3,2048]{1,0:T(4,128)S(1)}, u32[]{:S(2)}, u32[]{:S(2)}) collective-permute-start(f32[3,2048]{1,0:T(4,128)} %get-tuple-element.248), channel_id=1, source_target_pairs={{0,7},{1,6},{2,5},{3,4},{4,3},{5,2},{6,1},{7,0},{8,15},{9,14},{10,... | collective-permute-start | bytes 73736 | tf_op jit(solution)/shard_map/ppermute | solution.py:71
  363.4 27.6 %collective-permute-start.70 = (f32[3,2048]{1,0:T(4,128)}, f32[3,2048]{1,0:T(4,128)S(1)}, u32[]{:S(2)}, u32[]{:S(2)}) collective-permute-start(f32[3,2048]{1,0:T(4,128)} %get-tuple-element.248), channel_id=1, source_target_pairs={{0,5},{1,4},{2,7},{3,6},{4,1},{5,0},{6,3},{7,2},{8,13},{9,12},{10,... | collective-permute-start | bytes 73736 | tf_op jit(solution)/shard_map/ppermute | solution.py:71
  364.0 26.9 %collective-permute-start.68 = (f32[3,2048]{1,0:T(4,128)}, f32[3,2048]{1,0:T(4,128)S(1)}, u32[]{:S(2)}, u32[]{:S(2)}) collective-permute-start(f32[3,2048]{1,0:T(4,128)} %get-tuple-element.248), channel_id=1, source_target_pairs={{0,3},{1,2},{2,1},{3,0},{4,7},{5,6},{6,5},{7,4},{8,11},{9,10},{10,... | collective-permute-start | bytes 73736 | tf_op jit(solution)/shard_map/ppermute | solution.py:71
  364.2 21.7 %collective-permute-start.66 = (f32[3,2048]{1,0:T(4,128)}, f32[3,2048]{1,0:T(4,128)S(1)}, u32[]{:S(2)}, u32[]{:S(2)}) collective-permute-start(f32[3,2048]{1,0:T(4,128)} %get-tuple-element.248), channel_id=1, source_target_pairs={{0,1},{1,0},{2,3},{3,2},{4,5},{5,4},{6,7},{7,6},{8,9},{9,8},{10,11... | collective-permute-start | bytes 73736 | tf_op jit(solution)/shard_map/ppermute | solution.py:71
  397.1 25.0 %collective-permute-start.73 = (bf16[256,768]{1,0:T(8,128)(2,1)S(1)}, bf16[256,768]{1,0:T(8,128)(2,1)S(1)}, u32[]{:S(2)}, u32[]{:S(2)}) collective-permute-start(bf16[256,768]{1,0:T(8,128)(2,1)S(1)} %get-tuple-element.560), channel_id=1, source_target_pairs={{0,1},{1,0},{2,3},{3,2},{4,5},{5,4},{6,7},{7,6},{8,9},{9,8},{10,11... | collective-permute-start | bytes 1179656 | tf_op jit(solution)/shard_map/ppermute | solution.py:71
  397.1 24.9 %collective-permute-start.74 = (bf16[256,768]{1,0:T(8,128)(2,1)S(1)}, bf16[256,768]{1,0:T(8,128)(2,1)S(1)}, u32[]{:S(2)}, u32[]{:S(2)}) collective-permute-start(bf16[256,768]{1,0:T(8,128)(2,1)S(1)} %get-tuple-element.559), channel_id=1, source_target_pairs={{0,1},{1,0},{2,3},{3,2},{4,5},{5,4},{6,7},{7,6},{8,9},{9,8},{10,11... | collective-permute-start | bytes 1179656 | tf_op jit(solution)/shard_map/ppermute | solution.py:71
  397.6 24.5 %collective-permute-start.76 = (bf16[256,768]{1,0:T(8,128)(2,1)S(1)}, bf16[256,768]{1,0:T(8,128)(2,1)S(1)}, u32[]{:S(2)}, u32[]{:S(2)}) collective-permute-start(bf16[256,768]{1,0:T(8,128)(2,1)S(1)} %get-tuple-element.558), channel_id=1, source_target_pairs={{0,1},{1,0},{2,3},{3,2},{4,5},{5,4},{6,7},{7,6},{8,9},{9,8},{10,11... | collective-permute-start | bytes 1179656 | tf_op jit(solution)/shard_map/ppermute | solution.py:71
  397.7 24.4 %collective-permute-start.77 = (bf16[256,768]{1,0:T(8,128)(2,1)S(1)}, bf16[256,768]{1,0:T(8,128)(2,1)S(1)}, u32[]{:S(2)}, u32[]{:S(2)}) collective-permute-start(bf16[256,768]{1,0:T(8,128)(2,1)S(1)} %get-tuple-element.557), channel_id=1, source_target_pairs={{0,1},{1,0},{2,3},{3,2},{4,5},{5,4},{6,7},{7,6},{8,9},{9,8},{10,11... | collective-permute-start | bytes 1179656 | tf_op jit(solution)/shard_map/ppermute | solution.py:71
  429.1 292.0 %reduce-scatter.5.cloned.1.call-start = ((), (), s32[]{:S(2)}) async-start(), calls=%async_computation.4 | async-start | bytes 11796480 | tf_op jit(solution)/shard_map/reduce_scatter | solution.py:177
  453.2 17.0 %collective-permute-start.87 = (bf16[128,768]{1,0:T(8,128)(2,1)S(1)}, bf16[128,768]{1,0:T(8,128)(2,1)S(1)}, u32[]{:S(2)}, u32[]{:S(2)}) collective-permute-start(bf16[128,768]{1,0:T(8,128)(2,1)S(1)} %get-tuple-element.581), channel_id=1, source_target_pairs={{0,5},{1,4},{2,7},{3,6},{4,1},{5,0},{6,3},{7,2},{8,13},{9,12},{10,... | collective-permute-start | bytes 589832 | tf_op jit(solution)/shard_map/ppermute | solution.py:71
  499.5 25.1 %collective-permute-start.90 = (bf16[128,768]{1,0:T(8,128)(2,1)}, bf16[128,768]{1,0:T(8,128)(2,1)}, u32[]{:S(2)}, u32[]{:S(2)}) collective-permute-start(bf16[128,768]{1,0:T(8,128)(2,1)} %get-tuple-element.577), channel_id=1, source_target_pairs={{0,1},{1,0},{2,3},{3,2},{4,5},{5,4},{6,7},{7,6},{8,9},{9,8},{10,11... | collective-permute-start | bytes 589832 | tf_op jit(solution)/shard_map/ppermute | solution.py:71
  500.4 26.6 %collective-permute-start.91 = (bf16[128,768]{1,0:T(8,128)(2,1)}, bf16[128,768]{1,0:T(8,128)(2,1)}, u32[]{:S(2)}, u32[]{:S(2)}) collective-permute-start(bf16[128,768]{1,0:T(8,128)(2,1)} %get-tuple-element.576), channel_id=1, source_target_pairs={{0,2},{1,3},{2,0},{3,1},{4,6},{5,7},{6,4},{7,5},{8,10},{9,11},{10,... | collective-permute-start | bytes 589832 | tf_op jit(solution)/shard_map/ppermute | solution.py:71
  501.8 27.1 %collective-permute-start.92 = (bf16[128,768]{1,0:T(8,128)(2,1)}, bf16[128,768]{1,0:T(8,128)(2,1)}, u32[]{:S(2)}, u32[]{:S(2)}) collective-permute-start(bf16[128,768]{1,0:T(8,128)(2,1)} %get-tuple-element.575), channel_id=1, source_target_pairs={{0,3},{1,2},{2,1},{3,0},{4,7},{5,6},{6,5},{7,4},{8,11},{9,10},{10,... | collective-permute-start | bytes 589832 | tf_op jit(solution)/shard_map/ppermute | solution.py:71
  501.8 28.1 %collective-permute-start.93 = (bf16[128,768]{1,0:T(8,128)(2,1)}, bf16[128,768]{1,0:T(8,128)(2,1)}, u32[]{:S(2)}, u32[]{:S(2)}) collective-permute-start(bf16[128,768]{1,0:T(8,128)(2,1)} %get-tuple-element.574), channel_id=1, source_target_pairs={{0,4},{1,5},{2,6},{3,7},{4,0},{5,1},{6,2},{7,3},{8,12},{9,13},{10,... | collective-permute-start | bytes 589832 | tf_op jit(solution)/shard_map/ppermute | solution.py:71
  573.8 19.8 %collective-permute-start.100 = (bf16[256,768]{1,0:T(8,128)(2,1)S(1)}, bf16[256,768]{1,0:T(8,128)(2,1)S(1)}, u32[]{:S(2)}, u32[]{:S(2)}) collective-permute-start(bf16[256,768]{1,0:T(8,128)(2,1)S(1)} %get-tuple-element.550), channel_id=1, source_target_pairs={{0,1},{1,0},{2,3},{3,2},{4,5},{5,4},{6,7},{7,6},{8,9},{9,8},{10,11... | collective-permute-start | bytes 1179656 | tf_op jit(solution)/shard_map/ppermute | solution.py:71
  574.2 19.6 %collective-permute-start.101 = (bf16[256,768]{1,0:T(8,128)(2,1)S(1)}, bf16[256,768]{1,0:T(8,128)(2,1)S(1)}, u32[]{:S(2)}, u32[]{:S(2)}) collective-permute-start(bf16[256,768]{1,0:T(8,128)(2,1)S(1)} %get-tuple-element.549), channel_id=1, source_target_pairs={{0,1},{1,0},{2,3},{3,2},{4,5},{5,4},{6,7},{7,6},{8,9},{9,8},{10,11... | collective-permute-start | bytes 1179656 | tf_op jit(solution)/shard_map/ppermute | solution.py:71
  574.3 19.8 %collective-permute-start.97 = (bf16[256,768]{1,0:T(8,128)(2,1)S(1)}, bf16[256,768]{1,0:T(8,128)(2,1)S(1)}, u32[]{:S(2)}, u32[]{:S(2)}) collective-permute-start(bf16[256,768]{1,0:T(8,128)(2,1)S(1)} %get-tuple-element.552), channel_id=1, source_target_pairs={{0,1},{1,0},{2,3},{3,2},{4,5},{5,4},{6,7},{7,6},{8,9},{9,8},{10,11... | collective-permute-start | bytes 1179656 | tf_op jit(solution)/shard_map/ppermute | solution.py:71
  611.3 16.9 %collective-permute-start.121 = (bf16[384,384]{1,0:T(8,128)(2,1)S(1)}, bf16[384,384]{1,0:T(8,128)(2,1)S(1)}, u32[]{:S(2)}, u32[]{:S(2)}) collective-permute-start(bf16[384,384]{1,0:T(8,128)(2,1)S(1)} %slice.1387), channel_id=1, source_target_pairs={{0,2},{1,3},{2,0},{3,1},{4,6},{5,7},{6,4},{7,5},{8,10},{9,11},{10,... | collective-permute-start | bytes 884744 | tf_op jit(solution)/shard_map/ppermute | solution.py:71
  624.8 17.2 %collective-permute-start.107 = (bf16[256,768]{1,0:T(8,128)(2,1)S(1)}, bf16[256,768]{1,0:T(8,128)(2,1)S(1)}, u32[]{:S(2)}, u32[]{:S(2)}) collective-permute-start(bf16[256,768]{1,0:T(8,128)(2,1)S(1)} %get-tuple-element.516), channel_id=1, source_target_pairs={{0,1},{1,0},{2,3},{3,2},{4,5},{5,4},{6,7},{7,6},{8,9},{9,8},{10,11... | collective-permute-start | bytes 1179656 | tf_op jit(solution)/shard_map/ppermute | solution.py:71
  635.7 31.5 %collective-permute-start.131 = (bf16[192,384]{1,0:T(8,128)(2,1)S(1)}, bf16[192,384]{1,0:T(8,128)(2,1)S(1)}, u32[]{:S(2)}, u32[]{:S(2)}) collective-permute-start(bf16[192,384]{1,0:T(8,128)(2,1)S(1)} %get-tuple-element.622), channel_id=1, source_target_pairs={{0,24},{8,0},{16,8},{24,16},{1,25},{9,1},{17,9},{25,17},{2,26},{10... | collective-permute-start | bytes 442376 | tf_op jit(solution)/shard_map/ppermute | solution.py:76
  662.1 26.6 %collective-permute-start.117 = (bf16[128,768]{1,0:T(8,128)(2,1)S(1)}, bf16[128,768]{1,0:T(8,128)(2,1)S(1)}, u32[]{:S(2)}, u32[]{:S(2)}) collective-permute-start(bf16[128,768]{1,0:T(8,128)(2,1)S(1)} %get-tuple-element.609), channel_id=1, source_target_pairs={{0,16},{8,24},{16,0},{24,8},{1,17},{9,25},{17,1},{25,9},{2,18},{10... | collective-permute-start | bytes 589832 | tf_op jit(solution)/shard_map/ppermute | solution.py:76
  664.2 24.5 %collective-permute-start.118 = (bf16[128,768]{1,0:T(8,128)(2,1)S(1)}, bf16[128,768]{1,0:T(8,128)(2,1)S(1)}, u32[]{:S(2)}, u32[]{:S(2)}) collective-permute-start(bf16[128,768]{1,0:T(8,128)(2,1)S(1)} %get-tuple-element.608), channel_id=1, source_target_pairs={{0,24},{8,0},{16,8},{24,16},{1,25},{9,1},{17,9},{25,17},{2,26},{10... | collective-permute-start | bytes 589832 | tf_op jit(solution)/shard_map/ppermute | solution.py:76
  668.6 57.5 %collective-permute-start.140 = (bf16[192,384]{1,0:T(8,128)(2,1)}, bf16[192,384]{1,0:T(8,128)(2,1)}, u32[]{:S(2)}, u32[]{:S(2)}) collective-permute-start(bf16[192,384]{1,0:T(8,128)(2,1)} %get-tuple-element.605.refs_0_), channel_id=1, source_target_pairs={{0,2},{1,3},{2,0},{3,1},{4,6},{5,7},{6,4},{7,5},{8,10},{9,11},{10,... | collective-permute-start | bytes 442376 | tf_op jit(solution)/shard_map/ppermute | solution.py:71
  669.5 59.0 %collective-permute-start.142 = (bf16[192,384]{1,0:T(8,128)(2,1)}, bf16[192,384]{1,0:T(8,128)(2,1)}, u32[]{:S(2)}, u32[]{:S(2)}) collective-permute-start(bf16[192,384]{1,0:T(8,128)(2,1)} %get-tuple-element.605.refs_0_), channel_id=1, source_target_pairs={{0,4},{1,5},{2,6},{3,7},{4,0},{5,1},{6,2},{7,3},{8,12},{9,13},{10,... | collective-permute-start | bytes 442376 | tf_op jit(solution)/shard_map/ppermute | solution.py:71
  (212 other events, 2551.9 us)
Sparse Core Ops, SparseCore 0:
  17.5 197.1 all-gather.3
  216.8 111.1 all-gather.5
  429.2 105.8 reduce-scatter.2
  537.3 183.7 reduce-scatter.4

commit v3 on v2

--- a/solution.py
+++ b/solution.py
@@ -122,28 +122,34 @@
     return jnp.concatenate([piece for _, _, piece in gather_pieces(rows)])
 
 
-def sum_blocks(blocks, earlier=None):
+def sum_blocks(blocks, firsts=None):
     if not quick_expert():
         return lax.psum_scatter(
             jnp.stack(blocks), "expert", scatter_dimension=0, tiled=False
         ).astype(F32)
     half = blocks[0].shape[0] // 2
-    other = [swap(blocks[j], 1, "expert") for j in (6 + 1, 2 + 1, 4 + 1, 1)]
-    other[0] = after(other[0], earlier)
-    six = (blocks[6].astype(F32) + other[0].astype(F32)).astype(BF)
-    two = blocks[2].astype(F32) + other[1].astype(F32)
-    four = blocks[4].astype(F32) + other[2].astype(F32)
-    six_a = swap(six[:half], 2, "expert")
-    six_b = swap(six[half:], 4, "expert")
-    two_a = swap(two[:half].astype(BF), 2, "expert")
-    four_b = swap(four[half:].astype(BF), 4, "expert")
-    four_a = swap((four[:half] + six_a.astype(F32)).astype(BF), 4, "expert")
-    two_b = swap((two[half:] + six_b.astype(F32)).astype(BF), 2, "expert")
-    mine = blocks[0].astype(F32) + other[3].astype(F32)
-    return jnp.concatenate(
+    width = blocks[0].shape[1]
+    other = [swap(blocks[j], 1, "expert") for j in (7, 3, 5, 1)]
+    piece, piece_f = (jax.ShapeDtypeStruct((half, width), t) for t in (BF, F32))
+    six_a, six_b, two_a, four_b, two_f, four_f, mine = whole_call(
+        first_sum_kernel,
+        [piece] * 4 + [piece_f] * 2 + [jax.ShapeDtypeStruct((2 * half, width), F32)],
+        "first_sum",
+        *[blocks[j] for j in (6, 2, 4, 0)],
+        *other,
+    )
+    if firsts is not None:
+        firsts.append((six_a, two_a))
+    six_a = swap(six_a, 2, "expert")
+    six_b = swap(six_b, 4, "expert")
+    two_a = swap(two_a, 2, "expert")
+    four_b = swap(four_b, 4, "expert")
+    four_a = swap((four_f + six_a.astype(F32)).astype(BF), 4, "expert")
+    two_b = swap((two_f + six_b.astype(F32)).astype(BF), 2, "expert")
+    return mine + jnp.concatenate(
         [
-            mine[:half] + two_a.astype(F32) + four_a.astype(F32),
-            mine[half:] + two_b.astype(F32) + four_b.astype(F32),
+            two_a.astype(F32) + four_a.astype(F32),
+            two_b.astype(F32) + four_b.astype(F32),
         ]
     )
 
@@ -174,7 +180,7 @@
 
 
 def sum_shards(parts):
-    return lax.psum_scatter(parts, "dp", scatter_dimension=0, tiled=False).astype(F32)
+    return lax.psum_scatter(parts, "dp", scatter_dimension=0, tiled=False)
 
 
 def sum_everywhere(array):
@@ -325,6 +331,20 @@
     )(queries, keys, values, grad_out, mixed, lse, key_place, query_place)
 
 
+def first_sum_kernel(
+    six_ref, two_ref, four_ref, own_ref, six_o, two_o, four_o, own_o, six_a, six_b, two_a,
+    four_b, two_f, four_f, mine
+):
+    half = six_a.shape[0]
+    six = (six_ref[...].astype(F32) + six_o[...].astype(F32)).astype(BF)
+    six_a[...], six_b[...] = six[:half], six[half:]
+    two = two_ref[...].astype(F32) + two_o[...].astype(F32)
+    two_a[...], two_f[...] = two[:half].astype(BF), two[half:]
+    four = four_ref[...].astype(F32) + four_o[...].astype(F32)
+    four_f[...], four_b[...] = four[:half], four[half:].astype(BF)
+    mine[...] = own_ref[...].astype(F32) + own_o[...].astype(F32)
+
+
 def place_kernel(spots, member_ref, *refs):
     pieces, out_ref = refs[: len(spots)], refs[len(spots)]
     half = out_ref.shape[2] // 2
@@ -430,9 +450,8 @@
     return (word == lanes).astype(BF)
 
 
-def stats_kernel(
-    capacity, rounds_ref, rank_ref, word_ref, heads_ref, rows_ref, sums_ref, out_ref, stats_ref,
-    ratio_ref
+def wanted_kernel(
+    capacity, rounds_ref, rank_ref, word_ref, heads_ref, out_ref
 ):
     count, words, _ = heads_ref.shape
 
@@ -450,18 +469,71 @@
     def _(turn_no):
         out_ref[...] = (out_ref[...].astype(F32) + wanted(turn_no)).astype(BF)
 
-    product = rows_ref[...].astype(F32) * out_ref[...].astype(F32)
+
+def picked_kernel(rows_ref, wanted_ref, picked_ref):
+    product = rows_ref[...].astype(F32) * wanted_ref[...].astype(F32)
     high = product.astype(BF)
     low = (product - high.astype(F32)).astype(BF)
     ones = jnp.ones((8, product.shape[1]), BF)
     picked = dot_nt(ones, high) + dot_nt(ones, low)
+    picked_ref[...] = picked[0:1, :]
+
+
+def stats_kernel(sums_ref, out_ref):
+    count = sums_ref.shape[0] // 2
     tops = sums_ref[:count, :]
     top = jnp.max(tops, axis=0, keepdims=True)
-    ratio = jnp.exp(tops - top)
-    ratio_ref[...] = ratio
-    stats_ref[0:1, :] = top
-    stats_ref[1:2, :] = jnp.sum(sums_ref[count:, :] * ratio, axis=0, keepdims=True)
-    stats_ref[2:3, :] = picked[0:1, :]
+    out_ref[0:1, :] = top
+    out_ref[1:2, :] = jnp.sum(sums_ref[count:, :] * jnp.exp(tops - top), axis=0, keepdims=True)
+
+
+def scale_kernel(orders, sums_ref, weight_ref, *refs):
+    count = sums_ref.shape[0] // 2
+    stats, logsum_ref, columns_ref = refs[: len(orders)], refs[-2], refs[-1]
+    length = sums_ref.shape[1] // len(orders)
+    tops, sums = [], []
+    for ref, order in zip(stats, orders):
+        pieces = [ref[:, j * length : (j + 1) * length] for j in order]
+        together = jnp.concatenate(pieces, axis=1)
+        tops.append(together[0:1, :])
+        sums.append(together[1:2, :])
+    top = functools.reduce(jnp.maximum, tops)
+    total = sum(s * jnp.exp(t - top) for s, t in zip(sums, tops))
+    logsum = top + jnp.log(total)
+    logsum_ref[...] = logsum
+    weight = weight_ref[...]
+    scales = weight * jnp.exp(sums_ref[:count, :] - logsum)
+    rest = columns_ref.shape[1] - count - 1
+    columns_ref[...] = jnp.transpose(
+        jnp.concatenate([scales, weight, jnp.zeros((rest, weight.shape[1]), F32)], axis=0)
+    )
+
+
+def head_weight_kernel(exps_ref, rows_ref, columns_ref, terms_ref, out_ref):
+    lanes = lax.broadcasted_iota(jnp.int32, columns_ref.shape, 1)
+    mine = jnp.where(lanes == pl.program_id(0), columns_ref[...], 0.0)
+    scaled = (rows_ref[...].astype(F32) * jnp.sum(mine, axis=1, keepdims=True)).astype(BF)
+    out_ref[0] = (dot_nn(exps_ref[0], scaled) - terms_ref[0].astype(F32)).astype(BF)
+
+
+def head_weight_back(exps, rows, columns, terms):
+    count, depth, group = exps.shape
+    width = rows.shape[1]
+    return pl.pallas_call(
+        head_weight_kernel,
+        grid=(count,),
+        in_specs=[
+            pl.BlockSpec((1, depth, group), lambda i: (i, 0, 0)),
+            pl.BlockSpec((group, width), lambda i: (0, 0)),
+            pl.BlockSpec(columns.shape, lambda i: (0, 0)),
+            pl.BlockSpec((1, depth, width), lambda i: (i, 0, 0)),
+        ],
+        out_specs=pl.BlockSpec((1, depth, width), lambda i: (i, 0, 0)),
+        out_shape=jax.ShapeDtypeStruct((count, depth, width), BF),
+        compiler_params=params(),
+        cost_estimate=cost(2 * group * width * depth * count),
+        name="head_weight_back",
+    )(exps, rows, columns, terms)
 
 
 def target_kernel(capacity, rounds_ref, rank_ref, word_ref, weight_ref, rows_ref, out_ref):
@@ -484,9 +556,10 @@
 
 def whole_call(kernel, out_shape, name, *arrays):
     vmem = pl.BlockSpec(memory_space=pltpu.VMEM)
+    smem = pl.BlockSpec(memory_space=pltpu.SMEM)
     return pl.pallas_call(
         kernel,
-        in_specs=[pl.BlockSpec(memory_space=pltpu.SMEM)] + [vmem] * (len(arrays) - 1),
+        in_specs=[smem if a.dtype == jnp.int32 else vmem for a in arrays],
         out_specs=jax.tree.map(lambda _: vmem, out_shape),
         out_shape=out_shape,
         compiler_params=pltpu.CompilerParams(vmem_limit_bytes=VMEM_BYTES),
@@ -495,33 +568,34 @@
     )(*arrays)
 
 
-def head_rows_kernel(coef_ref, heads_ref, exps_ref, out_ref):
-    coef = jnp.transpose(coef_ref[...])
-    out = None
-    for k in range(heads_ref.shape[0]):
-        term = dot_tn(exps_ref[k], heads_ref[k]) * coef[:, k : k + 1]
-        out = term if out is None else out + term
+def head_rows_kernel(columns_ref, wanted_ref, heads_ref, exps_ref, out_ref):
+    count = heads_ref.shape[0]
+    out = wanted_ref[...].astype(F32) * (-columns_ref[:, count : count + 1])
+    for k in range(count):
+        out = out + dot_tn(exps_ref[k], heads_ref[k]) * columns_ref[:, k : k + 1]
     out_ref[...] = out.astype(BF)
 
 
-def head_rows_back(coef, heads, exps):
+def head_rows_back(columns, wanted, heads, exps):
     count, depth, width = heads.shape
     group = exps.shape[2]
     block = min(256, group)
+    rows = pl.BlockSpec((block, width), lambda i: (i, 0))
     return pl.pallas_call(
         head_rows_kernel,
         grid=(group // block,),
         in_specs=[
-            pl.BlockSpec((count, block), lambda i: (0, i)),
+            pl.BlockSpec((block, columns.shape[1]), lambda i: (i, 0)),
+            rows,
             pl.BlockSpec((count, depth, width), lambda i: (0, 0, 0)),
             pl.BlockSpec((count, depth, block), lambda i: (0, 0, i)),
         ],
-        out_specs=pl.BlockSpec((block, width), lambda i: (i, 0)),
+        out_specs=rows,
         out_shape=jax.ShapeDtypeStruct((group, width), BF),
         compiler_params=params(),
         cost_estimate=cost(2 * group * width * depth * count),
         name="head_rows_back",
-    )(coef, heads, exps)
+    )(columns, wanted, heads, exps)
 
 
 def ranks(hits):
@@ -582,14 +656,15 @@
             (member // 2, 0, (member % 2) * (width // 2)),
             (1, attn.shape[1], width // 2),
         )[0]
-        attn_parts = jnp.stack([mine] + [turn(mine, k) for k in range(1, 4)])
+        below, above = turn(mine, 1), turn(mine, -1)
+        attn_parts = jnp.stack([mine, below, turn(below, 1), above])
         attn_parts = attn_parts[slot_shards()].reshape(width, width // 2)
         attn_pieces = gather_pieces(attn_parts)
     table_b = tables[0].astype(BF)
     experts_b = experts[0].astype(BF)
     head_b = tables[1].astype(BF)
 
-    capacity = min(group, 2 * (-(-group // (shards * rows_dp))))
+    capacity = min(group, 3 * group // (2 * shards * rows_dp))
     capacity = -(-capacity // 16) * 16
     ids_dp = jnp.stack([ids] + [turn(ids, k) for k in range(1, rows_dp)])
     first_word = (member * rows_dp + batch_row) * words
@@ -700,8 +775,9 @@
     slot_gates = jnp.sum(gate_table, axis=2).reshape(-1, 1)
     gate_high, gate_low = split_high_low(gate_table.reshape(-1, local))
     send = dot_nn(hot_b, normed_bb).astype(BF)
-    received = jnp.concatenate(exchange(split_blocks(send)))
-    head_shards = lax.all_gather(after(head_b, expert_shards), "dp")
+    received = exchange(split_blocks(send))
+    head_shards = lax.all_gather(after(head_b, (expert_shards, received[1])), "dp")
+    received = jnp.concatenate(received)
     pres, hiddens, produced = [], [], None
     for shard in expert_shards:
         pre = dot_nn(received, shard[0])
@@ -726,59 +802,52 @@
         token_weight[None, :],
         rows_all,
     )
-    exps, head_stats = head_forward(rows_all, head_shards)
-    tops = head_stats[:rows_dp]
-    wanted, stats, ratios = whole_call(
-        functools.partial(stats_kernel, capacity),
-        (
-            jax.ShapeDtypeStruct((group, width), BF),
-            jax.ShapeDtypeStruct((3, group), F32),
-            jax.ShapeDtypeStruct((rows_dp, group), F32),
-        ),
-        "target_stats",
+    exps, head_stats = head_forward(after(rows_all, target_terms), head_shards)
+    stats = whole_call(
+        stats_kernel, jax.ShapeDtypeStruct((2, group), F32), "head_stats", head_stats
+    )
+    if quick_expert():
+        gathered = [stats] + [swap(stats, k, "expert") for k in range(1, 8)]
+        orders = [[j ^ k for j in range(8)] for k in range(8)]
+    else:
+        gathered = list(lax.all_gather(stats, "expert"))
+        orders = [list(range(shards))] * shards
+    wanted = whole_call(
+        functools.partial(wanted_kernel, capacity),
+        jax.ShapeDtypeStruct((group, width), BF),
+        "wanted_rows",
         word_rounds,
         word_rank,
         word_row,
         head_shards,
-        rows_all,
+    )
+    logsum_tok, columns = whole_call(
+        functools.partial(scale_kernel, orders),
+        (
+            jax.ShapeDtypeStruct((1, group), F32),
+            jax.ShapeDtypeStruct((group, -(-(rows_dp + 1) // 8) * 8), F32),
+        ),
+        "head_scales",
         head_stats,
-    )
-    top_here = stats[0]
-    if quick_expert():
-        gathered = [stats]
-        for k in range(1, 8):
-            other = swap(stats, k, "expert")
-            gathered.append(
-                jnp.concatenate([other[:, (j ^ k) * local : (j ^ k) * local + local] for j in range(8)], axis=1)
-            )
-        gathered = jnp.stack(gathered)
-    else:
-        gathered = lax.all_gather(stats, "expert")
-    top = jnp.max(gathered[:, 0], axis=0)
-    total = jnp.sum(gathered[:, 1] * jnp.exp(gathered[:, 0] - top[None, :]), axis=0)
-    logsum_tok = top + jnp.log(total)
-    loss_tok = logsum_tok - jnp.sum(gathered[:, 2], axis=0)
+        token_weight[None, :],
+        *gathered,
+    )
     own_block = 0 if quick_expert() else member
+    grad_rows_c = head_rows_back(columns, wanted, head_shards, exps)
+    grad_heads = head_weight_back(exps, rows_all, columns, target_terms)
+    grad_head = sum_shards(grad_heads)
+    picked = whole_call(
+        picked_kernel,
+        jax.ShapeDtypeStruct((1, group), F32),
+        "picked_logits",
+        after(rows_all, grad_heads),
+        wanted,
+    )
     own_sums = jnp.sum(
         lax.dynamic_slice_in_dim(group_hits, own_block * local, local, 0)
-        * lax.dynamic_slice_in_dim(loss_tok, own_block * local, local, 0)[:, None],
+        * lax.dynamic_slice_in_dim(logsum_tok[0], own_block * local, local, 0)[:, None],
         axis=0,
-    )
-    spread_rows = head_rows_back(ratios, head_shards, exps)
-    scales = token_weight[None, :] * jnp.exp(tops - logsum_tok[None, :])
-    scale_here = token_weight * jnp.exp(top_here - logsum_tok)
-    grad_heads = [
-        (
-            dot_nn(exps[k], (rows_all.astype(F32) * scales[k][:, None]).astype(BF))
-            - target_terms[k].astype(F32)
-        ).astype(BF)
-        for k in range(rows_dp)
-    ]
-    grad_head = sum_shards(jnp.stack(grad_heads))
-    grad_rows_c = (
-        spread_rows.astype(F32) * scale_here[:, None]
-        - wanted.astype(F32) * token_weight[:, None]
-    ).astype(BF)
+    ) - jnp.sum(group_hits * picked[0][:, None], axis=0)
     grad_normed_c = sum_blocks(split_blocks(grad_rows_c))
     grad_two, grad_gain_c = norm_back(resid_two, gains[2], grad_normed_c)
 
@@ -788,18 +857,22 @@
     grad_produced = jnp.concatenate(
         exchange(split_blocks((grad_slot * slot_gates).astype(BF)))
     )
-    grad_parts, grad_sent = [], None
+    grad_pres, grad_sent = [], None
     for k in range(rows_dp):
         grad_hidden = dot_nn(grad_produced, expert_shards[k, 1])
         _, gelu_pull = jax.vjp(gelu, pres[k])
-        grad_pre = gelu_pull(grad_hidden)[0].astype(BF)
-        grad_parts.append(dot_tn(received, grad_pre).astype(BF))
-        grad_parts.append(dot_tn(grad_produced, hiddens[k]).astype(BF))
-        term = dot_nt(grad_pre, expert_shards[k, 0])
+        grad_pres.append(gelu_pull(grad_hidden)[0].astype(BF))
+        term = dot_nt(grad_pres[k], expert_shards[k, 0])
         grad_sent = term if grad_sent is None else grad_sent + term
+    grad_sent = grad_sent.astype(BF)
+    late_produced, late_received = after((grad_produced, received), grad_sent)
+    grad_parts = []
+    for grad_pre, hidden in zip(grad_pres, hiddens):
+        grad_parts.append(dot_tn(late_received, grad_pre).astype(BF))
+        grad_parts.append(dot_tn(late_produced, hidden).astype(BF))
     grad_parts = jnp.stack(grad_parts).reshape(rows_dp, 2, width, -1)
     grad_experts = sum_shards(grad_parts)[None]
-    grad_back = jnp.concatenate(exchange(split_blocks(grad_sent.astype(BF))))
+    grad_back = jnp.concatenate(exchange(split_blocks(grad_sent)))
     grad_normed_b = dot_tn(hot_b, grad_back)
     grad_gates = jnp.sum(
         jnp.where(hot, grad_gate_slot.reshape(shards, slots)[:, :, None], 0.0), axis=1
@@ -818,7 +891,8 @@
         queries, keys, values, grad_mixed, mixed_b, logsum, key_place, query_place
     )
     grad_normed_rows = dot_nt(grad_keys, attn_full[1]) + dot_nt(grad_values, attn_full[2])
-    grad_normed_a = sum_blocks(split_blocks(grad_normed_rows.astype(BF)))
+    firsts = []
+    grad_normed_a = sum_blocks(split_blocks(grad_normed_rows.astype(BF)), firsts)
     grad_normed_a = grad_normed_a + dot_nt(grad_query, attn_full[0])
     normal_front, grad_gain_a = norm_back(embedded, gains[0], grad_normed_a)
     grad_embedded = (grad_one + normal_front).astype(BF)
@@ -842,18 +916,19 @@
         blocks = attn_weight_back(
             member,
             normed_ab,
-            normed_all,
+            after(normed_all, firsts[0]),
             mixed_b,
             grad_query,
             grad_keys,
             grad_values,
             grad_branch,
         )
+        blocks = after(blocks, grad_embedded_all)
         part = sum_blocks([blocks[j] for j in range(8)]).astype(BF)
         part = part.reshape(4, width // 4, width // 2)[slot_shards()]
         part = sum_turns([part[k] for k in range(4)])
         attn_squares = jnp.sum(part * part)
-        grad_attn = place_halves(member, gather_pieces(part.astype(BF))).astype(F32)
+        grad_attn = place_halves(member, gather_pieces(part.astype(BF)))
     else:
         grad_attn = jnp.stack(
             [
@@ -864,38 +939,35 @@
             ]
         ).astype(BF)
         grad_attn = lax.psum_scatter(grad_attn, "dp", scatter_dimension=1, tiled=True)
-        grad_attn = lax.psum(grad_attn, "expert").astype(F32)
-        attn_squares = jnp.sum(grad_attn * grad_attn) / shards
-    squares = (
-        jnp.sum(grad_embed * grad_embed)
-        + jnp.sum(grad_head * grad_head)
-        + jnp.sum(grad_experts * grad_experts)
-        + attn_squares
-    )
+        grad_attn = lax.psum(grad_attn, "expert")
+        attn_squares = jnp.sum(jnp.square(grad_attn.astype(F32))) / shards
     small = jnp.concatenate(
-        [
-            grad_router.reshape(-1),
-            grad_gain_a,
-            grad_gain_b,
-            grad_gain_c,
-            own_sums,
-            squares[None],
-        ]
-    )
+        [grad_router.reshape(-1), grad_gain_a, grad_gain_b, grad_gain_c, own_sums]
+    )
+    small = after(small, grad_embedded_all)
     small = jnp.pad(small, (0, -small.shape[0] % 1024)).reshape(-1, 128)
     small = sum_everywhere(small).reshape(-1)
     edge = router.size
     grad_router = small[:edge].reshape(router.shape)
     grad_gains = small[edge : edge + 3 * width].reshape(3, width)
     domain_sums = small[edge + 3 * width : edge + 3 * width + NDOM]
-    squares = small[edge + 3 * width + NDOM]
-    grad_norm = jnp.sqrt(
-        squares + jnp.sum(grad_router * grad_router) + jnp.sum(grad_gains * grad_gains)
-    )
+    small_squares = jnp.sum(grad_router * grad_router) + jnp.sum(grad_gains * grad_gains)
+    grad_head = grad_head.astype(F32)
+    head_squares = jnp.sum(grad_head * grad_head)
+    grad_experts = after(grad_experts, (small, small_squares, grad_head, head_squares))
+    grad_experts = grad_experts.astype(F32)
+    squares = (
+        jnp.sum(grad_embed * grad_embed)
+        + head_squares
+        + jnp.sum(grad_experts * grad_experts)
+        + attn_squares
+    )
+    squares = sum_everywhere(jnp.broadcast_to(squares, (1, 128)))[0, 0]
+    grad_norm = jnp.sqrt(squares + small_squares)
     factor = jnp.minimum(1.0, CLIP / (grad_norm + 1e-06))
     grad_tables = jnp.stack([grad_embed, grad_head])
     tables_out = adam(tables, grad_tables * factor, tables_m, tables_v, 0.1, 0.01)
-    attn_out = adam(attn, grad_attn * factor, attn_m, attn_v, 0.1, 0.01)
+    attn_out = adam(attn, grad_attn.astype(F32) * factor, attn_m, attn_v, 0.1, 0.01)
     experts_out = adam(experts, grad_experts * factor, experts_m, experts_v, 0.1, 0.01)
     router_out = adam(router, grad_router * factor, router_m, router_v, 0.04, 0.01)
     gains_out = adam(gains, grad_gains * factor, gains_m, gains_v, 0.4, 0.0)

time: 810 us -> 799 us (0.986)
  Pallas kernels: 124 us -> 165 us
  matrix products: 127 us -> 104 us
  starting transfers between devices: 148 us -> 130 us
  other arithmetic: 93.6 us -> 83.3 us
    ppermute x127 -> x134, waiting for transfers between devices: 101 us -> 143 us  [swap(): return lax.ppermute(array, axis, pairs)]
    pallas_call x2 -> x10, Pallas kernels: 18.3 us -> 59.4 us  [the longest x9 40.3 us: whole_call(): pl.pallas_call(kernel, in_specs=[smem if a.dtype == jnp.int32 else vmem f...]
    reduce_scatter x2, waiting for transfers between devices: 25.7 us -> 0.02 us  [sum_shards(): return lax.psum_scatter(parts, 'dp', scatter_dimension=0, tiled=False)]
    dot_general x49 -> x45, matrix products: 127 us -> 104 us  [dot(): lax.dot_general(a, b, ((contract[0], contract[1]), ((), ())), preferred_e...]
    ppermute x15, starting transfers between devices: 41 us -> 29 us  [turn(): lax.ppermute(array, 'dp', [(i, (i + steps) % count) for i in range(count)])]
    ppermute x127 -> x134, starting transfers between devices: 106 us -> 100 us  [swap(): return lax.ppermute(array, axis, pairs)]
    unnamed x317 -> x324, local copies, waits for them, and re-layouts: 42.1 us -> 44.4 us
  transfers between devices with their start and end apart: 146 -> 153, of which waited for: 45 -> 54; matrix products, arithmetic and copies ran while one was open for 31% -> 28% of each run, Pallas kernels for 11% -> 15%
where the time goes in v3:
time: 799 us; the launch traced here: 788 us
  waiting for transfers between devices  200 us (25%)
  Pallas kernels  165 us (21%)
  starting transfers between devices  130 us (16%)
  matrix products  104 us (13%)
  other arithmetic  83.3 us (10%)
  local copies, waits for them, and re-layouts  82.1 us (10%)
  between operations  23.2 us (3%)
    ppermute x134, waiting for transfers between devices, swap(): return lax.ppermute(array, axis, pairs)  143 us
    dot_general x45, matrix products, dot(): lax.dot_general(a, b, ((contract[0], contract[1]), ((), ())), preferred_e...  104 us
    ppermute x134, starting transfers between devices, swap(): return lax.ppermute(array, axis, pairs)  100 us
    ppermute x15, waiting for transfers between devices, turn(): lax.ppermute(array, 'dp', [(i, (i + steps) % count) for i in range(count)])  47.4 us
    unnamed x324, local copies, waits for them, and re-layouts  44.4 us
    pallas_call x9, Pallas kernels, whole_call(): pl.pallas_call(kernel, in_specs=[smem if a.dtype == jnp.int32 else vmem f...  40.3 us
    convert_element_type x5, other arithmetic, adam(): return (first, second, weight, weight.astype(BF))  32.1 us
    ppermute x15, starting transfers between devices, turn(): lax.ppermute(array, 'dp', [(i, (i + steps) % count) for i in range(count)])  29 us
  transfers between devices with their start and end apart: 153, of which 54 were waited for; matrix products, arithmetic and copies ran while one was open for 28% of the time, Pallas kernels for 15%

profile of v3, /device:TPU:0, one launch (start us, length us, event | category | flops | bytes accessed | tf_op | source)
XLA Modules:
  0.0 788.5 jit_solution(11440711566666609847)
XLA Ops:
  7.3 4.1 collective-permute-start.7
  16.8 4.0 convert_element_type.419
  35.5 4.3 collective-permute-start.10
  41.2 5.9 collective-permute-done.11
  47.1 8.7 %collective-permute-done.10 = bf16[96,768]{1,0:T(8,128)(2,1)S(1)} collective-permute-done((bf16[96,768]{1,0:T(8,128)(2,1)S(1)}, bf16[96,768]{1,0:T(8,128)(2,1)S(1)}, u32[]{:S(2)}, u32[]{:S(2)}) %collective-permute-start.10) | collective-permute-done | bytes 147488 | tf_op jit(solution)/shard_map/ppermute | solution.py:76
  58.3 4.5 convolution_convert_fusion.4
  67.2 11.3 %collective-permute-start.24 = (bf16[192,384]{1,0:T(8,128)(2,1)}, bf16[192,384]{1,0:T(8,128)(2,1)}, u32[]{:S(2)}, u32[]{:S(2)}) collective-permute-start(bf16[192,384]{1,0:T(8,128)(2,1)} %fusion.255), channel_id=1, source_target_pairs={{0,24},{8,0},{16,8},{24,16},{1,25},{9,1},{17,9},{25,17},{2,26},{10... | collective-permute-start | bytes 442376 | tf_op jit(solution)/shard_map/ppermute | solution.py:76
  87.0 6.9 collective-permute-done.24
  102.7 13.6 %collective-permute-done.19 = bf16[128,768]{1,0:T(8,128)(2,1)S(1)} collective-permute-done((bf16[128,768]{1,0:T(8,128)(2,1)}, bf16[128,768]{1,0:T(8,128)(2,1)S(1)}, u32[]{:S(2)}, u32[]{:S(2)}) %collective-permute-start.19) | collective-permute-done | bytes 196640 | tf_op jit(solution)/shard_map/ppermute | solution.py:71
  133.5 5.3 collective-permute-done.37
  151.2 5.0 place_halves.2
  165.7 6.4 convolution_convert_fusion.2.v_ref
  172.0 4.0 convolution_convert_fusion.3.k_ref
  176.0 18.7 %attend.1 = (bf16[256,768]{1,0:T(8,128)(2,1)}, f32[12,256]{1,0:T(8,128)}) custom-call(bf16[256,768]{1,0:T(8,128)(2,1)} %convolution_convert_fusion.16.q_ref, bf16[2048,768]{1,0:T(8,128)(2,1)} %convolution_convert_fusion.3.k_ref, bf16[2048,768]{1,0:T(8,128)(2,1)} %convolution_convert_fusion.2.v_ref, s32[2048,1]{1,0:T(8,128)} %compare_select_fusion.kp_ref, ...), custom_call_target="tpu_custom_call" | custom-call | flops 1000 | bytes 2 | tf_op jit(solution)/shard_map/attend/pallas_call | solution.py:243
  202.8 5.2 all-gather.4.cloned.1.call-done
  211.0 7.2 collective-permute-done.44
  221.2 4.8 collective-permute-done.47
  232.1 4.0 fusion.94
  259.5 9.6 %collective-permute-done.52 = bf16[128,768]{1,0:T(8,128)(2,1)S(1)} collective-permute-done((bf16[128,768]{1,0:T(8,128)(2,1)}, bf16[128,768]{1,0:T(8,128)(2,1)S(1)}, u32[]{:S(2)}, u32[]{:S(2)}) %collective-permute-start.52) | collective-permute-done | bytes 196640 | tf_op jit(solution)/shard_map/ppermute | solution.py:71
  270.6 4.2 collective-permute-done.54
  279.1 9.7 %collective-permute-done.58 = bf16[256,768]{1,0:T(8,128)(2,1)} collective-permute-done((bf16[256,768]{1,0:T(8,128)(2,1)}, bf16[256,768]{1,0:T(8,128)(2,1)}, u32[]{:S(2)}, u32[]{:S(2)}) %collective-permute-start.58) | collective-permute-done | bytes 393248 | tf_op jit(solution)/shard_map/ppermute | solution.py:71
  308.2 9.0 %target_terms.1.terms_ref = bf16[4,1000,768]{2,1,0:T(8,128)(2,1)} custom-call(s32[1]{0:T(128)} %bitcast.37.rounds_ref, f32[4,2048]{1,0:T(4,128)} %bitcast.351, f32[1,2048]{1,0:T(1,128)} %fusion.150.word_ref, f32[1,2048]{1,0:T(1,128)} %bitcast.367, bf16[2048,768]{1,0:T(8,128)(2,1)} %constant_dynamic-update-slice_fusion.24.rows_ref), custom_call_target="tpu_custom_call" | custom-call | flops 1000 | bytes 2 | tf_op jit(solution)/shard_map/target_terms/pallas_call | solution.py:560
  317.2 4.2 all-gather.6.cloned.1.call-done
  321.3 23.9 %head_forward.1 = (bf16[4,1000,2048]{2,1,0:T(8,128)(2,1)}, f32[8,2048]{1,0:T(8,128)}) custom-call(bf16[2048,768]{1,0:T(8,128)(2,1)} %constant_dynamic-update-slice_fusion.24.rows_ref, bf16[4,1000,768]{2,1,0:T(8,128)(2,1)} %bitcast.331), custom_call_target="tpu_custom_call" | custom-call | flops 12582912000 | bytes 25165824 | tf_op jit(solution)/shard_map/head_forward/pallas_call | solution.py:418
  353.6 7.7 wanted_rows.1.wanted_ref
  364.9 19.9 %head_rows_back.1 = bf16[2048,768]{1,0:T(8,128)(2,1)} custom-call(f32[2048,8]{1,0:T(8,128)} %get-tuple-element.289.columns_ref, bf16[2048,768]{1,0:T(8,128)(2,1)} %wanted_rows.1.wanted_ref, bf16[4,1000,768]{2,1,0:T(8,128)(2,1)} %bitcast.333, bf16[4,1000,2048]{2,1,0:T(8,128)(2,1)} %get-tuple-element.290.exps_ref), custom_call_target="tpu_custom_call" | custom-call | flops 12582912000 | bytes 25165824 | tf_op jit(solution)/shard_map/head_rows_back/pallas_call | solution.py:584
  396.1 19.1 %head_weight_back.1 = bf16[4,1000,768]{2,1,0:T(8,128)(2,1)} custom-call(bf16[4,1000,2048]{2,1,0:T(8,128)(2,1)} %get-tuple-element.290.exps_ref, bf16[2048,768]{1,0:T(8,128)(2,1)} %constant_dynamic-update-slice_fusion.24.rows_ref, f32[2048,8]{1,0:T(8,128)} %get-tuple-element.289.columns_ref, bf16[4,1000,768]{2,1,0:T(8,128)(2,1)} %target_terms.1.terms_ref), custom_call_target="tpu_custom_call" | custom-call | flops 12582912000 | bytes 25165824 | tf_op jit(solution)/shard_map/head_weight_back/pallas_call | solution.py:522
  420.6 4.0 collective-permute-done.80
  426.5 5.4 collective-permute-done.79
  446.5 10.6 %collective-permute-done.85 = bf16[128,768]{1,0:T(8,128)(2,1)S(1)} collective-permute-done((bf16[128,768]{1,0:T(8,128)(2,1)S(1)}, bf16[128,768]{1,0:T(8,128)(2,1)S(1)}, u32[]{:S(2)}, u32[]{:S(2)}) %collective-permute-start.85) | collective-permute-done | bytes 196640 | tf_op jit(solution)/shard_map/ppermute | solution.py:71
  458.0 4.2 collective-permute-done.87
  462.2 4.5 fusion.34
  532.4 20.9 %attend_back.1 = (bf16[256,768]{1,0:T(8,128)(2,1)}, bf16[2048,768]{1,0:T(8,128)(2,1)}, bf16[2048,768]{1,0:T(8,128)(2,1)}) custom-call(bf16[256,768]{1,0:T(8,128)(2,1)} %convolution_convert_fusion.16.q_ref, bf16[2048,768]{1,0:T(8,128)(2,1)} %convolution_convert_fusion.3.k_ref, bf16[2048,768]{1,0:T(8,128)(2,1)} %convolution_convert_fusion.2.v_ref, ...), custom_call_target="tpu_custom_call" | custom-call | flops 1000 | bytes 2 | tf_op jit(solution)/shard_map/attend_back/pallas_call | solution.py:309
  553.4 4.8 fusion.84
  564.2 5.6 picked_logits.1
  587.6 4.3 collective-permute-done.102
  603.1 6.9 collective-permute-done.108
  613.3 4.0 collective-permute-done.113
  622.0 15.1 %attn_weight_back.1 = bf16[8,768,384]{2,1,0:T(8,128)(2,1)} custom-call(s32[1]{0:T(128)} %bitcast.15.member_ref, bf16[256,768]{1,0:T(8,128)(2,1)} %get-tuple-element.590.x_ref, bf16[2048,768]{1,0:T(8,128)(2,1)} %constant_dynamic-update-slice_fusion.all_ref, bf16[256,768]{1,0:T(8,128)(2,1)} %get-tuple-element.285.o_ref.mixed_ref, ...), custom_call_target="tpu_custom_call" | custom-call | flops 5435817984 | bytes 10871635 | tf_op jit(solution)/shard_map/attn_weight_back/pallas_call | solution.py:389
  639.3 4.0 slice_bitcast_fusion.46
  648.7 4.1 collective-permute-start.120
  654.6 4.2 first_sum.7
  663.6 5.4 collective-permute-done.131
  683.2 4.7 collective-permute-done.125
  687.9 15.7 %collective-permute-done.124 = bf16[96,768]{1,0:T(8,128)(2,1)} collective-permute-done((bf16[96,768]{1,0:T(8,128)(2,1)}, bf16[96,768]{1,0:T(8,128)(2,1)}, u32[]{:S(2)}, u32[]{:S(2)}) %collective-permute-start.124) | collective-permute-done | bytes 147488 | tf_op jit(solution)/shard_map/ppermute | solution.py:76
  748.2 12.7 %fusion.181 = (bf16[1,2,768,768]{3,2,1,0:T(8,128)(2,1)}, f32[1,2,768,768]{3,2,1,0:T(8,128)}, f32[1,2,768,768]{3,2,1,0:T(8,128)}, f32[1,2,768,768]{3,2,1,0:T(8,128)}) fusion(f32[1,2,768,768]{3,2,1,0:T(8,128)} %param.35, f32[]{:T(128)S(6)} %min.3, bf16[1,2,768,768]{3,2,1,0:T(8,128)(2,1)} %reduce-scatter.5.cloned.1.call-done, f32[1,2,768,768]{3,2,1,0:T(8,128)} %param.37, ...), kind=kLoop, calls=%fused_computation.495 | loop fusion | flops 20054016 | bytes 33030148 | tf_op jit(solution)/shard_map/convert_element_type | solution.py:46
  762.3 4.8 fusion.183
  767.1 13.3 %fusion.185 = (bf16[2,1000,768]{2,1,0:T(8,128)(2,1)}, f32[2,1000,768]{2,1,0:T(8,128)}, f32[2,1000,768]{2,1,0:T(8,128)}, f32[2,1000,768]{2,1,0:T(8,128)}) fusion(f32[2,1000,768]{2,1,0:T(8,128)} %param.29, f32[]{:T(128)S(6)} %min.3, f32[1,1000,768]{2,1,0:T(8,128)S(1)} %copy-done.6, f32[1,1000,768]{2,1,0:T(8,128)S(1)} %bitcast.327, f32[2,1000,768]{2,1,0:T(8,128)} %param.31, ...), kind=kLoop, calls=%fused_computation.497 | loop fusion | flops 26112000 | bytes 46080004 | tf_op jit(solution)/shard_map/convert_element_type | solution.py:46
  (820 shorter events, 374.9 us)
Async XLA Ops:
  7.2 200.8 %all-gather.4.cloned.1.call-start = ((), (), s32[]{:S(2)}) async-start(), calls=%async_computation.2 | async-start | bytes 11796480 | tf_op jit(solution)/shard_map/all_gather | solution.py:737
  7.3 24.1 %collective-permute-start.7 = (s32[2048]{0:T(1024)}, s32[2048]{0:T(1024)S(1)}, u32[]{:S(2)}, u32[]{:S(2)}) collective-permute-start(s32[2048]{0:T(1024)} %param.24), channel_id=1, source_target_pairs={{0,16},{8,24},{16,0},{24,8},{1,17},{9,25},{17,1},{25,9},{2,18},{10... | collective-permute-start | bytes 24584 | tf_op jit(solution)/shard_map/ppermute | solution.py:76
  11.4 20.0 %collective-permute-start.6 = (s32[2048]{0:T(1024)}, s32[2048]{0:T(1024)S(1)}, u32[]{:S(2)}, u32[]{:S(2)}) collective-permute-start(s32[2048]{0:T(1024)} %param.24), channel_id=1, source_target_pairs={{0,8},{8,16},{16,24},{24,0},{1,9},{9,17},{17,25},{25,1},{2,10},{10... | collective-permute-start | bytes 24584 | tf_op jit(solution)/shard_map/ppermute | solution.py:76
  12.9 18.5 %collective-permute-start.8 = (s32[2048]{0:T(1024)}, s32[2048]{0:T(1024)S(1)}, u32[]{:S(2)}, u32[]{:S(2)}) collective-permute-start(s32[2048]{0:T(1024)} %param.24), channel_id=1, source_target_pairs={{0,24},{8,0},{16,8},{24,16},{1,25},{9,1},{17,9},{25,17},{2,26},{10... | collective-permute-start | bytes 24584 | tf_op jit(solution)/shard_map/ppermute | solution.py:76
  16.8 50.4 %collective-permute-start.22 = (bf16[192,384]{1,0:T(8,128)(2,1)}, bf16[192,384]{1,0:T(8,128)(2,1)}, u32[]{:S(2)}, u32[]{:S(2)}) collective-permute-start(bf16[192,384]{1,0:T(8,128)(2,1)} %fusion.255), channel_id=1, source_target_pairs={{0,8},{8,16},{16,24},{24,0},{1,9},{9,17},{17,25},{25,1},{2,10},{10... | collective-permute-start | bytes 442376 | tf_op jit(solution)/shard_map/ppermute | solution.py:76
  20.9 300.5 %all-gather.6.cloned.1.call-start = ((), (), s32[]{:S(2)}) async-start(), calls=%async_computation.5 | async-start | bytes 7680000 | tf_op jit(solution)/shard_map/all_gather | solution.py:779
  35.5 20.3 %collective-permute-start.10 = (bf16[96,768]{1,0:T(8,128)(2,1)S(1)}, bf16[96,768]{1,0:T(8,128)(2,1)S(1)}, u32[]{:S(2)}, u32[]{:S(2)}) collective-permute-start(bf16[96,768]{1,0:T(8,128)(2,1)S(1)} %get-tuple-element.681), channel_id=1, source_target_pairs={{0,16},{8,24},{16,0},{24,8},{1,17},{9,25},{17,1},{25,9},{2,18},{10... | collective-permute-start | bytes 442376 | tf_op jit(solution)/shard_map/ppermute | solution.py:76
  39.8 17.8 %collective-permute-start.9 = (bf16[96,768]{1,0:T(8,128)(2,1)S(1)}, bf16[96,768]{1,0:T(8,128)(2,1)S(1)}, u32[]{:S(2)}, u32[]{:S(2)}) collective-permute-start(bf16[96,768]{1,0:T(8,128)(2,1)S(1)} %get-tuple-element.682), channel_id=1, source_target_pairs={{0,24},{8,0},{16,8},{24,16},{1,25},{9,1},{17,9},{25,17},{2,26},{10... | collective-permute-start | bytes 442376 | tf_op jit(solution)/shard_map/ppermute | solution.py:76
  66.2 15.2 %collective-permute-start.14 = (bf16[256,768]{1,0:T(8,128)(2,1)}, bf16[256,768]{1,0:T(8,128)(2,1)S(1)}, u32[]{:S(2)}, u32[]{:S(2)}) collective-permute-start(bf16[256,768]{1,0:T(8,128)(2,1)} %get-tuple-element.630), channel_id=1, source_target_pairs={{0,1},{1,0},{2,3},{3,2},{4,5},{5,4},{6,7},{7,6},{8,9},{9,8},{10,11... | collective-permute-start | bytes 1179656 | tf_op jit(solution)/shard_map/ppermute | solution.py:71
  66.6 14.7 %collective-permute-start.13 = (bf16[256,768]{1,0:T(8,128)(2,1)S(1)}, bf16[256,768]{1,0:T(8,128)(2,1)S(1)}, u32[]{:S(2)}, u32[]{:S(2)}) collective-permute-start(bf16[256,768]{1,0:T(8,128)(2,1)S(1)} %get-tuple-element.631), channel_id=1, source_target_pairs={{0,1},{1,0},{2,3},{3,2},{4,5},{5,4},{6,7},{7,6},{8,9},{9,8},{10,11... | collective-permute-start | bytes 1179656 | tf_op jit(solution)/shard_map/ppermute | solution.py:71
  66.7 14.6 %collective-permute-start.12 = (bf16[256,768]{1,0:T(8,128)(2,1)S(1)}, bf16[256,768]{1,0:T(8,128)(2,1)}, u32[]{:S(2)}, u32[]{:S(2)}) collective-permute-start(bf16[256,768]{1,0:T(8,128)(2,1)S(1)} %get-tuple-element.632), channel_id=1, source_target_pairs={{0,1},{1,0},{2,3},{3,2},{4,5},{5,4},{6,7},{7,6},{8,9},{9,8},{10,11... | collective-permute-start | bytes 1179656 | tf_op jit(solution)/shard_map/ppermute | solution.py:71
  67.2 26.7 %collective-permute-start.24 = (bf16[192,384]{1,0:T(8,128)(2,1)}, bf16[192,384]{1,0:T(8,128)(2,1)}, u32[]{:S(2)}, u32[]{:S(2)}) collective-permute-start(bf16[192,384]{1,0:T(8,128)(2,1)} %fusion.255), channel_id=1, source_target_pairs={{0,24},{8,0},{16,8},{24,16},{1,25},{9,1},{17,9},{25,17},{2,26},{10... | collective-permute-start | bytes 442376 | tf_op jit(solution)/shard_map/ppermute | solution.py:76
  78.5 15.5 %collective-permute-start.23 = (bf16[192,384]{1,0:T(8,128)(2,1)}, bf16[192,384]{1,0:T(8,128)(2,1)}, u32[]{:S(2)}, u32[]{:S(2)}) collective-permute-start(bf16[192,384]{1,0:T(8,128)(2,1)} %collective-permute-done.22), channel_id=1, source_target_pairs={{0,8},{8,16},{16,24},{24,0},{1,9},{9,17},{17,25},{25,1},{2,10},{10... | collective-permute-start | bytes 442376 | tf_op jit(solution)/shard_map/ppermute | solution.py:76
  95.8 23.0 %collective-permute-start.28 = (bf16[768,384]{1,0:T(8,128)(2,1)S(1)}, bf16[768,384]{1,0:T(8,128)(2,1)S(1)}, u32[]{:S(2)}, u32[]{:S(2)}) collective-permute-start(bf16[768,384]{1,0:T(8,128)(2,1)S(1)} %bitcast.343), channel_id=1, source_target_pairs={{0,4},{1,5},{2,6},{3,7},{4,0},{5,1},{6,2},{7,3},{8,12},{9,13},{10,... | collective-permute-start | bytes 1769480 | tf_op jit(solution)/shard_map/ppermute | solution.py:71
  97.4 23.1 %collective-permute-start.26 = (bf16[768,384]{1,0:T(8,128)(2,1)S(1)}, bf16[768,384]{1,0:T(8,128)(2,1)}, u32[]{:S(2)}, u32[]{:S(2)}) collective-permute-start(bf16[768,384]{1,0:T(8,128)(2,1)S(1)} %bitcast.344), channel_id=1, source_target_pairs={{0,2},{1,3},{2,0},{3,1},{4,6},{5,7},{6,4},{7,5},{8,10},{9,11},{10,... | collective-permute-start | bytes 1769480 | tf_op jit(solution)/shard_map/ppermute | solution.py:71
  98.9 23.2 %collective-permute-start.16 = (bf16[128,768]{1,0:T(8,128)(2,1)}, bf16[128,768]{1,0:T(8,128)(2,1)S(1)}, u32[]{:S(2)}, u32[]{:S(2)}) collective-permute-start(bf16[128,768]{1,0:T(8,128)(2,1)} %get-tuple-element.279), channel_id=1, source_target_pairs={{0,2},{1,3},{2,0},{3,1},{4,6},{5,7},{6,4},{7,5},{8,10},{9,11},{10,... | collective-permute-start | bytes 589832 | tf_op jit(solution)/shard_map/ppermute | solution.py:71
  99.5 16.8 %collective-permute-start.19 = (bf16[128,768]{1,0:T(8,128)(2,1)}, bf16[128,768]{1,0:T(8,128)(2,1)S(1)}, u32[]{:S(2)}, u32[]{:S(2)}) collective-permute-start(bf16[128,768]{1,0:T(8,128)(2,1)} %get-tuple-element.283), channel_id=1, source_target_pairs={{0,4},{1,5},{2,6},{3,7},{4,0},{5,1},{6,2},{7,3},{8,12},{9,13},{10,... | collective-permute-start | bytes 589832 | tf_op jit(solution)/shard_map/ppermute | solution.py:71
  101.1 21.5 %collective-permute-start.18 = (bf16[128,768]{1,0:T(8,128)(2,1)S(1)}, bf16[128,768]{1,0:T(8,128)(2,1)S(1)}, u32[]{:S(2)}, u32[]{:S(2)}) collective-permute-start(bf16[128,768]{1,0:T(8,128)(2,1)S(1)} %add_convert_fusion.10), channel_id=1, source_target_pairs={{0,4},{1,5},{2,6},{3,7},{4,0},{5,1},{6,2},{7,3},{8,12},{9,13},{10,... | collective-permute-start | bytes 589832 | tf_op jit(solution)/shard_map/ppermute | solution.py:71
  130.9 16.5 %collective-permute-start.25 = (bf16[768,384]{1,0:T(8,128)(2,1)S(1)}, bf16[768,384]{1,0:T(8,128)(2,1)}, u32[]{:S(2)}, u32[]{:S(2)}) collective-permute-start(bf16[768,384]{1,0:T(8,128)(2,1)S(1)} %bitcast.345), channel_id=1, source_target_pairs={{0,1},{1,0},{2,3},{3,2},{4,5},{5,4},{6,7},{7,6},{8,9},{9,8},{10,11... | collective-permute-start | bytes 1769480 | tf_op jit(solution)/shard_map/ppermute | solution.py:71
  130.9 18.9 %collective-permute-start.29 = (bf16[768,384]{1,0:T(8,128)(2,1)S(1)}, bf16[768,384]{1,0:T(8,128)(2,1)}, u32[]{:S(2)}, u32[]{:S(2)}) collective-permute-start(bf16[768,384]{1,0:T(8,128)(2,1)S(1)} %collective-permute-done.28.refs_4_), channel_id=1, source_target_pairs={{0,1},{1,0},{2,3},{3,2},{4,5},{5,4},{6,7},{7,6},{8,9},{9,8},{10,11... | collective-permute-start | bytes 1769480 | tf_op jit(solution)/shard_map/ppermute | solution.py:71
  131.4 19.8 %collective-permute-start.27 = (bf16[768,384]{1,0:T(8,128)(2,1)}, bf16[768,384]{1,0:T(8,128)(2,1)}, u32[]{:S(2)}, u32[]{:S(2)}) collective-permute-start(bf16[768,384]{1,0:T(8,128)(2,1)} %collective-permute-done.26.refs_2_), channel_id=1, source_target_pairs={{0,1},{1,0},{2,3},{3,2},{4,5},{5,4},{6,7},{7,6},{8,9},{9,8},{10,11... | collective-permute-start | bytes 1769480 | tf_op jit(solution)/shard_map/ppermute | solution.py:71
  198.4 29.1 %collective-permute-start.49 = (bf16[128,768]{1,0:T(8,128)(2,1)S(1)}, bf16[128,768]{1,0:T(8,128)(2,1)S(1)}, u32[]{:S(2)}, u32[]{:S(2)}) collective-permute-start(bf16[128,768]{1,0:T(8,128)(2,1)S(1)} %get-tuple-element.663), channel_id=1, source_target_pairs={{0,7},{1,6},{2,5},{3,4},{4,3},{5,2},{6,1},{7,0},{8,15},{9,14},{10,... | collective-permute-start | bytes 589832 | tf_op jit(solution)/shard_map/ppermute | solution.py:71
  198.4 28.4 %collective-permute-start.48 = (bf16[128,768]{1,0:T(8,128)(2,1)S(1)}, bf16[128,768]{1,0:T(8,128)(2,1)S(1)}, u32[]{:S(2)}, u32[]{:S(2)}) collective-permute-start(bf16[128,768]{1,0:T(8,128)(2,1)S(1)} %get-tuple-element.664), channel_id=1, source_target_pairs={{0,6},{1,7},{2,4},{3,5},{4,2},{5,3},{6,0},{7,1},{8,14},{9,15},{10,... | collective-permute-start | bytes 589832 | tf_op jit(solution)/shard_map/ppermute | solution.py:71
  201.0 18.8 %collective-permute-start.45 = (bf16[128,768]{1,0:T(8,128)(2,1)}, bf16[128,768]{1,0:T(8,128)(2,1)S(1)}, u32[]{:S(2)}, u32[]{:S(2)}) collective-permute-start(bf16[128,768]{1,0:T(8,128)(2,1)} %get-tuple-element.667), channel_id=1, source_target_pairs={{0,3},{1,2},{2,1},{3,0},{4,7},{5,6},{6,5},{7,4},{8,11},{9,10},{10,... | collective-permute-start | bytes 589832 | tf_op jit(solution)/shard_map/ppermute | solution.py:71
  201.2 17.1 %collective-permute-start.44 = (bf16[128,768]{1,0:T(8,128)(2,1)}, bf16[128,768]{1,0:T(8,128)(2,1)S(1)}, u32[]{:S(2)}, u32[]{:S(2)}) collective-permute-start(bf16[128,768]{1,0:T(8,128)(2,1)} %get-tuple-element.668), channel_id=1, source_target_pairs={{0,2},{1,3},{2,0},{3,1},{4,6},{5,7},{6,4},{7,5},{8,10},{9,11},{10,... | collective-permute-start | bytes 589832 | tf_op jit(solution)/shard_map/ppermute | solution.py:71
  208.1 512.0 %reduce-scatter.3.cloned.1.call-start = ((), (), s32[]{:S(2)}) async-start(), calls=%async_computation.3 | async-start | bytes 7680000 | tf_op jit(solution)/shard_map/reduce_scatter | solution.py:183
  251.1 23.7 %collective-permute-start.56 = (bf16[128,768]{1,0:T(8,128)(2,1)S(1)}, bf16[128,768]{1,0:T(8,128)(2,1)S(1)}, u32[]{:S(2)}, u32[]{:S(2)}) collective-permute-start(bf16[128,768]{1,0:T(8,128)(2,1)S(1)} %get-tuple-element.655), channel_id=1, source_target_pairs={{0,7},{1,6},{2,5},{3,4},{4,3},{5,2},{6,1},{7,0},{8,15},{9,14},{10,... | collective-permute-start | bytes 589832 | tf_op jit(solution)/shard_map/ppermute | solution.py:71
  254.0 20.8 %collective-permute-start.55 = (bf16[128,768]{1,0:T(8,128)(2,1)S(1)}, bf16[128,768]{1,0:T(8,128)(2,1)S(1)}, u32[]{:S(2)}, u32[]{:S(2)}) collective-permute-start(bf16[128,768]{1,0:T(8,128)(2,1)S(1)} %get-tuple-element.656), channel_id=1, source_target_pairs={{0,6},{1,7},{2,4},{3,5},{4,2},{5,3},{6,0},{7,1},{8,14},{9,15},{10,... | collective-permute-start | bytes 589832 | tf_op jit(solution)/shard_map/ppermute | solution.py:71
  254.2 14.8 %collective-permute-start.52 = (bf16[128,768]{1,0:T(8,128)(2,1)}, bf16[128,768]{1,0:T(8,128)(2,1)S(1)}, u32[]{:S(2)}, u32[]{:S(2)}) collective-permute-start(bf16[128,768]{1,0:T(8,128)(2,1)} %get-tuple-element.659), channel_id=1, source_target_pairs={{0,3},{1,2},{2,1},{3,0},{4,7},{5,6},{6,5},{7,4},{8,11},{9,10},{10,... | collective-permute-start | bytes 589832 | tf_op jit(solution)/shard_map/ppermute | solution.py:71
  258.8 16.0 %collective-permute-start.54 = (bf16[128,768]{1,0:T(8,128)(2,1)}, bf16[128,768]{1,0:T(8,128)(2,1)S(1)}, u32[]{:S(2)}, u32[]{:S(2)}) collective-permute-start(bf16[128,768]{1,0:T(8,128)(2,1)} %get-tuple-element.657), channel_id=1, source_target_pairs={{0,5},{1,4},{2,7},{3,6},{4,1},{5,0},{6,3},{7,2},{8,13},{9,12},{10,... | collective-permute-start | bytes 589832 | tf_op jit(solution)/shard_map/ppermute | solution.py:71
  278.3 16.2 %collective-permute-start.57 = (bf16[256,768]{1,0:T(8,128)(2,1)}, bf16[256,768]{1,0:T(8,128)(2,1)}, u32[]{:S(2)}, u32[]{:S(2)}) collective-permute-start(bf16[256,768]{1,0:T(8,128)(2,1)} %get-tuple-element.588), channel_id=1, source_target_pairs={{0,1},{1,0},{2,3},{3,2},{4,5},{5,4},{6,7},{7,6},{8,9},{9,8},{10,11... | collective-permute-start | bytes 1179656 | tf_op jit(solution)/shard_map/ppermute | solution.py:71
  395.4 23.3 %collective-permute-start.78 = (bf16[128,768]{1,0:T(8,128)(2,1)}, bf16[128,768]{1,0:T(8,128)(2,1)}, u32[]{:S(2)}, u32[]{:S(2)}) collective-permute-start(bf16[128,768]{1,0:T(8,128)(2,1)} %get-tuple-element.294), channel_id=1, source_target_pairs={{0,2},{1,3},{2,0},{3,1},{4,6},{5,7},{6,4},{7,5},{8,10},{9,11},{10,... | collective-permute-start | bytes 589832 | tf_op jit(solution)/shard_map/ppermute | solution.py:71
  415.2 309.0 %reduce-scatter.5.cloned.1.call-start = ((), (), s32[]{:S(2)}) async-start(), calls=%async_computation.4 | async-start | bytes 11796480 | tf_op jit(solution)/shard_map/reduce_scatter | solution.py:183
  417.4 14.6 %collective-permute-start.82 = (bf16[128,768]{1,0:T(8,128)(2,1)}, bf16[128,768]{1,0:T(8,128)(2,1)S(1)}, u32[]{:S(2)}, u32[]{:S(2)}) collective-permute-start(bf16[128,768]{1,0:T(8,128)(2,1)} %get-tuple-element.297), channel_id=1, source_target_pairs={{0,4},{1,5},{2,6},{3,7},{4,0},{5,1},{6,2},{7,3},{8,12},{9,13},{10,... | collective-permute-start | bytes 589832 | tf_op jit(solution)/shard_map/ppermute | solution.py:71
  440.4 21.8 %collective-permute-start.89 = (bf16[128,768]{1,0:T(8,128)(2,1)S(1)}, bf16[128,768]{1,0:T(8,128)(2,1)S(1)}, u32[]{:S(2)}, u32[]{:S(2)}) collective-permute-start(bf16[128,768]{1,0:T(8,128)(2,1)S(1)} %get-tuple-element.647), channel_id=1, source_target_pairs={{0,7},{1,6},{2,5},{3,4},{4,3},{5,2},{6,1},{7,0},{8,15},{9,14},{10,... | collective-permute-start | bytes 589832 | tf_op jit(solution)/shard_map/ppermute | solution.py:71
  442.0 20.1 %collective-permute-start.88 = (bf16[128,768]{1,0:T(8,128)(2,1)S(1)}, bf16[128,768]{1,0:T(8,128)(2,1)S(1)}, u32[]{:S(2)}, u32[]{:S(2)}) collective-permute-start(bf16[128,768]{1,0:T(8,128)(2,1)S(1)} %get-tuple-element.648), channel_id=1, source_target_pairs={{0,6},{1,7},{2,4},{3,5},{4,2},{5,3},{6,0},{7,1},{8,14},{9,15},{10,... | collective-permute-start | bytes 589832 | tf_op jit(solution)/shard_map/ppermute | solution.py:71
  446.1 16.0 %collective-permute-start.87 = (bf16[128,768]{1,0:T(8,128)(2,1)S(1)}, bf16[128,768]{1,0:T(8,128)(2,1)S(1)}, u32[]{:S(2)}, u32[]{:S(2)}) collective-permute-start(bf16[128,768]{1,0:T(8,128)(2,1)S(1)} %get-tuple-element.649), channel_id=1, source_target_pairs={{0,5},{1,4},{2,7},{3,6},{4,1},{5,0},{6,3},{7,2},{8,13},{9,12},{10,... | collective-permute-start | bytes 589832 | tf_op jit(solution)/shard_map/ppermute | solution.py:71
  488.6 38.1 %collective-permute-start.96 = (bf16[128,768]{1,0:T(8,128)(2,1)S(1)}, bf16[128,768]{1,0:T(8,128)(2,1)}, u32[]{:S(2)}, u32[]{:S(2)}) collective-permute-start(bf16[128,768]{1,0:T(8,128)(2,1)S(1)} %get-tuple-element.639), channel_id=1, source_target_pairs={{0,7},{1,6},{2,5},{3,4},{4,3},{5,2},{6,1},{7,0},{8,15},{9,14},{10,... | collective-permute-start | bytes 589832 | tf_op jit(solution)/shard_map/ppermute | solution.py:71
  489.8 36.0 %collective-permute-start.95 = (bf16[128,768]{1,0:T(8,128)(2,1)}, bf16[128,768]{1,0:T(8,128)(2,1)}, u32[]{:S(2)}, u32[]{:S(2)}) collective-permute-start(bf16[128,768]{1,0:T(8,128)(2,1)} %get-tuple-element.640), channel_id=1, source_target_pairs={{0,6},{1,7},{2,4},{3,5},{4,2},{5,3},{6,0},{7,1},{8,14},{9,15},{10,... | collective-permute-start | bytes 589832 | tf_op jit(solution)/shard_map/ppermute | solution.py:71
  491.4 25.5 %collective-permute-start.91 = (bf16[128,768]{1,0:T(8,128)(2,1)}, bf16[128,768]{1,0:T(8,128)(2,1)}, u32[]{:S(2)}, u32[]{:S(2)}) collective-permute-start(bf16[128,768]{1,0:T(8,128)(2,1)} %get-tuple-element.644), channel_id=1, source_target_pairs={{0,2},{1,3},{2,0},{3,1},{4,6},{5,7},{6,4},{7,5},{8,10},{9,11},{10,... | collective-permute-start | bytes 589832 | tf_op jit(solution)/shard_map/ppermute | solution.py:71
  492.9 21.6 %collective-permute-start.90 = (bf16[128,768]{1,0:T(8,128)(2,1)}, bf16[128,768]{1,0:T(8,128)(2,1)}, u32[]{:S(2)}, u32[]{:S(2)}) collective-permute-start(bf16[128,768]{1,0:T(8,128)(2,1)} %get-tuple-element.645), channel_id=1, source_target_pairs={{0,1},{1,0},{2,3},{3,2},{4,5},{5,4},{6,7},{7,6},{8,9},{9,8},{10,11... | collective-permute-start | bytes 589832 | tf_op jit(solution)/shard_map/ppermute | solution.py:71
  579.0 15.4 %collective-permute-start.106 = (bf16[128,768]{1,0:T(8,128)(2,1)}, bf16[128,768]{1,0:T(8,128)(2,1)S(1)}, u32[]{:S(2)}, u32[]{:S(2)}) collective-permute-start(bf16[128,768]{1,0:T(8,128)(2,1)} %get-tuple-element.307), channel_id=1, source_target_pairs={{0,4},{1,5},{2,6},{3,7},{4,0},{5,1},{6,2},{7,3},{8,12},{9,13},{10,... | collective-permute-start | bytes 589832 | tf_op jit(solution)/shard_map/ppermute | solution.py:71
  579.8 15.5 %collective-permute-start.101 = (bf16[128,768]{1,0:T(8,128)(2,1)}, bf16[128,768]{1,0:T(8,128)(2,1)S(1)}, u32[]{:S(2)}, u32[]{:S(2)}) collective-permute-start(bf16[128,768]{1,0:T(8,128)(2,1)} %get-tuple-element.302), channel_id=1, source_target_pairs={{0,2},{1,3},{2,0},{3,1},{4,6},{5,7},{6,4},{7,5},{8,10},{9,11},{10,... | collective-permute-start | bytes 589832 | tf_op jit(solution)/shard_map/ppermute | solution.py:71
  621.9 15.2 %collective-permute-start.116 = (f32[72,128]{1,0:T(8,128)S(1)}, f32[72,128]{1,0:T(8,128)S(1)}, u32[]{:S(2)}, u32[]{:S(2)}) collective-permute-start(f32[72,128]{1,0:T(8,128)S(1)} %pad_bitcast_fusion), channel_id=1, source_target_pairs={{0,1},{1,0},{2,3},{3,2},{4,5},{5,4},{6,7},{7,6},{8,9},{9,8},{10,11... | collective-permute-start | bytes 110600 | tf_op jit(solution)/shard_map/ppermute | solution.py:71
  662.9 17.8 %collective-permute-start.135 = (bf16[384,384]{1,0:T(8,128)(2,1)}, bf16[384,384]{1,0:T(8,128)(2,1)S(1)}, u32[]{:S(2)}, u32[]{:S(2)}) collective-permute-start(bf16[384,384]{1,0:T(8,128)(2,1)} %get-tuple-element.324), channel_id=1, source_target_pairs={{0,4},{1,5},{2,6},{3,7},{4,0},{5,1},{6,2},{7,3},{8,12},{9,13},{10,... | collective-permute-start | bytes 884744 | tf_op jit(solution)/shard_map/ppermute | solution.py:71
  675.9 27.7 %collective-permute-start.124 = (bf16[96,768]{1,0:T(8,128)(2,1)}, bf16[96,768]{1,0:T(8,128)(2,1)}, u32[]{:S(2)}, u32[]{:S(2)}) collective-permute-start(bf16[96,768]{1,0:T(8,128)(2,1)} %get-tuple-element.677), channel_id=1, source_target_pairs={{0,16},{8,24},{16,0},{24,8},{1,17},{9,25},{17,1},{25,9},{2,18},{10... | collective-permute-start | bytes 442376 | tf_op jit(solution)/shard_map/ppermute | solution.py:76
  680.4 23.3 %collective-permute-start.123 = (bf16[96,768]{1,0:T(8,128)(2,1)}, bf16[96,768]{1,0:T(8,128)(2,1)S(1)}, u32[]{:S(2)}, u32[]{:S(2)}) collective-permute-start(bf16[96,768]{1,0:T(8,128)(2,1)} %get-tuple-element.678), channel_id=1, source_target_pairs={{0,8},{8,16},{16,24},{24,0},{1,9},{9,17},{17,25},{25,1},{2,10},{10... | collective-permute-start | bytes 442376 | tf_op jit(solution)/shard_map/ppermute | solution.py:76
  682.5 24.0 %collective-permute-start.136 = (bf16[192,384]{1,0:T(8,128)(2,1)S(1)}, bf16[192,384]{1,0:T(8,128)(2,1)S(1)}, u32[]{:S(2)}, u32[]{:S(2)}) collective-permute-start(bf16[192,384]{1,0:T(8,128)(2,1)S(1)} %get-tuple-element.673), channel_id=1, source_target_pairs={{0,8},{8,16},{16,24},{24,0},{1,9},{9,17},{17,25},{25,1},{2,10},{10... | collective-permute-start | bytes 442376 | tf_op jit(solution)/shard_map/ppermute | solution.py:76
  (237 other events, 2417.7 us)
Sparse Core Ops, SparseCore 0:
  21.0 187.0 all-gather.3
  210.2 111.0 all-gather.5
  415.3 105.8 reduce-scatter.2
  523.5 174.2 reduce-scatter.4

commit v4 on v3

--- a/solution.py
+++ b/solution.py
@@ -399,42 +399,49 @@
     )(member.reshape(1), *arrays)
 
 
-def head_kernel(rows_ref, heads_ref, exps_ref, stats_ref):
-    rows = rows_ref[...]
-    count = heads_ref.shape[0]
+def head_kernel(rows_ref, place_ref, heads_ref, exps_ref, stats_ref, picked_ref):
+    rows, place = rows_ref[...], place_ref[...]
+    count, words, _ = heads_ref.shape
+    picked = 0.0
     for k in range(count):
         scores = dot_nt(heads_ref[k], rows)
         top = jnp.max(scores, axis=0, keepdims=True)
         weights = jnp.exp(scores - top)
+        iota = lax.broadcasted_iota(jnp.int32, scores.shape, 0)
+        chosen = jnp.where(iota == place - k * words, scores, 0.0)
+        picked = picked + jnp.sum(chosen, axis=0, keepdims=True)
         stats_ref[k : k + 1, :] = top
         stats_ref[count + k : count + k + 1, :] = jnp.sum(weights, axis=0, keepdims=True)
         exps_ref[k] = weights.astype(BF)
-
-
-def head_forward(rows, heads):
+    picked_ref[...] = picked
+
+
+def head_forward(rows, place, heads):
     group, width = rows.shape
     count, depth, _ = heads.shape
     block = min(512, group)
-    exps, stats = pl.pallas_call(
+    return pl.pallas_call(
         head_kernel,
         grid=(group // block,),
         in_specs=[
             pl.BlockSpec((block, width), lambda i: (i, 0)),
+            pl.BlockSpec((1, block), lambda i: (0, i)),
             pl.BlockSpec((count, depth, width), lambda i: (0, 0, 0)),
         ],
         out_specs=[
             pl.BlockSpec((count, depth, block), lambda i: (0, 0, i)),
             pl.BlockSpec((2 * count, block), lambda i: (0, i)),
+            pl.BlockSpec((1, block), lambda i: (0, i)),
         ],
         out_shape=[
             jax.ShapeDtypeStruct((count, depth, group), BF),
             jax.ShapeDtypeStruct((2 * count, group), F32),
+            jax.ShapeDtypeStruct((1, group), F32),
         ],
         compiler_params=params(),
         cost_estimate=cost(2 * group * width * depth * count),
         name="head_forward",
-    )(rows, heads)
-    return exps, stats
+    )(rows, place, heads)
 
 
 def chosen_tokens(rank_ref, word_ref, k, turn_no, capacity):
@@ -450,35 +457,6 @@
     return (word == lanes).astype(BF)
 
 
-def wanted_kernel(
-    capacity, rounds_ref, rank_ref, word_ref, heads_ref, out_ref
-):
-    count, words, _ = heads_ref.shape
-
-    def wanted(turn_no):
-        picks, found = [], []
-        for k in range(count):
-            chosen, word = chosen_tokens(rank_ref, word_ref, k, turn_no, capacity)
-            picks.append(jnp.where(chosen, 1.0, 0.0).astype(BF))
-            found.append(dot_nn(word_hots(word, words), heads_ref[k]).astype(BF))
-        return dot_tn(jnp.concatenate(picks), jnp.concatenate(found))
-
-    out_ref[...] = wanted(0).astype(BF)
-
-    @pl.loop(1, rounds_ref[0])
-    def _(turn_no):
-        out_ref[...] = (out_ref[...].astype(F32) + wanted(turn_no)).astype(BF)
-
-
-def picked_kernel(rows_ref, wanted_ref, picked_ref):
-    product = rows_ref[...].astype(F32) * wanted_ref[...].astype(F32)
-    high = product.astype(BF)
-    low = (product - high.astype(F32)).astype(BF)
-    ones = jnp.ones((8, product.shape[1]), BF)
-    picked = dot_nt(ones, high) + dot_nt(ones, low)
-    picked_ref[...] = picked[0:1, :]
-
-
 def stats_kernel(sums_ref, out_ref):
     count = sums_ref.shape[0] // 2
     tops = sums_ref[:count, :]
@@ -489,7 +467,7 @@
 
 def scale_kernel(orders, sums_ref, weight_ref, *refs):
     count = sums_ref.shape[0] // 2
-    stats, logsum_ref, columns_ref = refs[: len(orders)], refs[-2], refs[-1]
+    stats, (logsum_ref, scales_ref, columns_ref) = refs[: len(orders)], refs[-3:]
     length = sums_ref.shape[1] // len(orders)
     tops, sums = [], []
     for ref, order in zip(stats, orders):
@@ -503,10 +481,11 @@
     logsum_ref[...] = logsum
     weight = weight_ref[...]
     scales = weight * jnp.exp(sums_ref[:count, :] - logsum)
-    rest = columns_ref.shape[1] - count - 1
-    columns_ref[...] = jnp.transpose(
-        jnp.concatenate([scales, weight, jnp.zeros((rest, weight.shape[1]), F32)], axis=0)
-    )
+    scales_ref[...] = jnp.concatenate([scales, weight], axis=0)
+    rest = columns_ref.shape[1] - count
+    if rest:
+        scales = jnp.concatenate([scales, jnp.zeros((rest, weight.shape[1]), F32)], axis=0)
+    columns_ref[...] = jnp.transpose(scales)
 
 
 def head_weight_kernel(exps_ref, rows_ref, columns_ref, terms_ref, out_ref):
@@ -568,34 +547,38 @@
     )(*arrays)
 
 
-def head_rows_kernel(columns_ref, wanted_ref, heads_ref, exps_ref, out_ref):
-    count = heads_ref.shape[0]
-    out = wanted_ref[...].astype(F32) * (-columns_ref[:, count : count + 1])
+def head_rows_kernel(scales_ref, place_ref, heads_ref, exps_ref, out_ref):
+    count, words, _ = heads_ref.shape
+    place, weight = place_ref[...], scales_ref[count : count + 1, :]
+    out = None
     for k in range(count):
-        out = out + dot_tn(exps_ref[k], heads_ref[k]) * columns_ref[:, k : k + 1]
+        grads = exps_ref[k].astype(F32) * scales_ref[k : k + 1, :]
+        rows = lax.broadcasted_iota(jnp.int32, grads.shape, 0)
+        grads = (grads - jnp.where(rows == place - k * words, weight, 0.0)).astype(BF)
+        term = dot_tn(grads, heads_ref[k])
+        out = term if out is None else out + term
     out_ref[...] = out.astype(BF)
 
 
-def head_rows_back(columns, wanted, heads, exps):
+def head_rows_back(scales, place, heads, exps):
     count, depth, width = heads.shape
     group = exps.shape[2]
     block = min(256, group)
-    rows = pl.BlockSpec((block, width), lambda i: (i, 0))
     return pl.pallas_call(
         head_rows_kernel,
         grid=(group // block,),
         in_specs=[
-            pl.BlockSpec((block, columns.shape[1]), lambda i: (i, 0)),
-            rows,
+            pl.BlockSpec((count + 1, block), lambda i: (0, i)),
+            pl.BlockSpec((1, block), lambda i: (0, i)),
             pl.BlockSpec((count, depth, width), lambda i: (0, 0, 0)),
             pl.BlockSpec((count, depth, block), lambda i: (0, 0, i)),
         ],
-        out_specs=rows,
+        out_specs=pl.BlockSpec((block, width), lambda i: (i, 0)),
         out_shape=jax.ShapeDtypeStruct((group, width), BF),
         compiler_params=params(),
         cost_estimate=cost(2 * group * width * depth * count),
         name="head_rows_back",
-    )(columns, wanted, heads, exps)
+    )(scales, place, heads, exps)
 
 
 def ranks(hits):
@@ -699,10 +682,10 @@
     def put(arrived, select_from):
         return dot_tn(select_from, arrived).astype(BF)
 
-    def spread(turn_no, grads, select_own, select_from):
+    def spread(turn_no, grads, select_own, select_from, earlier=None):
         chosen = dot_nn(select_from, grads).astype(BF).reshape(rows_dp, capacity, width)
         arrived = [chosen[0]] + [turn(chosen[k], k) for k in range(1, rows_dp)]
-        return dot_tn(select_own, jnp.concatenate(arrived))
+        return dot_tn(select_own, jnp.concatenate(after(arrived, earlier)))
 
     targets_mine = targets.reshape(shards, local)[order].reshape(-1)
     word = targets_mine - member * (rows_dp * words)
@@ -802,7 +785,10 @@
         token_weight[None, :],
         rows_all,
     )
-    exps, head_stats = head_forward(after(rows_all, target_terms), head_shards)
+    word_place = jnp.where(word_slot < rows_dp, word_slot * words + word % words, -1)[None, :]
+    exps, head_stats, picked = head_forward(
+        after(rows_all, target_terms), word_place, head_shards
+    )
     stats = whole_call(
         stats_kernel, jax.ShapeDtypeStruct((2, group), F32), "head_stats", head_stats
     )
@@ -812,20 +798,12 @@
     else:
         gathered = list(lax.all_gather(stats, "expert"))
         orders = [list(range(shards))] * shards
-    wanted = whole_call(
-        functools.partial(wanted_kernel, capacity),
-        jax.ShapeDtypeStruct((group, width), BF),
-        "wanted_rows",
-        word_rounds,
-        word_rank,
-        word_row,
-        head_shards,
-    )
-    logsum_tok, columns = whole_call(
+    logsum_tok, scales, columns = whole_call(
         functools.partial(scale_kernel, orders),
         (
             jax.ShapeDtypeStruct((1, group), F32),
-            jax.ShapeDtypeStruct((group, -(-(rows_dp + 1) // 8) * 8), F32),
+            jax.ShapeDtypeStruct((rows_dp + 1, group), F32),
+            jax.ShapeDtypeStruct((group, -(-rows_dp // 8) * 8), F32),
         ),
         "head_scales",
         head_stats,
@@ -833,16 +811,9 @@
         *gathered,
     )
     own_block = 0 if quick_expert() else member
-    grad_rows_c = head_rows_back(columns, wanted, head_shards, exps)
+    grad_rows_c = head_rows_back(scales, word_place, head_shards, exps)
     grad_heads = head_weight_back(exps, rows_all, columns, target_terms)
     grad_head = sum_shards(grad_heads)
-    picked = whole_call(
-        picked_kernel,
-        jax.ShapeDtypeStruct((1, group), F32),
-        "picked_logits",
-        after(rows_all, grad_heads),
-        wanted,
-    )
     own_sums = jnp.sum(
         lax.dynamic_slice_in_dim(group_hits, own_block * local, local, 0)
         * lax.dynamic_slice_in_dim(logsum_tok[0], own_block * local, local, 0)[:, None],
@@ -897,21 +868,6 @@
     normal_front, grad_gain_a = norm_back(embedded, gains[0], grad_normed_a)
     grad_embedded = (grad_one + normal_front).astype(BF)
     grad_embedded_all = gather_rows(grad_embedded)
-    grad_embed = spread(0, grad_embedded_all, select_own, select_from)
-    _, grad_embed = lax.while_loop(
-        lambda state: state[0] < rounds,
-        lambda state: (
-            state[0] + 1,
-            state[1]
-            + spread(
-                state[0],
-                grad_embedded_all,
-                own_select(state[0].astype(F32)),
-                from_select(state[0].astype(F32)),
-            ),
-        ),
-        (jnp.int32(1), grad_embed),
-    )
     if quick_expert() and quick_dp():
         blocks = attn_weight_back(
             member,
@@ -927,9 +883,11 @@
         part = sum_blocks([blocks[j] for j in range(8)]).astype(BF)
         part = part.reshape(4, width // 4, width // 2)[slot_shards()]
         part = sum_turns([part[k] for k in range(4)])
+        attn_ready = part
         attn_squares = jnp.sum(part * part)
         grad_attn = place_halves(member, gather_pieces(part.astype(BF)))
     else:
+        attn_ready = None
         grad_attn = jnp.stack(
             [
                 dot_tn(normed_ab, grad_query),
@@ -941,10 +899,25 @@
         grad_attn = lax.psum_scatter(grad_attn, "dp", scatter_dimension=1, tiled=True)
         grad_attn = lax.psum(grad_attn, "expert")
         attn_squares = jnp.sum(jnp.square(grad_attn.astype(F32))) / shards
+    grad_embed = spread(0, grad_embedded_all, select_own, select_from, attn_ready)
+    _, grad_embed = lax.while_loop(
+        lambda state: state[0] < rounds,
+        lambda state: (
+            state[0] + 1,
+            state[1]
+            + spread(
+                state[0],
+                grad_embedded_all,
+                own_select(state[0].astype(F32)),
+                from_select(state[0].astype(F32)),
+            ),
+        ),
+        (jnp.int32(1), grad_embed),
+    )
     small = jnp.concatenate(
         [grad_router.reshape(-1), grad_gain_a, grad_gain_b, grad_gain_c, own_sums]
     )
-    small = after(small, grad_embedded_all)
+    head_squares = jnp.sum(jnp.square(grad_head.astype(F32)))
     small = jnp.pad(small, (0, -small.shape[0] % 1024)).reshape(-1, 128)
     small = sum_everywhere(small).reshape(-1)
     edge = router.size
@@ -952,9 +925,7 @@
     grad_gains = small[edge : edge + 3 * width].reshape(3, width)
     domain_sums = small[edge + 3 * width : edge + 3 * width + NDOM]
     small_squares = jnp.sum(grad_router * grad_router) + jnp.sum(grad_gains * grad_gains)
-    grad_head = grad_head.astype(F32)
-    head_squares = jnp.sum(grad_head * grad_head)
-    grad_experts = after(grad_experts, (small, small_squares, grad_head, head_squares))
+    grad_experts = after(grad_experts, head_squares)
     grad_experts = grad_experts.astype(F32)
     squares = (
         jnp.sum(grad_embed * grad_embed)
@@ -965,7 +936,7 @@
     squares = sum_everywhere(jnp.broadcast_to(squares, (1, 128)))[0, 0]
     grad_norm = jnp.sqrt(squares + small_squares)
     factor = jnp.minimum(1.0, CLIP / (grad_norm + 1e-06))
-    grad_tables = jnp.stack([grad_embed, grad_head])
+    grad_tables = jnp.stack([grad_embed, grad_head.astype(F32)])
     tables_out = adam(tables, grad_tables * factor, tables_m, tables_v, 0.1, 0.01)
     attn_out = adam(attn, grad_attn.astype(F32) * factor, attn_m, attn_v, 0.1, 0.01)
     experts_out = adam(experts, grad_experts * factor, experts_m, experts_v, 0.1, 0.01)

time: 799 us -> 793 us (level)
  Pallas kernels: 165 us -> 154 us
  starting transfers between devices: 130 us -> 138 us
    pallas_call x9 -> x7, Pallas kernels: 40.3 us -> 26.9 us  [whole_call(): pl.pallas_call(kernel, in_specs=[smem if a.dtype == jnp.int32 else vmem f...]
    ppermute x15, waiting for transfers between devices: 47.4 us -> 35.6 us  [turn(): lax.ppermute(array, 'dp', [(i, (i + steps) % count) for i in range(count)])]
    ppermute x134, waiting for transfers between devices: 143 us -> 152 us  [swap(): return lax.ppermute(array, axis, pairs)]
    unnamed x324 -> x329, local copies, waits for them, and re-layouts: 44.4 us -> 47.9 us
  transfers between devices with their start and end apart: 153 -> 153, of which waited for: 54 -> 62; matrix products, arithmetic and copies ran while one was open for 28% -> 29% of each run, Pallas kernels for 15% -> 13%
where the time goes in v4:
time: 793 us; the launch traced here: 784 us
  waiting for transfers between devices  197 us (25%)
  Pallas kernels  154 us (19%)
  starting transfers between devices  138 us (17%)
  matrix products  105 us (13%)
  other arithmetic  84.4 us (11%)
  local copies, waits for them, and re-layouts  82.2 us (10%)
  between operations  22.9 us (3%)
    ppermute x134, waiting for transfers between devices, swap(): return lax.ppermute(array, axis, pairs)  152 us
    dot_general x45, matrix products, dot(): lax.dot_general(a, b, ((contract[0], contract[1]), ((), ())), preferred_e...  104 us
    ppermute x134, starting transfers between devices, swap(): return lax.ppermute(array, axis, pairs)  103 us
    unnamed x329, local copies, waits for them, and re-layouts  47.9 us
    ppermute x15, waiting for transfers between devices, turn(): lax.ppermute(array, 'dp', [(i, (i + steps) % count) for i in range(count)])  35.6 us
    ppermute x15, starting transfers between devices, turn(): lax.ppermute(array, 'dp', [(i, (i + steps) % count) for i in range(count)])  34.6 us
    convert_element_type x5, other arithmetic, adam(): return (first, second, weight, weight.astype(BF))  32.3 us
    pallas_call x7, Pallas kernels, whole_call(): pl.pallas_call(kernel, in_specs=[smem if a.dtype == jnp.int32 else vmem f...  26.9 us
  transfers between devices with their start and end apart: 153, of which 62 were waited for; matrix products, arithmetic and copies ran while one was open for 29% of the time, Pallas kernels for 13%

profile of v4, /device:TPU:0, one launch (start us, length us, event | category | flops | bytes accessed | tf_op | source)
XLA Modules:
  0.0 783.5 jit_solution(8619411855910366689)
XLA Ops:
  7.3 4.1 collective-permute-start.7
  16.8 4.0 convert_element_type.416
  36.1 4.4 collective-permute-start.10
  41.8 5.9 collective-permute-done.11
  47.7 8.1 %collective-permute-done.10 = bf16[96,768]{1,0:T(8,128)(2,1)S(1)} collective-permute-done((bf16[96,768]{1,0:T(8,128)(2,1)S(1)}, bf16[96,768]{1,0:T(8,128)(2,1)S(1)}, u32[]{:S(2)}, u32[]{:S(2)}) %collective-permute-start.10) | collective-permute-done | bytes 147488 | tf_op jit(solution)/shard_map/ppermute | solution.py:76
  59.3 4.5 convolution_convert_fusion.4
  68.3 10.3 %collective-permute-start.24 = (bf16[192,384]{1,0:T(8,128)(2,1)}, bf16[192,384]{1,0:T(8,128)(2,1)}, u32[]{:S(2)}, u32[]{:S(2)}) collective-permute-start(bf16[192,384]{1,0:T(8,128)(2,1)} %fusion.256), channel_id=1, source_target_pairs={{0,24},{8,0},{16,8},{24,16},{1,25},{9,1},{17,9},{25,17},{2,26},{10... | collective-permute-start | bytes 442376 | tf_op jit(solution)/shard_map/ppermute | solution.py:76
  88.9 5.1 collective-permute-done.24
  102.7 13.6 %collective-permute-done.19 = bf16[128,768]{1,0:T(8,128)(2,1)S(1)} collective-permute-done((bf16[128,768]{1,0:T(8,128)(2,1)}, bf16[128,768]{1,0:T(8,128)(2,1)S(1)}, u32[]{:S(2)}, u32[]{:S(2)}) %collective-permute-start.19) | collective-permute-done | bytes 196640 | tf_op jit(solution)/shard_map/ppermute | solution.py:71
  133.5 5.2 collective-permute-done.37
  151.3 5.0 place_halves.2
  165.7 6.4 convolution_convert_fusion.2.v_ref
  172.1 4.0 convolution_convert_fusion.3.k_ref
  176.1 18.7 %attend.1 = (bf16[256,768]{1,0:T(8,128)(2,1)}, f32[12,256]{1,0:T(8,128)}) custom-call(bf16[256,768]{1,0:T(8,128)(2,1)} %convolution_convert_fusion.16.q_ref, bf16[2048,768]{1,0:T(8,128)(2,1)} %convolution_convert_fusion.3.k_ref, bf16[2048,768]{1,0:T(8,128)(2,1)} %convolution_convert_fusion.2.v_ref, s32[2048,1]{1,0:T(8,128)} %compare_select_fusion.kp_ref, ...), custom_call_target="tpu_custom_call" | custom-call | flops 1000 | bytes 2 | tf_op jit(solution)/shard_map/attend/pallas_call | solution.py:243
  202.9 5.2 all-gather.4.cloned.1.call-done
  210.8 7.5 collective-permute-done.44
  221.3 4.8 collective-permute-done.47
  232.1 4.0 fusion.94
  259.8 9.3 %collective-permute-done.52 = bf16[128,768]{1,0:T(8,128)(2,1)S(1)} collective-permute-done((bf16[128,768]{1,0:T(8,128)(2,1)}, bf16[128,768]{1,0:T(8,128)(2,1)S(1)}, u32[]{:S(2)}, u32[]{:S(2)}) %collective-permute-start.52) | collective-permute-done | bytes 196640 | tf_op jit(solution)/shard_map/ppermute | solution.py:71
  270.7 4.2 collective-permute-done.54
  279.2 9.7 %collective-permute-done.58 = bf16[256,768]{1,0:T(8,128)(2,1)} collective-permute-done((bf16[256,768]{1,0:T(8,128)(2,1)}, bf16[256,768]{1,0:T(8,128)(2,1)}, u32[]{:S(2)}, u32[]{:S(2)}) %collective-permute-start.58) | collective-permute-done | bytes 393248 | tf_op jit(solution)/shard_map/ppermute | solution.py:71
  308.2 8.9 %target_terms.1.terms_ref = bf16[4,1000,768]{2,1,0:T(8,128)(2,1)} custom-call(s32[1]{0:T(128)} %bitcast.37.rounds_ref, f32[4,2048]{1,0:T(4,128)} %bitcast.360, f32[1,2048]{1,0:T(1,128)} %get-tuple-element.694.word_ref, f32[1,2048]{1,0:T(1,128)} %bitcast.370, bf16[2048,768]{1,0:T(8,128)(2,1)} %constant_dynamic-update-slice_fusion.24.rows_ref), custom_call_target="tpu_custom_call" | custom-call | flops 1000 | bytes 2 | tf_op jit(solution)/shard_map/target_terms/pallas_call | solution.py:539
  317.2 4.2 all-gather.6.cloned.1.call-done
  321.3 25.2 %head_forward.1 = (bf16[4,1000,2048]{2,1,0:T(8,128)(2,1)}, f32[8,2048]{1,0:T(8,128)}, f32[1,2048]{1,0:T(1,128)}) custom-call(bf16[2048,768]{1,0:T(8,128)(2,1)} %constant_dynamic-update-slice_fusion.24.rows_ref, s32[1,2048]{1,0:T(1,128)} %get-tuple-element.693.place_ref, bf16[4,1000,768]{2,1,0:T(8,128)(2,1)} %bitcast.393), custom_call_target="tpu_custom_call" | custom-call | flops 12582912000 | bytes 25165824 | tf_op jit(solution)/shard_map/head_forward/pallas_call | solution.py:423
  361.0 20.3 %head_rows_back.1 = bf16[2048,768]{1,0:T(8,128)(2,1)} custom-call(f32[5,2048]{1,0:T(8,128)} %get-tuple-element.293.scales_ref, s32[1,2048]{1,0:T(1,128)} %get-tuple-element.693.place_ref, bf16[4,1000,768]{2,1,0:T(8,128)(2,1)} %bitcast.394, bf16[4,1000,2048]{2,1,0:T(8,128)(2,1)} %get-tuple-element.294.exps_ref), custom_call_target="tpu_custom_call" | custom-call | flops 12582912000 | bytes 25165824 | tf_op jit(solution)/shard_map/head_rows_back/pallas_call | solution.py:567
  392.4 19.0 %head_weight_back.1 = bf16[4,1000,768]{2,1,0:T(8,128)(2,1)} custom-call(bf16[4,1000,2048]{2,1,0:T(8,128)(2,1)} %get-tuple-element.294.exps_ref, bf16[2048,768]{1,0:T(8,128)(2,1)} %constant_dynamic-update-slice_fusion.24.rows_ref, f32[2048,8]{1,0:T(8,128)} %get-tuple-element.329.columns_ref, bf16[4,1000,768]{2,1,0:T(8,128)(2,1)} %target_terms.1.terms_ref), custom_call_target="tpu_custom_call" | custom-call | flops 12582912000 | bytes 25165824 | tf_op jit(solution)/shard_map/head_weight_back/pallas_call | solution.py:501
  423.1 5.3 collective-permute-done.79
  443.0 10.5 %collective-permute-done.85 = bf16[128,768]{1,0:T(8,128)(2,1)S(1)} collective-permute-done((bf16[128,768]{1,0:T(8,128)(2,1)S(1)}, bf16[128,768]{1,0:T(8,128)(2,1)S(1)}, u32[]{:S(2)}, u32[]{:S(2)}) %collective-permute-start.85) | collective-permute-done | bytes 196640 | tf_op jit(solution)/shard_map/ppermute | solution.py:71
  455.2 4.0 collective-permute-done.87
  459.3 4.4 fusion.34
  516.4 3.8 collective-permute-done.93
  529.0 20.9 %attend_back.1 = (bf16[256,768]{1,0:T(8,128)(2,1)}, bf16[2048,768]{1,0:T(8,128)(2,1)}, bf16[2048,768]{1,0:T(8,128)(2,1)}) custom-call(bf16[256,768]{1,0:T(8,128)(2,1)} %convolution_convert_fusion.16.q_ref, bf16[2048,768]{1,0:T(8,128)(2,1)} %convolution_convert_fusion.3.k_ref, bf16[2048,768]{1,0:T(8,128)(2,1)} %convolution_convert_fusion.2.v_ref, ...), custom_call_target="tpu_custom_call" | custom-call | flops 1000 | bytes 2 | tf_op jit(solution)/shard_map/attend_back/pallas_call | solution.py:309
  549.9 4.8 fusion.84
  576.5 6.5 collective-permute-done.102
  595.4 5.9 collective-permute-done.115
  601.3 14.9 %attn_weight_back.1 = bf16[8,768,384]{2,1,0:T(8,128)(2,1)} custom-call(s32[1]{0:T(128)} %bitcast.15.member_ref, bf16[256,768]{1,0:T(8,128)(2,1)} %get-tuple-element.600.x_ref, bf16[2048,768]{1,0:T(8,128)(2,1)} %constant_dynamic-update-slice_fusion.all_ref, bf16[256,768]{1,0:T(8,128)(2,1)} %get-tuple-element.289.o_ref.mixed_ref, ...), custom_call_target="tpu_custom_call" | custom-call | flops 5435817984 | bytes 10871635 | tf_op jit(solution)/shard_map/attn_weight_back/pallas_call | solution.py:389
  619.1 4.4 collective-permute-done.120
  636.4 4.2 first_sum.7
  646.6 4.0 collective-permute-done.131
  657.6 4.3 collective-permute-done.130
  663.2 4.2 collective-permute-done.135
  671.8 3.9 collective-permute-start.138
  675.7 4.6 collective-permute-done.136
  693.1 8.7 %collective-permute-start.112 = (f32[72,128]{1,0:T(8,128)S(1)}, f32[72,128]{1,0:T(8,128)}, u32[]{:S(2)}, u32[]{:S(2)}) collective-permute-start(f32[72,128]{1,0:T(8,128)S(1)} %add_add_fusion.4), channel_id=1, source_target_pairs={{0,16},{8,24},{16,0},{24,8},{1,17},{9,25},{17,1},{25,9},{2,18},{10... | collective-permute-start | bytes 110600 | tf_op jit(solution)/shard_map/ppermute | solution.py:71
  701.8 4.3 collective-permute-done.124
  743.3 12.9 %fusion.180 = (bf16[1,2,768,768]{3,2,1,0:T(8,128)(2,1)}, f32[1,2,768,768]{3,2,1,0:T(8,128)}, f32[1,2,768,768]{3,2,1,0:T(8,128)}, f32[1,2,768,768]{3,2,1,0:T(8,128)}) fusion(f32[1,2,768,768]{3,2,1,0:T(8,128)} %param.35, f32[]{:T(128)S(6)} %min.3, bf16[1,2,768,768]{3,2,1,0:T(8,128)(2,1)} %reduce-scatter.5.cloned.1.call-done, f32[1,2,768,768]{3,2,1,0:T(8,128)} %param.37, ...), kind=kLoop, calls=%fused_computation.496 | loop fusion | flops 20054016 | bytes 33030148 | tf_op jit(solution)/shard_map/convert_element_type | solution.py:46
  757.5 4.8 fusion.182
  762.3 13.3 %fusion.186 = (bf16[2,1000,768]{2,1,0:T(8,128)(2,1)}, f32[2,1000,768]{2,1,0:T(8,128)}, f32[2,1000,768]{2,1,0:T(8,128)}, f32[2,1000,768]{2,1,0:T(8,128)}) fusion(f32[2,1000,768]{2,1,0:T(8,128)} %param.29, f32[]{:T(128)S(6)} %min.3, f32[1,1000,768]{2,1,0:T(8,128)S(1)} %copy-done.6, f32[1,1000,768]{2,1,0:T(8,128)S(1)} %bitcast.332, f32[2,1000,768]{2,1,0:T(8,128)} %param.31, ...), kind=kLoop, calls=%fused_computation.499 | loop fusion | flops 26112000 | bytes 46080004 | tf_op jit(solution)/shard_map/convert_element_type | solution.py:46
  (824 shorter events, 384.4 us)
Async XLA Ops:
  7.2 200.9 %all-gather.4.cloned.1.call-start = ((), (), s32[]{:S(2)}) async-start(), calls=%async_computation.2 | async-start | bytes 11796480 | tf_op jit(solution)/shard_map/all_gather | solution.py:720
  7.3 24.7 %collective-permute-start.7 = (s32[2048]{0:T(1024)}, s32[2048]{0:T(1024)S(1)}, u32[]{:S(2)}, u32[]{:S(2)}) collective-permute-start(s32[2048]{0:T(1024)} %param.24), channel_id=1, source_target_pairs={{0,16},{8,24},{16,0},{24,8},{1,17},{9,25},{17,1},{25,9},{2,18},{10... | collective-permute-start | bytes 24584 | tf_op jit(solution)/shard_map/ppermute | solution.py:76
  11.4 20.6 %collective-permute-start.6 = (s32[2048]{0:T(1024)}, s32[2048]{0:T(1024)S(1)}, u32[]{:S(2)}, u32[]{:S(2)}) collective-permute-start(s32[2048]{0:T(1024)} %param.24), channel_id=1, source_target_pairs={{0,8},{8,16},{16,24},{24,0},{1,9},{9,17},{17,25},{25,1},{2,10},{10... | collective-permute-start | bytes 24584 | tf_op jit(solution)/shard_map/ppermute | solution.py:76
  12.9 19.0 %collective-permute-start.8 = (s32[2048]{0:T(1024)}, s32[2048]{0:T(1024)S(1)}, u32[]{:S(2)}, u32[]{:S(2)}) collective-permute-start(s32[2048]{0:T(1024)} %param.24), channel_id=1, source_target_pairs={{0,24},{8,0},{16,8},{24,16},{1,25},{9,1},{17,9},{25,17},{2,26},{10... | collective-permute-start | bytes 24584 | tf_op jit(solution)/shard_map/ppermute | solution.py:76
  16.8 51.4 %collective-permute-start.22 = (bf16[192,384]{1,0:T(8,128)(2,1)}, bf16[192,384]{1,0:T(8,128)(2,1)}, u32[]{:S(2)}, u32[]{:S(2)}) collective-permute-start(bf16[192,384]{1,0:T(8,128)(2,1)} %fusion.256), channel_id=1, source_target_pairs={{0,8},{8,16},{16,24},{24,0},{1,9},{9,17},{17,25},{25,1},{2,10},{10... | collective-permute-start | bytes 442376 | tf_op jit(solution)/shard_map/ppermute | solution.py:76
  20.9 300.5 %all-gather.6.cloned.1.call-start = ((), (), s32[]{:S(2)}) async-start(), calls=%async_computation.5 | async-start | bytes 7680000 | tf_op jit(solution)/shard_map/all_gather | solution.py:762
  36.1 19.7 %collective-permute-start.10 = (bf16[96,768]{1,0:T(8,128)(2,1)S(1)}, bf16[96,768]{1,0:T(8,128)(2,1)S(1)}, u32[]{:S(2)}, u32[]{:S(2)}) collective-permute-start(bf16[96,768]{1,0:T(8,128)(2,1)S(1)} %get-tuple-element.689), channel_id=1, source_target_pairs={{0,16},{8,24},{16,0},{24,8},{1,17},{9,25},{17,1},{25,9},{2,18},{10... | collective-permute-start | bytes 442376 | tf_op jit(solution)/shard_map/ppermute | solution.py:76
  40.4 18.2 %collective-permute-start.9 = (bf16[96,768]{1,0:T(8,128)(2,1)S(1)}, bf16[96,768]{1,0:T(8,128)(2,1)S(1)}, u32[]{:S(2)}, u32[]{:S(2)}) collective-permute-start(bf16[96,768]{1,0:T(8,128)(2,1)S(1)} %get-tuple-element.690), channel_id=1, source_target_pairs={{0,24},{8,0},{16,8},{24,16},{1,25},{9,1},{17,9},{25,17},{2,26},{10... | collective-permute-start | bytes 442376 | tf_op jit(solution)/shard_map/ppermute | solution.py:76
  67.2 16.0 %collective-permute-start.14 = (bf16[256,768]{1,0:T(8,128)(2,1)}, bf16[256,768]{1,0:T(8,128)(2,1)S(1)}, u32[]{:S(2)}, u32[]{:S(2)}) collective-permute-start(bf16[256,768]{1,0:T(8,128)(2,1)} %get-tuple-element.640), channel_id=1, source_target_pairs={{0,1},{1,0},{2,3},{3,2},{4,5},{5,4},{6,7},{7,6},{8,9},{9,8},{10,11... | collective-permute-start | bytes 1179656 | tf_op jit(solution)/shard_map/ppermute | solution.py:71
  67.7 15.5 %collective-permute-start.13 = (bf16[256,768]{1,0:T(8,128)(2,1)S(1)}, bf16[256,768]{1,0:T(8,128)(2,1)S(1)}, u32[]{:S(2)}, u32[]{:S(2)}) collective-permute-start(bf16[256,768]{1,0:T(8,128)(2,1)S(1)} %get-tuple-element.641), channel_id=1, source_target_pairs={{0,1},{1,0},{2,3},{3,2},{4,5},{5,4},{6,7},{7,6},{8,9},{9,8},{10,11... | collective-permute-start | bytes 1179656 | tf_op jit(solution)/shard_map/ppermute | solution.py:71
  67.8 15.5 %collective-permute-start.12 = (bf16[256,768]{1,0:T(8,128)(2,1)S(1)}, bf16[256,768]{1,0:T(8,128)(2,1)}, u32[]{:S(2)}, u32[]{:S(2)}) collective-permute-start(bf16[256,768]{1,0:T(8,128)(2,1)S(1)} %get-tuple-element.642), channel_id=1, source_target_pairs={{0,1},{1,0},{2,3},{3,2},{4,5},{5,4},{6,7},{7,6},{8,9},{9,8},{10,11... | collective-permute-start | bytes 1179656 | tf_op jit(solution)/shard_map/ppermute | solution.py:71
  68.3 25.7 %collective-permute-start.24 = (bf16[192,384]{1,0:T(8,128)(2,1)}, bf16[192,384]{1,0:T(8,128)(2,1)}, u32[]{:S(2)}, u32[]{:S(2)}) collective-permute-start(bf16[192,384]{1,0:T(8,128)(2,1)} %fusion.256), channel_id=1, source_target_pairs={{0,24},{8,0},{16,8},{24,16},{1,25},{9,1},{17,9},{25,17},{2,26},{10... | collective-permute-start | bytes 442376 | tf_op jit(solution)/shard_map/ppermute | solution.py:76
  95.8 23.0 %collective-permute-start.28 = (bf16[768,384]{1,0:T(8,128)(2,1)S(1)}, bf16[768,384]{1,0:T(8,128)(2,1)S(1)}, u32[]{:S(2)}, u32[]{:S(2)}) collective-permute-start(bf16[768,384]{1,0:T(8,128)(2,1)S(1)} %bitcast.345), channel_id=1, source_target_pairs={{0,4},{1,5},{2,6},{3,7},{4,0},{5,1},{6,2},{7,3},{8,12},{9,13},{10,... | collective-permute-start | bytes 1769480 | tf_op jit(solution)/shard_map/ppermute | solution.py:71
  97.4 23.1 %collective-permute-start.26 = (bf16[768,384]{1,0:T(8,128)(2,1)S(1)}, bf16[768,384]{1,0:T(8,128)(2,1)}, u32[]{:S(2)}, u32[]{:S(2)}) collective-permute-start(bf16[768,384]{1,0:T(8,128)(2,1)S(1)} %bitcast.346), channel_id=1, source_target_pairs={{0,2},{1,3},{2,0},{3,1},{4,6},{5,7},{6,4},{7,5},{8,10},{9,11},{10,... | collective-permute-start | bytes 1769480 | tf_op jit(solution)/shard_map/ppermute | solution.py:71
  98.9 23.2 %collective-permute-start.16 = (bf16[128,768]{1,0:T(8,128)(2,1)}, bf16[128,768]{1,0:T(8,128)(2,1)S(1)}, u32[]{:S(2)}, u32[]{:S(2)}) collective-permute-start(bf16[128,768]{1,0:T(8,128)(2,1)} %get-tuple-element.283), channel_id=1, source_target_pairs={{0,2},{1,3},{2,0},{3,1},{4,6},{5,7},{6,4},{7,5},{8,10},{9,11},{10,... | collective-permute-start | bytes 589832 | tf_op jit(solution)/shard_map/ppermute | solution.py:71
  99.5 16.8 %collective-permute-start.19 = (bf16[128,768]{1,0:T(8,128)(2,1)}, bf16[128,768]{1,0:T(8,128)(2,1)S(1)}, u32[]{:S(2)}, u32[]{:S(2)}) collective-permute-start(bf16[128,768]{1,0:T(8,128)(2,1)} %get-tuple-element.287), channel_id=1, source_target_pairs={{0,4},{1,5},{2,6},{3,7},{4,0},{5,1},{6,2},{7,3},{8,12},{9,13},{10,... | collective-permute-start | bytes 589832 | tf_op jit(solution)/shard_map/ppermute | solution.py:71
  101.1 21.5 %collective-permute-start.18 = (bf16[128,768]{1,0:T(8,128)(2,1)S(1)}, bf16[128,768]{1,0:T(8,128)(2,1)S(1)}, u32[]{:S(2)}, u32[]{:S(2)}) collective-permute-start(bf16[128,768]{1,0:T(8,128)(2,1)S(1)} %add_convert_fusion.10), channel_id=1, source_target_pairs={{0,4},{1,5},{2,6},{3,7},{4,0},{5,1},{6,2},{7,3},{8,12},{9,13},{10,... | collective-permute-start | bytes 589832 | tf_op jit(solution)/shard_map/ppermute | solution.py:71
  130.9 16.5 %collective-permute-start.25 = (bf16[768,384]{1,0:T(8,128)(2,1)S(1)}, bf16[768,384]{1,0:T(8,128)(2,1)}, u32[]{:S(2)}, u32[]{:S(2)}) collective-permute-start(bf16[768,384]{1,0:T(8,128)(2,1)S(1)} %bitcast.347), channel_id=1, source_target_pairs={{0,1},{1,0},{2,3},{3,2},{4,5},{5,4},{6,7},{7,6},{8,9},{9,8},{10,11... | collective-permute-start | bytes 1769480 | tf_op jit(solution)/shard_map/ppermute | solution.py:71
  130.9 18.9 %collective-permute-start.29 = (bf16[768,384]{1,0:T(8,128)(2,1)S(1)}, bf16[768,384]{1,0:T(8,128)(2,1)}, u32[]{:S(2)}, u32[]{:S(2)}) collective-permute-start(bf16[768,384]{1,0:T(8,128)(2,1)S(1)} %collective-permute-done.28.refs_4_), channel_id=1, source_target_pairs={{0,1},{1,0},{2,3},{3,2},{4,5},{5,4},{6,7},{7,6},{8,9},{9,8},{10,11... | collective-permute-start | bytes 1769480 | tf_op jit(solution)/shard_map/ppermute | solution.py:71
  131.4 19.8 %collective-permute-start.27 = (bf16[768,384]{1,0:T(8,128)(2,1)}, bf16[768,384]{1,0:T(8,128)(2,1)}, u32[]{:S(2)}, u32[]{:S(2)}) collective-permute-start(bf16[768,384]{1,0:T(8,128)(2,1)} %collective-permute-done.26.refs_2_), channel_id=1, source_target_pairs={{0,1},{1,0},{2,3},{3,2},{4,5},{5,4},{6,7},{7,6},{8,9},{9,8},{10,11... | collective-permute-start | bytes 1769480 | tf_op jit(solution)/shard_map/ppermute | solution.py:71
  198.5 29.1 %collective-permute-start.49 = (bf16[128,768]{1,0:T(8,128)(2,1)S(1)}, bf16[128,768]{1,0:T(8,128)(2,1)S(1)}, u32[]{:S(2)}, u32[]{:S(2)}) collective-permute-start(bf16[128,768]{1,0:T(8,128)(2,1)S(1)} %get-tuple-element.673), channel_id=1, source_target_pairs={{0,7},{1,6},{2,5},{3,4},{4,3},{5,2},{6,1},{7,0},{8,15},{9,14},{10,... | collective-permute-start | bytes 589832 | tf_op jit(solution)/shard_map/ppermute | solution.py:71
  198.5 28.4 %collective-permute-start.48 = (bf16[128,768]{1,0:T(8,128)(2,1)S(1)}, bf16[128,768]{1,0:T(8,128)(2,1)S(1)}, u32[]{:S(2)}, u32[]{:S(2)}) collective-permute-start(bf16[128,768]{1,0:T(8,128)(2,1)S(1)} %get-tuple-element.674), channel_id=1, source_target_pairs={{0,6},{1,7},{2,4},{3,5},{4,2},{5,3},{6,0},{7,1},{8,14},{9,15},{10,... | collective-permute-start | bytes 589832 | tf_op jit(solution)/shard_map/ppermute | solution.py:71
  201.1 18.8 %collective-permute-start.45 = (bf16[128,768]{1,0:T(8,128)(2,1)}, bf16[128,768]{1,0:T(8,128)(2,1)S(1)}, u32[]{:S(2)}, u32[]{:S(2)}) collective-permute-start(bf16[128,768]{1,0:T(8,128)(2,1)} %get-tuple-element.677), channel_id=1, source_target_pairs={{0,3},{1,2},{2,1},{3,0},{4,7},{5,6},{6,5},{7,4},{8,11},{9,10},{10,... | collective-permute-start | bytes 589832 | tf_op jit(solution)/shard_map/ppermute | solution.py:71
  201.3 17.0 %collective-permute-start.44 = (bf16[128,768]{1,0:T(8,128)(2,1)}, bf16[128,768]{1,0:T(8,128)(2,1)S(1)}, u32[]{:S(2)}, u32[]{:S(2)}) collective-permute-start(bf16[128,768]{1,0:T(8,128)(2,1)} %get-tuple-element.678), channel_id=1, source_target_pairs={{0,2},{1,3},{2,0},{3,1},{4,6},{5,7},{6,4},{7,5},{8,10},{9,11},{10,... | collective-permute-start | bytes 589832 | tf_op jit(solution)/shard_map/ppermute | solution.py:71
  208.1 505.5 %reduce-scatter.3.cloned.1.call-start = ((), (), s32[]{:S(2)}) async-start(), calls=%async_computation.3 | async-start | bytes 7680000 | tf_op jit(solution)/shard_map/reduce_scatter | solution.py:183
  251.5 23.4 %collective-permute-start.56 = (bf16[128,768]{1,0:T(8,128)(2,1)S(1)}, bf16[128,768]{1,0:T(8,128)(2,1)S(1)}, u32[]{:S(2)}, u32[]{:S(2)}) collective-permute-start(bf16[128,768]{1,0:T(8,128)(2,1)S(1)} %get-tuple-element.665), channel_id=1, source_target_pairs={{0,7},{1,6},{2,5},{3,4},{4,3},{5,2},{6,1},{7,0},{8,15},{9,14},{10,... | collective-permute-start | bytes 589832 | tf_op jit(solution)/shard_map/ppermute | solution.py:71
  254.3 20.6 %collective-permute-start.55 = (bf16[128,768]{1,0:T(8,128)(2,1)S(1)}, bf16[128,768]{1,0:T(8,128)(2,1)S(1)}, u32[]{:S(2)}, u32[]{:S(2)}) collective-permute-start(bf16[128,768]{1,0:T(8,128)(2,1)S(1)} %get-tuple-element.666), channel_id=1, source_target_pairs={{0,6},{1,7},{2,4},{3,5},{4,2},{5,3},{6,0},{7,1},{8,14},{9,15},{10,... | collective-permute-start | bytes 589832 | tf_op jit(solution)/shard_map/ppermute | solution.py:71
  259.1 15.8 %collective-permute-start.54 = (bf16[128,768]{1,0:T(8,128)(2,1)}, bf16[128,768]{1,0:T(8,128)(2,1)S(1)}, u32[]{:S(2)}, u32[]{:S(2)}) collective-permute-start(bf16[128,768]{1,0:T(8,128)(2,1)} %get-tuple-element.667), channel_id=1, source_target_pairs={{0,5},{1,4},{2,7},{3,6},{4,1},{5,0},{6,3},{7,2},{8,13},{9,12},{10,... | collective-permute-start | bytes 589832 | tf_op jit(solution)/shard_map/ppermute | solution.py:71
  278.4 16.2 %collective-permute-start.57 = (bf16[256,768]{1,0:T(8,128)(2,1)}, bf16[256,768]{1,0:T(8,128)(2,1)}, u32[]{:S(2)}, u32[]{:S(2)}) collective-permute-start(bf16[256,768]{1,0:T(8,128)(2,1)} %get-tuple-element.598), channel_id=1, source_target_pairs={{0,1},{1,0},{2,3},{3,2},{4,5},{5,4},{6,7},{7,6},{8,9},{9,8},{10,11... | collective-permute-start | bytes 1179656 | tf_op jit(solution)/shard_map/ppermute | solution.py:71
  391.8 23.6 %collective-permute-start.78 = (bf16[128,768]{1,0:T(8,128)(2,1)}, bf16[128,768]{1,0:T(8,128)(2,1)}, u32[]{:S(2)}, u32[]{:S(2)}) collective-permute-start(bf16[128,768]{1,0:T(8,128)(2,1)} %get-tuple-element.298), channel_id=1, source_target_pairs={{0,2},{1,3},{2,0},{3,1},{4,6},{5,7},{6,4},{7,5},{8,10},{9,11},{10,... | collective-permute-start | bytes 589832 | tf_op jit(solution)/shard_map/ppermute | solution.py:71
  411.4 306.3 %reduce-scatter.5.cloned.1.call-start = ((), (), s32[]{:S(2)}) async-start(), calls=%async_computation.4 | async-start | bytes 11796480 | tf_op jit(solution)/shard_map/reduce_scatter | solution.py:183
  436.8 22.4 %collective-permute-start.89 = (bf16[128,768]{1,0:T(8,128)(2,1)S(1)}, bf16[128,768]{1,0:T(8,128)(2,1)S(1)}, u32[]{:S(2)}, u32[]{:S(2)}) collective-permute-start(bf16[128,768]{1,0:T(8,128)(2,1)S(1)} %get-tuple-element.657), channel_id=1, source_target_pairs={{0,7},{1,6},{2,5},{3,4},{4,3},{5,2},{6,1},{7,0},{8,15},{9,14},{10,... | collective-permute-start | bytes 589832 | tf_op jit(solution)/shard_map/ppermute | solution.py:71
  439.4 19.8 %collective-permute-start.88 = (bf16[128,768]{1,0:T(8,128)(2,1)S(1)}, bf16[128,768]{1,0:T(8,128)(2,1)S(1)}, u32[]{:S(2)}, u32[]{:S(2)}) collective-permute-start(bf16[128,768]{1,0:T(8,128)(2,1)S(1)} %get-tuple-element.658), channel_id=1, source_target_pairs={{0,6},{1,7},{2,4},{3,5},{4,2},{5,3},{6,0},{7,1},{8,14},{9,15},{10,... | collective-permute-start | bytes 589832 | tf_op jit(solution)/shard_map/ppermute | solution.py:71
  442.4 16.8 %collective-permute-start.87 = (bf16[128,768]{1,0:T(8,128)(2,1)S(1)}, bf16[128,768]{1,0:T(8,128)(2,1)S(1)}, u32[]{:S(2)}, u32[]{:S(2)}) collective-permute-start(bf16[128,768]{1,0:T(8,128)(2,1)S(1)} %get-tuple-element.659), channel_id=1, source_target_pairs={{0,5},{1,4},{2,7},{3,6},{4,1},{5,0},{6,3},{7,2},{8,13},{9,12},{10,... | collective-permute-start | bytes 589832 | tf_op jit(solution)/shard_map/ppermute | solution.py:71
  485.4 38.1 %collective-permute-start.96 = (bf16[128,768]{1,0:T(8,128)(2,1)S(1)}, bf16[128,768]{1,0:T(8,128)(2,1)}, u32[]{:S(2)}, u32[]{:S(2)}) collective-permute-start(bf16[128,768]{1,0:T(8,128)(2,1)S(1)} %get-tuple-element.649), channel_id=1, source_target_pairs={{0,7},{1,6},{2,5},{3,4},{4,3},{5,2},{6,1},{7,0},{8,15},{9,14},{10,... | collective-permute-start | bytes 589832 | tf_op jit(solution)/shard_map/ppermute | solution.py:71
  486.0 36.6 %collective-permute-start.95 = (bf16[128,768]{1,0:T(8,128)(2,1)}, bf16[128,768]{1,0:T(8,128)(2,1)}, u32[]{:S(2)}, u32[]{:S(2)}) collective-permute-start(bf16[128,768]{1,0:T(8,128)(2,1)} %get-tuple-element.650), channel_id=1, source_target_pairs={{0,6},{1,7},{2,4},{3,5},{4,2},{5,3},{6,0},{7,1},{8,14},{9,15},{10,... | collective-permute-start | bytes 589832 | tf_op jit(solution)/shard_map/ppermute | solution.py:71
  488.3 24.4 %collective-permute-start.91 = (bf16[128,768]{1,0:T(8,128)(2,1)}, bf16[128,768]{1,0:T(8,128)(2,1)}, u32[]{:S(2)}, u32[]{:S(2)}) collective-permute-start(bf16[128,768]{1,0:T(8,128)(2,1)} %get-tuple-element.654), channel_id=1, source_target_pairs={{0,2},{1,3},{2,0},{3,1},{4,6},{5,7},{6,4},{7,5},{8,10},{9,11},{10,... | collective-permute-start | bytes 589832 | tf_op jit(solution)/shard_map/ppermute | solution.py:71
  488.8 22.4 %collective-permute-start.90 = (bf16[128,768]{1,0:T(8,128)(2,1)}, bf16[128,768]{1,0:T(8,128)(2,1)}, u32[]{:S(2)}, u32[]{:S(2)}) collective-permute-start(bf16[128,768]{1,0:T(8,128)(2,1)} %get-tuple-element.655), channel_id=1, source_target_pairs={{0,1},{1,0},{2,3},{3,2},{4,5},{5,4},{6,7},{7,6},{8,9},{9,8},{10,11... | collective-permute-start | bytes 589832 | tf_op jit(solution)/shard_map/ppermute | solution.py:71
  594.4 21.7 %collective-permute-start.117 = (bf16[256,768]{1,0:T(8,128)(2,1)S(1)}, bf16[256,768]{1,0:T(8,128)(2,1)S(1)}, u32[]{:S(2)}, u32[]{:S(2)}) collective-permute-start(bf16[256,768]{1,0:T(8,128)(2,1)S(1)} %get-tuple-element.594), channel_id=1, source_target_pairs={{0,4},{1,5},{2,6},{3,7},{4,0},{5,1},{6,2},{7,3},{8,12},{9,13},{10,... | collective-permute-start | bytes 1179656 | tf_op jit(solution)/shard_map/ppermute | solution.py:71
  595.4 22.2 %collective-permute-start.114 = (bf16[256,768]{1,0:T(8,128)(2,1)S(1)}, bf16[256,768]{1,0:T(8,128)(2,1)S(1)}, u32[]{:S(2)}, u32[]{:S(2)}) collective-permute-start(bf16[256,768]{1,0:T(8,128)(2,1)S(1)} %get-tuple-element.594), channel_id=1, source_target_pairs={{0,1},{1,0},{2,3},{3,2},{4,5},{5,4},{6,7},{7,6},{8,9},{9,8},{10,11... | collective-permute-start | bytes 1179656 | tf_op jit(solution)/shard_map/ppermute | solution.py:71
  601.3 22.8 %collective-permute-start.116 = (bf16[256,768]{1,0:T(8,128)(2,1)S(1)}, bf16[256,768]{1,0:T(8,128)(2,1)S(1)}, u32[]{:S(2)}, u32[]{:S(2)}) collective-permute-start(bf16[256,768]{1,0:T(8,128)(2,1)S(1)} %collective-permute-done.115), channel_id=1, source_target_pairs={{0,1},{1,0},{2,3},{3,2},{4,5},{5,4},{6,7},{7,6},{8,9},{9,8},{10,11... | collective-permute-start | bytes 1179656 | tf_op jit(solution)/shard_map/ppermute | solution.py:71
  657.1 65.4 %collective-permute-start.113 = (f32[72,128]{1,0:T(8,128)S(1)}, f32[72,128]{1,0:T(8,128)}, u32[]{:S(2)}, u32[]{:S(2)}) collective-permute-start(f32[72,128]{1,0:T(8,128)S(1)} %add_add_fusion.4), channel_id=1, source_target_pairs={{0,24},{8,16},{16,8},{24,0},{1,25},{9,17},{17,9},{25,1},{2,26},{10... | collective-permute-start | bytes 110600 | tf_op jit(solution)/shard_map/ppermute | solution.py:71
  671.8 17.8 %collective-permute-start.138 = (bf16[192,384]{1,0:T(8,128)(2,1)S(1)}, bf16[192,384]{1,0:T(8,128)(2,1)S(1)}, u32[]{:S(2)}, u32[]{:S(2)}) collective-permute-start(bf16[192,384]{1,0:T(8,128)(2,1)S(1)} %get-tuple-element.682), channel_id=1, source_target_pairs={{0,24},{8,0},{16,8},{24,16},{1,25},{9,1},{17,9},{25,17},{2,26},{10... | collective-permute-start | bytes 442376 | tf_op jit(solution)/shard_map/ppermute | solution.py:76
  682.0 19.7 %collective-permute-start.125 = (bf16[96,768]{1,0:T(8,128)(2,1)S(1)}, bf16[96,768]{1,0:T(8,128)(2,1)S(1)}, u32[]{:S(2)}, u32[]{:S(2)}) collective-permute-start(bf16[96,768]{1,0:T(8,128)(2,1)S(1)} %get-tuple-element.683), channel_id=1, source_target_pairs={{0,24},{8,0},{16,8},{24,16},{1,25},{9,1},{17,9},{25,17},{2,26},{10... | collective-permute-start | bytes 442376 | tf_op jit(solution)/shard_map/ppermute | solution.py:76
  684.4 21.6 %collective-permute-start.124 = (bf16[96,768]{1,0:T(8,128)(2,1)S(1)}, bf16[96,768]{1,0:T(8,128)(2,1)S(1)}, u32[]{:S(2)}, u32[]{:S(2)}) collective-permute-start(bf16[96,768]{1,0:T(8,128)(2,1)S(1)} %get-tuple-element.684), channel_id=1, source_target_pairs={{0,16},{8,24},{16,0},{24,8},{1,17},{9,25},{17,1},{25,9},{2,18},{10... | collective-permute-start | bytes 442376 | tf_op jit(solution)/shard_map/ppermute | solution.py:76
  689.6 16.5 %collective-permute-start.123 = (bf16[96,768]{1,0:T(8,128)(2,1)S(1)}, bf16[96,768]{1,0:T(8,128)(2,1)S(1)}, u32[]{:S(2)}, u32[]{:S(2)}) collective-permute-start(bf16[96,768]{1,0:T(8,128)(2,1)S(1)} %get-tuple-element.685), channel_id=1, source_target_pairs={{0,8},{8,16},{16,24},{24,0},{1,9},{9,17},{17,25},{25,1},{2,10},{10... | collective-permute-start | bytes 442376 | tf_op jit(solution)/shard_map/ppermute | solution.py:76
  693.1 29.6 %collective-permute-start.112 = (f32[72,128]{1,0:T(8,128)S(1)}, f32[72,128]{1,0:T(8,128)}, u32[]{:S(2)}, u32[]{:S(2)}) collective-permute-start(f32[72,128]{1,0:T(8,128)S(1)} %add_add_fusion.4), channel_id=1, source_target_pairs={{0,16},{8,24},{16,0},{24,8},{1,17},{9,25},{17,1},{25,9},{2,18},{10... | collective-permute-start | bytes 110600 | tf_op jit(solution)/shard_map/ppermute | solution.py:71
  707.3 16.1 %collective-permute-start.149 = (bf16[192,384]{1,0:T(8,128)(2,1)}, bf16[192,384]{1,0:T(8,128)(2,1)S(1)}, u32[]{:S(2)}, u32[]{:S(2)}) collective-permute-start(bf16[192,384]{1,0:T(8,128)(2,1)} %get-tuple-element.587.refs_0_), channel_id=1, source_target_pairs={{0,4},{1,5},{2,6},{3,7},{4,0},{5,1},{6,2},{7,3},{8,12},{9,13},{10,... | collective-permute-start | bytes 442376 | tf_op jit(solution)/shard_map/ppermute | solution.py:71
  (238 other events, 2477.5 us)
Sparse Core Ops, SparseCore 0:
  21.0 187.0 all-gather.3
  210.2 111.0 all-gather.5
  411.5 106.6 reduce-scatter.2
  520.5 172.6 reduce-scatter.4
